TPU v7x, 128 devices: a whole 4x4x4 slice. The times are simulated.
128 devices in a mesh: dp: 32 (over z, y, core), seq: 4 (over x).
Axes of the slice: x: 4, y: 4, z: 4, core: 2. Of those that a mesh axis runs over, the one named last changes fastest.
Arguments:
- bases: int32 [32, 65536], P('dp', 'seq'), may hold values from 0 to 3
- skip: bfloat16 [32, 1024, 1536], P('dp', 'seq'), may hold values from -6 to 6
- base_table: float32 [4, 1536], replicated, may hold values from -3 to 3
- conv_weight: bfloat16 [5, 1536, 1536], replicated, may hold values from -0.0625 to 0.0625
- conv_gain: float32 [1536], replicated, may hold values from 0.25 to 1.75
- attn_gain: float32 [1536], replicated, may hold values from 0.25 to 1.75
- w_query: bfloat16 [1536, 1024], P(('dp', 'seq')), may hold values from -3.1001355 to 3.1001355
- w_kv: bfloat16 [1536, 320], P(('dp', 'seq')), may hold values from -0.10333785 to 0.10333785
- w_out: bfloat16 [1536, 1536], P(('dp', 'seq')), may hold values from -0.15625 to 0.15625
- cotangent: bfloat16 [32, 512, 1536], P('dp', 'seq'), may hold values from -6 to 6
Outputs:
- coarse: bfloat16 [32, 512, 1536], P('dp', 'seq')
- skip_grad: bfloat16 [32, 1024, 1536], P('dp', 'seq')
- grad_query: float32 [1536, 1024], P(('dp', 'seq'))
- grad_kv: float32 [1536, 320], P(('dp', 'seq'))
- grad_out: float32 [1536, 1536], P(('dp', 'seq'))
All inputs are finite; a program needn't handle non-finite values.
Results may differ from a plain program's by a relative error of at most 0.013.
Values may be sent and summed in bfloat16 or wider, within the bound.
No kernel may reach another device: no remote copies, remote signals or barrier semaphores. Data moves between devices by JAX's collectives and lax.ppermute only.
A program may use at most 192 MiB of HBM per device.

v0:
```python
import jax
import jax.numpy as jnp
from jax import lax
from jax.sharding import PartitionSpec as P

HQ = 8
HD = 128
VD = 192


HIGH = lax.Precision.HIGHEST


def padded_2(cells, sides, width):
    for axis, dim in sides:
        count = lax.axis_size(axis)
        ends = count - 1
        head = lax.slice_in_dim(cells, 0, width, axis=dim)
        tail = lax.slice_in_dim(cells, cells.shape[dim] - width, cells.shape[dim], axis=dim)
        cells = jnp.concatenate(
            [
                lax.ppermute(tail, axis, [(i, (i + 1) % count) for i in range(ends)]),
                cells,
                lax.ppermute(head, axis, [((i + 1) % count, i) for i in range(ends)]),
            ],
            axis=dim,
        )
    return cells


def rms_scale(value):
    return lax.rsqrt(jnp.mean(value * value, axis=-1, keepdims=True) + 1e-06)


def rms_back(value, gain, grad):
    scale = rms_scale(value)
    scaled = grad * gain
    return scale * scaled - value * (scale * scale * scale) * jnp.mean(
        value * scaled, axis=-1, keepdims=True
    )


def gelu_fwd(value):
    return 0.5 * value * (1.0 + jax.scipy.special.erf(value * 0.7071067811865476))


def gelu_slope(value):
    return (
        0.5 * (1.0 + jax.scipy.special.erf(value * 0.7071067811865476))
        + value * jnp.exp(-0.5 * value * value) * 0.3989422804014327
    )


def conv_forward(padded, weight):
    length = padded.shape[0] - 4
    window = jnp.stack([padded[k : k + length] for k in range(5)], axis=1)
    return lax.dot_general(
        window, weight, (((1, 2), (0, 1)), ((), ())), preferred_element_type=jnp.float32
    )


def conv_backward(padded, weight):
    length = padded.shape[0] - 4
    window = jnp.stack([padded[4 - k : 4 - k + length] for k in range(5)], axis=1)
    return lax.dot_general(
        window, weight, (((1, 2), (0, 2)), ((), ())), preferred_element_type=jnp.float32
    )


def tdot(left, right):
    return lax.dot_general(
        left, right, (((0,), (0,)), ((), ())), preferred_element_type=jnp.float32
    )


def rdot(left, right):
    return lax.dot_general(
        left, right, (((1,), (1,)), ((), ())), preferred_element_type=jnp.float32
    )


def per_device(
    bases, skip, base_table, conv_weight, conv_gain, attn_gain, w_query, w_kv, w_out, cotangent
):
    rows_fine = skip.shape[1]
    width = skip.shape[2]
    cells = bases[0].reshape(rows_fine, 64)
    counts = jnp.sum(
        (cells[:, :, None] == jnp.arange(4, dtype=jnp.int32)).astype(jnp.float32), axis=1
    )
    embed = jnp.dot((counts - 16.0) * 0.25, base_table, precision=HIGH)
    state = skip[0].astype(jnp.float32) + embed
    pre = state * rms_scale(state) * conv_gain
    active = gelu_fwd(pre).astype(jnp.bfloat16)
    padded = padded_2(active[None], (("seq", 1),), 2)[0]
    level = state + conv_forward(padded, conv_weight)
    pairs = level.reshape(-1, 2, width)
    pooled = (pairs[:, 0] + pairs[:, 1]) * 0.5
    normed = (pooled * rms_scale(pooled) * attn_gain).astype(jnp.bfloat16)
    full_query, full_kv, full_out = (
        lax.all_gather(w_query, ("dp", "seq"), axis=0, tiled=True),
        lax.all_gather(w_kv, ("dp", "seq"), axis=0, tiled=True),
        lax.all_gather(w_out, ("dp", "seq"), axis=0, tiled=True),
    )
    query = jnp.dot(normed, full_query, preferred_element_type=jnp.float32).astype(jnp.bfloat16)
    keyval = jnp.dot(normed, full_kv, preferred_element_type=jnp.float32).astype(jnp.bfloat16)
    sample_kv = lax.all_gather(keyval, "seq", axis=0, tiled=True)
    keys = sample_kv[:, :HD]
    values = sample_kv[:, HD:]
    positions = query.shape[0]
    heads_q = query.reshape(positions, HQ, HD)
    inv = 1.0 / HD**0.5
    scores = jnp.einsum("thd,sd->hts", heads_q, keys, preferred_element_type=jnp.float32) * inv
    peak = jnp.max(scores, axis=-1, keepdims=True)
    expo = jnp.exp(scores - peak)
    probs = expo / jnp.sum(expo, axis=-1, keepdims=True)
    weights = probs.astype(jnp.bfloat16)
    heads = (
        jnp.einsum("hts,se->the", weights, values, preferred_element_type=jnp.float32)
        .reshape(positions, HQ * VD)
        .astype(jnp.bfloat16)
    )
    coarse = (pooled + jnp.dot(heads, full_out, preferred_element_type=jnp.float32)).astype(
        jnp.bfloat16
    )
    back_query, back_kv, back_out = (full_query, full_kv, full_out)
    grad_in = cotangent[0]
    d_heads = rdot(grad_in, back_out).astype(jnp.bfloat16)
    d_split = d_heads.reshape(positions, HQ, VD)
    d_probs = jnp.einsum("the,se->hts", d_split, values, preferred_element_type=jnp.float32)
    d_scores = (probs * (d_probs - jnp.sum(probs * d_probs, axis=-1, keepdims=True)) * inv).astype(
        jnp.bfloat16
    )
    d_query = (
        jnp.einsum("hts,sd->thd", d_scores, keys, preferred_element_type=jnp.float32)
        .reshape(positions, HQ * HD)
        .astype(jnp.bfloat16)
    )
    d_keys = jnp.einsum("hts,thd->sd", d_scores, heads_q, preferred_element_type=jnp.float32)
    d_values = jnp.einsum("hts,the->se", weights, d_split, preferred_element_type=jnp.float32)
    own_kv = lax.psum_scatter(
        jnp.concatenate([d_keys, d_values], axis=1).astype(jnp.bfloat16),
        "seq",
        scatter_dimension=0,
        tiled=True,
    )
    right_side = jnp.concatenate([d_query, own_kv], axis=1)
    n_data = lax.axis_size("dp")
    summed = lax.psum_scatter(
        jnp.concatenate([tdot(normed, right_side), tdot(heads, grad_in)], axis=1),
        ("dp", "seq"),
        scatter_dimension=0,
        tiled=True,
    )
    summed = summed * (1.0 / n_data)
    query_cols = w_query.shape[1]
    kv_cols = w_kv.shape[1]
    grad_query = summed[:, :query_cols]
    grad_kv = summed[:, query_cols : query_cols + kv_cols]
    grad_out = summed[:, query_cols + kv_cols :]
    d_normed = rdot(d_query, back_query) + rdot(own_kv, back_kv)
    d_pooled = grad_in.astype(jnp.float32) + rms_back(pooled, attn_gain, d_normed)
    d_level = jnp.repeat(d_pooled * 0.5, 2, axis=0).astype(jnp.bfloat16)
    grad_pad = padded_2(d_level[None], (("seq", 1),), 2)[0]
    d_active = conv_backward(grad_pad, conv_weight)
    skip_grad = (
        d_level.astype(jnp.float32) + rms_back(state, conv_gain, gelu_slope(pre) * d_active)
    ).astype(jnp.bfloat16)
    return (coarse[None], skip_grad[None], grad_query, grad_kv, grad_out)


def solution(mesh):
    placed = (
        P("dp", "seq"),
        P("dp", "seq", None),
        P(),
        P(),
        P(),
        P(),
        P(("dp", "seq"), None),
        P(("dp", "seq"), None),
        P(("dp", "seq"), None),
        P("dp", "seq", None),
    )
    return jax.shard_map(
        per_device,
        mesh=mesh,
        in_specs=placed,
        out_specs=(
            P("dp", "seq", None),
            P("dp", "seq", None),
            P(("dp", "seq"), None),
            P(("dp", "seq"), None),
            P(("dp", "seq"), None),
        ),
        check_vma=False,
    )
```

profile of v0, /device:TPU:15, one launch (start us, length us, event | category | flops | bytes accessed | tf_op | source)
XLA Modules:
  0.0 437.2 jit_solution(4697993038751676623)
XLA Ops:
  11.1 2.8 multiply_reduce_fusion.1
  15.7 4.0 collective-permute-start.1
  19.7 69.8 %all-gather = bf16[128,12,320]{2,1,0:T(8,128)(2,1)} all-gather(bf16[1,12,320]{2,1,0:T(8,128)(2,1)S(1)} %bitcast.165), channel_id=1, replica_groups=mesh['dp'=32,'seq'=4] {'dp','seq'}, dimensions={0}, use_global_device_ids=true | all-gather | bytes 990720 | tf_op jit(solution)/shard_map/all_gather | solution.py:102
  89.5 3.3 reshape.117
  94.1 11.0 %fusion.4 = f32[256,1536]{1,0:T(8,128)S(1)} fusion(f32[256,1536]{1,0:T(8,128)S(1)} %get-tuple-element.38, bf16[256,5,1536]{2,0,1:T(8,128)(2,1)S(1)} %fusion.39, bf16[5,1536,1536]{2,1,0:T(8,128)(2,1)} %param.13), kind=kOutput, calls=%fused_computation.8 | convolution fusion | flops 6040190976 | bytes 30670848 | tf_op jit(solution)/shard_map/dot_general | solution.py:57
  109.6 11.4 %all_gather.13 = bf16[512,320]{0,1:T(8,128)(2,1)} all-gather(bf16[128,320]{0,1:T(8,128)(2,1)S(1)} %convolution_convert_fusion.4), channel_id=1, replica_groups=mesh['dp'=32,'seq'=4] {'seq'}, dimensions={0}, use_global_device_ids=true | all-gather | bytes 409600 | tf_op jit(solution)/shard_map/all_gather | solution.py:107
  121.0 4.7 %reshape.119 = bf16[1536,1024]{1,0:T(8,128)(2,1)S(1)} reshape(bf16[128,12,1024]{2,1,0:T(8,128)(2,1)} %all-gather.6.cloned.1.call-done) | data formatting | bytes 6291456
  128.1 3.2 fusion.73
  131.3 2.7 convolution_convert_fusion.1
  134.0 15.1 %all-gather.8.cloned.1.call-done = bf16[128,12,1536]{2,1,0:T(8,128)(2,1)} async-done(((bf16[1,12,1536]{2,1,0:T(8,128)(2,1)}), bf16[128,12,1536]{2,1,0:T(8,128)(2,1)}) %all-gather.8.cloned.1.call-update) | async-done | bytes 4718608 | tf_op jit(solution)/shard_map/all_gather | solution.py:103
  149.1 8.2 %reshape.121 = bf16[1536,1536]{1,0:T(8,128)(2,1)} reshape(bf16[128,12,1536]{2,1,0:T(8,128)(2,1)} %all-gather.8.cloned.1.call-done) | data formatting | bytes 9437184
  157.3 4.8 %convolution_convert_fusion = bf16[128,1536]{1,0:T(8,128)(2,1)} fusion(bf16[1536,1536]{1,0:T(8,128)(2,1)} %reshape.121, bf16[1,128,1536]{2,1,0:T(8,128)(2,1)} %param.19), kind=kOutput, calls=%fused_computation.12 | convolution fusion | flops 604176384 | bytes 5505024 | tf_op jit(solution)/shard_map/dot_general | solution.py:77
  164.0 2.8 fusion.20
  168.8 5.2 %fusion.21 = bf16[512,128]{0,1:T(8,128)(2,1)} fusion(bf16[128,8,128]{0,2,1:T(8,128)(2,1)} %bitcast.162, f32[512,128,8]{1,0,2:T(8,128)} %fusion.54, f32[8,128,512]{1,2,0:T(8,128)} %get-tuple-element.40, f32[8,128]{1,0:T(8,128)S(1)} %get-tuple-element.39), kind=kOutput, calls=%fused_computation.43 | convolution fusion | flops 137954816 | bytes 4591616 | tf_op jit(solution)/shard_map/hts,thd->sd/dot_general | solution.py:139
  176.0 6.2 %fusion.45 = f32[1536,1536]{0,1:T(8,128)} fusion(bf16[128,1536]{0,1:T(8,128)(2,1)} %bitcast.155, bf16[1,128,1536]{2,1,0:T(8,128)(2,1)} %param.19), kind=kOutput, calls=%fused_computation.86 | convolution fusion | flops 603979776 | bytes 10223616 | tf_op jit(solution)/shard_map/dot_general | solution.py:71
  182.2 4.5 %convolution_convert_fusion.2 = bf16[128,8,128]{2,0,1:T(8,128)(2,1)S(1)} fusion(f32[512,128,8]{1,0,2:T(8,128)} %fusion.54, bf16[512,320]{0,1:T(8,128)(2,1)} %all_gather.13, f32[8,128,512]{1,2,0:T(8,128)} %get-tuple-element.40, f32[8,128]{1,0:T(8,128)S(1)} %get-tuple-element.39), kind=kOutput, calls=%fused_computation.39 | convolution fusion | flops 138020352 | bytes 8790016 | tf_op jit(solution)/shard_map/hts,sd->thd/dot_general | solution.py:135
  186.6 6.2 %reduce-scatter.5.cloned.1.call-done = bf16[128,320]{1,0:T(8,128)(2,1)} async-done(((bf16[512,320]{1,0:T(8,128)(2,1)}), bf16[128,320]{1,0:T(8,128)(2,1)}) %reduce-scatter.5.cloned.1.call-update) | async-done | bytes 81936
  197.7 6.7 %pad_maximum_fusion = f32[1536,2880]{0,1:T(8,128)} fusion(f32[1536,1536]{0,1:T(8,128)S(1)} %copy-done.2, f32[1536,1344]{0,1:T(8,128)S(1)} %fusion.48), kind=kLoop, calls=%fused_computation.2 | loop fusion | flops 4423680 | bytes 35389440 | tf_op jit(solution)/shard_map/concatenate | solution.py:150
  204.5 4.3 fusion.7
  213.0 2.5 collective-permute-start.2
  227.4 14.0 %multiply_reduce_fusion = (f32[256]{0:T(256)S(1)}, f32[256,1536]{1,0:T(8,128)}) fusion(f32[256,1536]{1,0:T(8,128)S(1)} %copy-done.4, bf16[256,5,1536]{2,0,1:T(8,128)(2,1)} %fusion.35, bf16[5,1536,1536]{2,1,0:T(8,128)(2,1)} %param.13, f32[1536]{0:T(1024)S(1)} %copy-done.17, f32[256]{0:T(256)S(1)} %get-tuple-element.36), kind=kOutput, calls=%fused_computation.31 | convolution fusion | flops 6045302784 | bytes 30679040 | tf_op jit(solution)/shard_map/dot_general | solution.py:65
  241.4 3.3 fusion.33
  244.7 180.9 %all-reduce.3.cloned.1.call-done = f32[1536,2880]{0,1:T(8,128)} async-done(((f32[1536,2880]{0,1:T(8,128)}), f32[1536,2880]{0,1:T(8,128)}) %all-reduce.3.cloned.1.call-update) | async-done | bytes 17694736
  425.6 2.5 dynamic-slice_multiply_fusion
  (105 shorter events, 42.9 us)
Async XLA Ops:
  7.2 3.9 copy-start
  7.2 6.7 %copy-start.17 = (f32[1536]{0:T(1024)S(1)}, f32[1536]{0:T(1024)}, u32[]{:S(2)}) copy-start(f32[1536]{0:T(1024)} %param.14) | copy-start | bytes 18436
  7.2 113.8 %all-gather.6.cloned.1.call-start = ((), (), s32[]{:S(2)}) async-start(), calls=%async_computation.1 | async-start | bytes 4227072 | tf_op jit(solution)/shard_map/all_gather | solution.py:101
  7.9 141.2 %all-gather.8.cloned.1.call-start = ((), (), s32[]{:S(2)}) async-start(), calls=%async_computation.2 | async-start | bytes 6340608 | tf_op jit(solution)/shard_map/all_gather | solution.py:103
  8.7 184.2 %reduce-scatter.5.cloned.1.call-start = ((), (), s32[]{:S(2)}) async-start(), calls=%async_computation.3 | async-start | bytes 491520
  11.1 8.6 %copy-start.18 = (bf16[12,320]{1,0:T(8,128)(2,1)S(1)}, bf16[12,320]{1,0:T(8,128)(2,1)}, u32[]{:S(2)}) copy-start(bf16[12,320]{1,0:T(8,128)(2,1)} %param.17) | copy-start | bytes 23044
  13.9 80.2 %copy-start.3 = (f32[256,1536]{1,0:T(8,128)}, f32[256,1536]{1,0:T(8,128)S(1)}, u32[]{:S(2)}) copy-start(f32[256,1536]{1,0:T(8,128)S(1)} %get-tuple-element.38) | copy-start | bytes 4718596
  14.4 78.4 %collective-permute-start = (bf16[1,2,1536]{2,1,0:T(2,128)(2,1)S(1)}, bf16[1,2,1536]{2,1,0:T(2,128)(2,1)S(1)}, u32[]{:S(2)}, u32[]{:S(2)}) collective-permute-start(bf16[1,2,1536]{2,1,0:T(2,128)(2,1)S(1)} %get-tuple-element.34), channel_id=1, source_target_pairs={{0,1},{1,2},{2,3},{4,5},{5,6},{6,7},{8,9},{9,10},{10,11},{12,13},{... | collective-permute-start | bytes 18440 | tf_op jit(solution)/shard_map/ppermute | solution.py:22
  15.7 78.0 %collective-permute-start.1 = (bf16[1,2,1536]{2,1,0:T(2,128)(2,1)S(1)}, bf16[1,2,1536]{2,1,0:T(2,128)(2,1)S(1)}, u32[]{:S(2)}, u32[]{:S(2)}) collective-permute-start(bf16[1,2,1536]{2,1,0:T(2,128)(2,1)S(1)} %get-tuple-element.33), channel_id=1, source_target_pairs={{1,0},{2,1},{3,2},{5,4},{6,5},{7,6},{9,8},{10,9},{11,10},{13,12},{... | collective-permute-start | bytes 18440 | tf_op jit(solution)/shard_map/ppermute | solution.py:24
  106.0 2.3 copy-start.16
  107.3 1.6 copy-start.7
  128.1 3.2 copy-start.14
  164.0 2.9 copy-start.13
  175.9 249.6 %all-reduce.3.cloned.1.call-start = ((), (), s32[]{:S(2)}) async-start(), calls=%async_computation.4 | async-start | bytes 35389440
  193.9 3.8 copy-start.2
  204.4 4.3 copy-start.8
  204.4 4.3 copy-start.15
  208.8 1.1 copy-start.6
  209.9 1.3 copy-start.10
  213.0 8.9 %collective-permute-start.2 = (bf16[1,2,1536]{2,1,0:T(2,128)(2,1)S(1)}, bf16[1,2,1536]{2,1,0:T(2,128)(2,1)S(1)}, u32[]{:S(2)}, u32[]{:S(2)}) collective-permute-start(bf16[1,2,1536]{2,1,0:T(2,128)(2,1)S(1)} %get-tuple-element.32), channel_id=1, source_target_pairs={{1,0},{2,1},{3,2},{5,4},{6,5},{7,6},{9,8},{10,9},{11,10},{13,12},{... | collective-permute-start | bytes 18440 | tf_op jit(solution)/shard_map/ppermute | solution.py:24
  220.4 3.6 copy-start.12
  220.4 4.9 %collective-permute-start.3 = (bf16[1,2,1536]{2,1,0:T(2,128)(2,1)S(1)}, bf16[1,2,1536]{2,1,0:T(2,128)(2,1)S(1)}, u32[]{:S(2)}, u32[]{:S(2)}) collective-permute-start(bf16[1,2,1536]{2,1,0:T(2,128)(2,1)S(1)} %get-tuple-element.31), channel_id=1, source_target_pairs={{0,1},{1,2},{2,3},{4,5},{5,6},{6,7},{8,9},{9,10},{10,11},{12,13},{... | collective-permute-start | bytes 18440 | tf_op jit(solution)/shard_map/ppermute | solution.py:22
  224.0 3.4 copy-start.4
  425.6 5.0 %copy-start.1 = (f32[4,1536]{1,0:T(4,128)S(1)}, f32[4,1536]{1,0:T(4,128)}, u32[]{:S(2)}) copy-start(f32[4,1536]{1,0:T(4,128)} %param.12) | copy-start | bytes 73732
  (3 other events, 2.4 us)
Sparse Core Ops, SparseCore 0:
  11.2 67.8 all-gather.5
  82.1 66.9 all-gather.7
  176.1 16.7 reduce-scatter.4
  204.5 220.9 all-reduce.2
where the time goes:
time: 440 us; the launch traced here: 437 us
  waiting for transfers between devices  204 us (46%)
  blocking collectives  81.2 us (18%)
  matrix products  69.7 us (16%)
  local copies, waits for them, and re-layouts  39.3 us (9%)
  other arithmetic  19.6 us (4%)
  between operations  14.2 us (3%)
  starting transfers between devices  9.36 us (2%)
    unnamed x6, waiting for transfers between devices  189 us
    all_gather x1, blocking collectives, per_device(): lax.all_gather(w_kv, ('dp', 'seq'), axis=0, tiled=True)  69.8 us
    unnamed x51, local copies, waits for them, and re-layouts  28.5 us
    all_gather x1, waiting for transfers between devices, per_device(): lax.all_gather(w_out, ('dp', 'seq'), axis=0, tiled=True)  15.1 us
    dot_general x1, matrix products, conv_backward(): lax.dot_general(window, weight, (((1, 2), (0, 2)), ((), ())), preferred_e...  14 us
    all_gather x1, blocking collectives, per_device(): sample_kv = lax.all_gather(keyval, 'seq', axis=0, tiled=True)  11.4 us
    dot_general x1, matrix products, conv_forward(): lax.dot_general(window, weight, (((1, 2), (0, 1)), ((), ())), preferred_e...  11 us
  transfers between devices with their start and end apart: 8, of which 4 were waited for; matrix products, arithmetic and copies ran while one was open for 19% of the time, Pallas kernels for 0%

commit v1 on v0

v1 whole, which is shorter than its diff:
```python
import jax
import jax.numpy as jnp
from jax import lax
from jax.experimental import pallas as pl
from jax.experimental.pallas import tpu as pltpu
from jax.sharding import Mesh
from jax.sharding import PartitionSpec as P

HQ = 8
HD = 128
VD = 192
VMEM_LIMIT = 60 * 1024 * 1024
F32 = jnp.float32
BF16 = jnp.bfloat16


def ndot(left, right):
    return lax.dot_general(
        left, right, (((1,), (0,)), ((), ())), preferred_element_type=F32
    )


def rdot(left, right):
    return lax.dot_general(
        left, right, (((1,), (1,)), ((), ())), preferred_element_type=F32
    )


def tdot(left, right):
    return lax.dot_general(
        left, right, (((0,), (0,)), ((), ())), preferred_element_type=F32
    )


def embed_counts(counts, skip, table):
    state = skip.astype(F32)
    for base in range(4):
        state = state + ((counts[base] - 16.0) * 0.25) * table[base : base + 1, :]
    return state


def embed_rows(cells, skip, table):
    counts = [jnp.sum((cells == base).astype(F32), axis=1, keepdims=True) for base in range(4)]
    return embed_counts(counts, skip, table)


def row_scale(value):
    return lax.rsqrt(jnp.mean(value * value, axis=-1, keepdims=True) + 1e-06)


def front_kernel(
    ends, cells, skip, edge_prev, edge_next, table, gain, attn_gain,
    weight, pooled, normed, state_buf, active_buf, lhs, weight_buf, arrived,
):
    rows = skip.shape[0]
    half = rows // 2
    width = skip.shape[1]
    steps, _, _, block = weight_buf.shape

    def fetch(step):
        cols = pl.ds(pl.multiple_of(step * block, block), block)
        return pltpu.make_async_copy(weight.at[:, :, cols], weight_buf.at[step], arrived.at[step])

    for step in range(steps):
        fetch(step).start()

    def rows_in(state, at, keep):
        pre = state * row_scale(state) * gain[...]
        active = 0.5 * pre * (1.0 + lax.erf(pre * 0.7071067811865476))
        active = active.astype(BF16).astype(F32)
        if keep is not None:
            active = jnp.where(keep > 0, active, 0.0)
        count = state.shape[0]
        for tile in range(skip.shape[1] // 128):
            lanes = slice(tile * 128, (tile + 1) * 128)
            state_buf[tile, pl.ds(at, count), :] = state[:, lanes]
            active_buf[tile, pl.ds(at, count), :] = active[:, lanes]

    def edge_rows(edge):
        counts = [edge[:, width + base : width + base + 1].astype(F32) for base in range(4)]
        return embed_counts(counts, edge[:, 0:width], table)

    rows_in(edge_rows(edge_prev), 0, ends[0])
    rows_in(edge_rows(edge_next), rows + 8, ends[1])

    chunk = 64

    def one(i, carry):
        at = pl.multiple_of(i * chunk, chunk)
        state = embed_rows(cells[pl.ds(at, chunk), :], skip[pl.ds(at, chunk), :], table)
        rows_in(state, pl.multiple_of(at + 8, 8), None)
        return carry

    lax.fori_loop(0, rows // chunk, one, 0)
    for tile in range(width // 128):
        cols = slice(tile * 128, (tile + 1) * 128)
        part = [active_buf[tile, pl.ds(6 + j, half, 2), :] for j in range(6)]
        for k in range(5):
            lhs[k, :, cols] = ((part[k] + part[k + 1]) * 0.5).astype(BF16)
        pooled[:, cols] = (
            state_buf[tile, pl.ds(8, half, 2), :] + state_buf[tile, pl.ds(9, half, 2), :]
        ) * 0.5

    def one_block(step, carry):
        fetch(step).wait()
        total = ndot(lhs[0], weight_buf[step, 0])
        for k in range(1, 5):
            total = total + ndot(lhs[k], weight_buf[step, k])
        cols = pl.ds(pl.multiple_of(step * block, block), block)
        pooled[:, cols] = pooled[:, cols] + total
        return carry

    lax.fori_loop(0, steps, one_block, 0)

    def finish_rows(i, carry):
        rows_at = pl.ds(pl.multiple_of(i * 64, 64), 64)
        value = pooled[rows_at, :]
        normed[rows_at, :] = (value * row_scale(value) * attn_gain[...]).astype(BF16)
        return carry

    lax.fori_loop(0, half // 64, finish_rows, 0)


def front(ends, cells, skip, edge_prev, edge_next, table, gain, attn_gain, weight, block=256):
    rows, width = skip.shape
    half = rows // 2
    whole = lambda array: pl.BlockSpec(array.shape, lambda n, s: (0,) * array.ndim)
    small = (cells, skip, edge_prev, edge_next, table, gain, attn_gain)
    return pl.pallas_call(
        front_kernel,
        grid_spec=pltpu.PrefetchScalarGridSpec(
            num_scalar_prefetch=1,
            grid=(1,),
            in_specs=[whole(a) for a in small] + [pl.BlockSpec(memory_space=pl.ANY)],
            out_specs=[
                pl.BlockSpec((half, width), lambda n, s: (0, 0)),
                pl.BlockSpec((half, width), lambda n, s: (0, 0)),
            ],
            scratch_shapes=[
                pltpu.VMEM((width // 128, rows + 16, 128), F32),
                pltpu.VMEM((width // 128, rows + 16, 128), F32),
                pltpu.VMEM((5, half, width), BF16),
                pltpu.VMEM((width // block, 5, width, block), BF16),
                pltpu.SemaphoreType.DMA((width // block,)),
            ],
        ),
        out_shape=[
            jax.ShapeDtypeStruct((half, width), F32),
            jax.ShapeDtypeStruct((half, width), BF16),
        ],
        compiler_params=pltpu.CompilerParams(vmem_limit_bytes=VMEM_LIMIT),
        cost_estimate=pl.CostEstimate(
            flops=2 * half * 5 * width * width, bytes_accessed=10 * width * width + 8 * rows * width, transcendentals=rows * width
        ),
        name="front",
    )(ends, *small, weight)


def back_kernel(
    cells, skip, table, gain, grad, grad_prev, grad_next, weight, out,
    state_buf, scaled_buf, grad_buf, turned_buf, level_buf, scale_buf, sum_buf, weight_buf, arrived,
):
    rows, width = skip.shape
    half = rows // 2
    steps, _, block, _ = weight_buf.shape
    chunk = 64

    def fetch(step):
        at = pl.ds(pl.multiple_of(step * block, block), block)
        return pltpu.make_async_copy(weight.at[:, at, :], weight_buf.at[step], arrived.at[step])

    for step in range(steps):
        fetch(step).start()

    grad_buf[pl.ds(0, 16), :] = grad_prev[...].astype(F32)
    grad_buf[pl.ds(16, half), :] = grad[...].astype(F32)
    grad_buf[pl.ds(half + 16, 16), :] = grad_next[...].astype(F32)
    for tile in range(width // 128):
        lanes = slice(tile * 128, (tile + 1) * 128)
        before, here, later = [
            grad_buf[pl.ds(15 + shift, half), lanes].T.astype(BF16) for shift in range(3)
        ]
        pairs = ((later, later), (here, later), (here, here), (before, here), (before, before))
        for tap, (even, odd) in enumerate(pairs):
            turned_buf[tap, lanes, 0:half] = even
            turned_buf[tap, lanes, half:rows] = odd

    def one(i, carry):
        at = pl.ds(pl.multiple_of(i * chunk, chunk), chunk)
        state = embed_rows(cells[at, :], skip[at, :], table)
        state_buf[at, :] = state
        scale_buf[at, :] = row_scale(state)
        return carry

    lax.fori_loop(0, rows // chunk, one, 0, unroll=2)
    sum_buf[...] = jnp.zeros_like(sum_buf)

    def one_block(step, carry):
        fetch(step).wait()
        total = None
        for k in range(5):
            part = ndot(weight_buf[step, k], turned_buf[k])
            total = part if total is None else total + part
        for tile in range(block // 128):
            level = total[tile * 128 : (tile + 1) * 128, :].T
            level_buf[tile, pl.ds(0, half, 2), :] = level[0:half]
            level_buf[tile, pl.ds(1, half, 2), :] = level[half:]
        cols = pl.ds(pl.multiple_of(step * block, block), block)

        def two(i, carry):
            at = pl.ds(pl.multiple_of(i * 256, 256), 256)
            state = state_buf[at, cols]
            pre = state * scale_buf[at, :] * gain[:, cols]
            slope = 0.5 * (1.0 + lax.erf(pre * 0.7071067811865476)) + pre * jnp.exp(
                -0.5 * pre * pre
            ) * 0.3989422804014327
            level = jnp.concatenate([level_buf[t, at, :] for t in range(block // 128)], axis=1)
            scaled = slope * level * gain[:, cols]
            scaled_buf[at, cols] = scaled
            product = state * scaled
            folded = product[:, 0:128]
            for tile in range(1, block // 128):
                folded = folded + product[:, tile * 128 : (tile + 1) * 128]
            sum_buf[at, :] = sum_buf[at, :] + folded
            return carry

        lax.fori_loop(0, rows // 256, two, 0)
        return carry

    lax.fori_loop(0, steps, one_block, 0)

    scale = scale_buf[...]
    coef = (scale * scale * scale) * (jnp.sum(sum_buf[...], axis=1, keepdims=True) * (1.0 / width))
    for tile in range(width // 128):
        lanes = slice(tile * 128, (tile + 1) * 128)
        own = grad_buf[pl.ds(16, half), lanes]
        scaled = scaled_buf[:, lanes]
        state = state_buf[:, lanes]
        level_buf[0, pl.ds(0, half, 2), :] = own
        level_buf[0, pl.ds(1, half, 2), :] = own
        out[:, lanes] = (level_buf[0] + (scale * scaled - state * coef)).astype(BF16)


def back(cells, skip, table, gain, grad, grad_prev, grad_next, weight, block=256):
    rows, width = skip.shape
    half = rows // 2
    whole = lambda array: pl.BlockSpec(array.shape, lambda n: (0,) * array.ndim)
    small = (cells, skip, table, gain, grad, grad_prev, grad_next)
    return pl.pallas_call(
        back_kernel,
        grid=(1,),
        in_specs=[whole(a) for a in small] + [pl.BlockSpec(memory_space=pl.ANY)],
        out_specs=pl.BlockSpec((rows, width), lambda n: (0, 0)),
        scratch_shapes=[
            pltpu.VMEM((rows, width), F32),
            pltpu.VMEM((rows, width), F32),
            pltpu.VMEM((half + 32, width), F32),
            pltpu.VMEM((5, width, rows), BF16),
            pltpu.VMEM((block // 128, rows, 128), F32),
            pltpu.VMEM((rows, 1), F32),
            pltpu.VMEM((rows, 128), F32),
            pltpu.VMEM((width // block, 5, block, width), BF16),
            pltpu.SemaphoreType.DMA((width // block,)),
        ],
        out_shape=jax.ShapeDtypeStruct((rows, width), BF16),
        compiler_params=pltpu.CompilerParams(vmem_limit_bytes=VMEM_LIMIT),
        cost_estimate=pl.CostEstimate(
            flops=2 * half * 5 * width * width, bytes_accessed=10 * width * width + 8 * rows * width, transcendentals=2 * rows * width
        ),
        name="back",
    )(*small, weight)


def attend_kernel(
    place, norm0, norm1, norm2, norm3, cot0, cot1, cot2, near, far,
    d_in, heads, normed, cot, w_out, own, part1, part2, part3, w_in, query_kv, acc,
):
    head = pl.program_id(0)
    seq, core, depth, level = place[0], place[1], place[2], place[3]
    inv = 1.0 / HD**0.5
    half = own.shape[0]
    cols = w_in.shape[1]
    side = near.shape[2]
    first = cols - side + HD

    def rows_of(index):
        return pl.ds(pl.multiple_of(index * half, half), half)

    @pl.when(head == 0)
    def _():
        for source, side_core in ((near, core), (far, 1 - core)):
            for turn in range(4):
                z = lax.rem(depth + turn, 4)
                for other in range(4):
                    y = lax.rem(level + other, 4)
                    at = pl.ds(pl.multiple_of((z * 4 + y) * 96 + side_core * 48, 16), 48)
                    w_in[at, 0:side] = source[turn, other * 48 : (other + 1) * 48, :]
                    w_in[at, side:cols] = source[turn, 336:384, other * 128 : (other + 1) * 128]
                at = pl.ds(pl.multiple_of(z * 96 + side_core * 48, 16), 48)
                for b in range(3):
                    w_out[at, b * side : (b + 1) * side] = source[
                        turn, 192 + b * 48 : 240 + b * 48, :
                    ]
        for piece, value in enumerate((norm0, norm1, norm2, norm3)):
            normed[rows_of(lax.rem(seq + piece, 4)), :] = value[...]
        beside = seq + 1 - 2 * lax.rem(seq, 2)
        cot[rows_of(seq), :] = cot0[...]
        cot[rows_of(beside), :] = cot1[...]
        cot[rows_of(3 - seq), :] = cot2[0]
        cot[rows_of(3 - beside), :] = cot2[1]
        query_kv[...] = ndot(normed[...], w_in[...]).astype(BF16)

    keys = query_kv[:, first : first + HD]
    values = query_kv[:, first + HD : first + HD + VD]
    lanes = pl.ds(pl.multiple_of(head * HD, HD), HD)
    q = query_kv[:, lanes]
    d_heads = rdot(cot[...], w_out[pl.ds(pl.multiple_of(head * VD, VD), VD), :]).astype(BF16)
    scores = rdot(q, keys) * inv
    expo = jnp.exp(scores - jnp.max(scores, axis=1, keepdims=True))
    probs = expo * (1.0 / jnp.sum(expo, axis=1, keepdims=True))
    weights = probs.astype(BF16)
    heads[0] = ndot(weights, values).astype(BF16)
    d_probs = rdot(d_heads, values)
    inner = jnp.sum(probs * d_probs, axis=1, keepdims=True)
    d_scores = (probs * (d_probs - inner) * inv).astype(BF16)
    d_in[:, lanes] = ndot(d_scores, keys).astype(BF16)
    d_keys = tdot(d_scores, q)
    d_values = tdot(weights, d_heads)

    @pl.when(head == 0)
    def _():
        acc[:, 0:HD] = d_keys
        acc[:, HD : HD + VD] = d_values

    @pl.when(head > 0)
    def _():
        acc[:, 0:HD] += d_keys
        acc[:, HD : HD + VD] += d_values

    @pl.when(head == pl.num_programs(0) - 1)
    def _():
        d_in[:, first + HD :] = jnp.zeros((4 * half, cols - first - HD), BF16)
        d_in[:, first : first + HD + VD] = acc[...].astype(BF16)
        for piece, out in enumerate((own, part1, part2, part3)):
            rows = d_in[rows_of(lax.rem(seq + piece, 4)), :]
            out[...] = rdot(rows, w_in[...]).astype(out.dtype)


def attend(place, norms, cots, near, far):
    half, width = norms[0].shape
    rows = 4 * half
    cols = near.shape[2] + 128
    heads = 2
    whole = lambda array: pl.BlockSpec(array.shape, lambda h, s: (0,) * array.ndim)
    outs = [
        jax.ShapeDtypeStruct((rows, cols), BF16),
        jax.ShapeDtypeStruct((heads, rows, VD), BF16),
        jax.ShapeDtypeStruct((rows, width), BF16),
        jax.ShapeDtypeStruct((rows, width), BF16),
        jax.ShapeDtypeStruct((heads * VD, width), BF16),
        jax.ShapeDtypeStruct((half, width), F32),
    ] + [jax.ShapeDtypeStruct((half, width), BF16)] * 3
    specs = [whole(out) for out in outs]
    specs[1] = pl.BlockSpec((1, rows, VD), lambda h, s: (h, 0, 0))
    ins = (*norms, *cots, near, far)
    return pl.pallas_call(
        attend_kernel,
        grid_spec=pltpu.PrefetchScalarGridSpec(
            num_scalar_prefetch=1,
            grid=(heads,),
            in_specs=[whole(a) for a in ins],
            out_specs=specs,
            scratch_shapes=[
                pltpu.VMEM((width, cols), BF16),
                pltpu.VMEM((rows, cols), BF16),
                pltpu.VMEM((rows, HD + VD), F32),
            ],
        ),
        out_shape=outs,
        compiler_params=pltpu.CompilerParams(vmem_limit_bytes=VMEM_LIMIT),
        cost_estimate=pl.CostEstimate(
            flops=2 * rows * heads * (VD * width + 3 * rows * (HD + VD)) + 4 * rows * cols * width,
            bytes_accessed=8 * rows * width + 2 * heads * VD * width + 2 * cols * width,
            transcendentals=rows * heads * rows,
        ),
        name="attend",
    )(place, *ins)


def grads_kernel(place, normed, d_in, heads, cot, own, other, rows_in, rows_out):
    core, depth = place[1], place[2]
    width = cot.shape[1]
    cols = d_in.shape[1]
    side = width // 2
    blocks = rows_in.shape[1] // 128
    for turn, out in enumerate((other, own)):
        half = core if turn else 1 - core
        lanes = pl.ds(pl.multiple_of(half * side, side), side)
        rows_in[:, 0:cols] = tdot(normed[:, lanes], d_in[...]).astype(BF16)
        rows_out[...] = tdot(heads[half], cot[...]).astype(BF16)
        for k in range(4):
            quarter = lax.rem(depth + k, 4)
            count = side // 4
            at = pl.ds(pl.multiple_of(quarter * count, count), count)
            for b in range(blocks):
                out[k, b * count : (b + 1) * count, :] = rows_in[at, b * 128 : (b + 1) * 128]
            base = blocks * count
            count = VD // 4
            at = pl.ds(pl.multiple_of(quarter * count, count), count)
            for b in range(width // 128):
                out[k, base + b * count : base + (b + 1) * count, :] = rows_out[
                    at, b * 128 : (b + 1) * 128
                ]


def grads(place, normed, d_in, heads, cot):
    rows, width = cot.shape
    cols = d_in.shape[1]
    blocks = (cols + 127) // 128
    length = blocks * (width // 8) + width // 128 * (VD // 4)
    whole = lambda array: pl.BlockSpec(array.shape, lambda n, s: (0,) * array.ndim)
    outs = [jax.ShapeDtypeStruct((4, length, 128), BF16)] * 2
    ins = (normed, d_in, heads, cot)
    return pl.pallas_call(
        grads_kernel,
        grid_spec=pltpu.PrefetchScalarGridSpec(
            num_scalar_prefetch=1,
            grid=(1,),
            in_specs=[whole(a) for a in ins],
            out_specs=[whole(a) for a in outs],
            scratch_shapes=[
                pltpu.VMEM((width // 2, blocks * 128), BF16),
                pltpu.VMEM((VD, width), BF16),
            ],
        ),
        out_shape=outs,
        compiler_params=pltpu.CompilerParams(vmem_limit_bytes=VMEM_LIMIT),
        cost_estimate=pl.CostEstimate(
            flops=2 * rows * width * (cols + 2 * VD),
            bytes_accessed=16 * rows * width,
            transcendentals=0,
        ),
        name="grads",
    )(place, *ins)


def mix_kernel(place, heads, w_out, out):
    total = ndot(heads[0], w_out[0:VD, :]) + ndot(heads[1], w_out[VD : 2 * VD, :])
    out[0] = total.astype(BF16)


def mix(place, heads, w_out):
    rows = heads.shape[1] // 4
    width = w_out.shape[1]
    return pl.pallas_call(
        mix_kernel,
        grid_spec=pltpu.PrefetchScalarGridSpec(
            num_scalar_prefetch=1,
            grid=(4,),
            in_specs=[
                pl.BlockSpec((2, rows, VD), lambda n, s: (0, lax.rem(s[0] + n, 4), 0)),
                pl.BlockSpec(w_out.shape, lambda n, s: (0, 0)),
            ],
            out_specs=pl.BlockSpec((1, rows, width), lambda n, s: (n, 0, 0)),
        ),
        out_shape=jax.ShapeDtypeStruct((4, rows, width), BF16),
        compiler_params=pltpu.CompilerParams(vmem_limit_bytes=VMEM_LIMIT),
        cost_estimate=pl.CostEstimate(
            flops=16 * rows * width * VD, bytes_accessed=12 * rows * width, transcendentals=0
        ),
        name="mix",
    )(place, heads, w_out)


AXES = ("z", "y", "c", "x")
SIZES = (4, 4, 2, 4)


def place(z, y, c, x):
    return ((z * 4 + y) * 2 + c) * 4 + x


def moved(value, target):
    pairs = []
    for z in range(4):
        for y in range(4):
            for c in range(2):
                for x in range(4):
                    pairs.append((place(z, y, c, x), place(*target(z, y, c, x))))
    return lax.ppermute(value, AXES, pairs)


def flipped(value):
    return moved(value, lambda z, y, c, x: (z, y, 1 - c, x))


def turned(value, axis, by):
    return lax.ppermute(value, axis, [(i, (i + by) % 4) for i in range(4)])


def gathered(value, axis):
    me = lax.axis_index(axis)
    parts = [value, turned(value, axis, 3), turned(value, axis, 2), turned(value, axis, 1)]
    out = jnp.zeros((4, *value.shape), value.dtype)
    for j in range(4):
        out = lax.dynamic_update_index_in_dim(out, parts[j], lax.rem(me + j, 4), 0)
    return out


def summed(value, axis, dtype=BF16):
    me = lax.axis_index(axis)
    parts = [
        lax.dynamic_index_in_dim(value, lax.rem(me + j, 4), 0, keepdims=False) for j in range(4)
    ]
    total = parts[0].astype(F32)
    for j in range(1, 4):
        total = total + turned(parts[j], axis, j).astype(F32)
    return total.astype(dtype)


def by_core(own, other):
    first = lax.axis_index("c") == 0
    return jnp.where(first, own, other), jnp.where(first, other, own)


def around(value, axis="x"):
    return [value, turned(value, axis, 3), turned(value, axis, 2), turned(value, axis, 1)]


def returned(pieces):
    total = pieces[0].astype(F32)
    for k in range(1, 4):
        total = total + turned(pieces[k], "x", k).astype(F32)
    return total


def returned_along(pieces, axis):
    total = pieces[0].astype(F32)
    for k in range(1, 4):
        total = total + turned(pieces[k], axis, k).astype(F32)
    return total.astype(BF16)


def gather_in_x(w_query, w_kv):
    seq = lax.axis_index("x")
    cols = w_query.shape[1] // 4
    rows = jnp.zeros((4, w_query.shape[0], cols + w_kv.shape[1]), BF16)
    for k in range(4):
        head_cols = lax.dynamic_slice_in_dim(w_query, lax.rem(seq + k, 4) * cols, cols, 1)
        piece = jnp.concatenate([head_cols, w_kv], axis=1)
        if k:
            piece = turned(piece, "x", k)
        rows = lax.dynamic_update_index_in_dim(rows, piece, lax.rem(seq + 4 - k, 4), 0)
    return rows.reshape(48, rows.shape[2])


def after(value, *others):
    return lax.optimization_barrier((value, *others))[0]


def split_rows(pieces):
    first = pieces[:960].reshape(5, 4, 48, 128).transpose(1, 0, 2, 3).reshape(4, 240, 128)
    second = pieces[960:].reshape(12, 4, 12, 128).transpose(1, 0, 2, 3).reshape(4, 144, 128)
    return jnp.concatenate([first, second], axis=1)


def finish(value, cols, width):
    seq = lax.axis_index("x")
    pieces = value[:240].reshape(5, 4, 12, 128).transpose(1, 2, 0, 3).reshape(4, 12, 640)
    grad_query = jnp.zeros((4, 12, cols), F32)
    grad_kv = jnp.zeros((12, HD + VD), F32)
    for k in range(4):

        def home(z, y, c, x):
            block = 16 * c + 4 * z + y
            return block // 8, block // 2 % 4, block % 2, (x + k) % 4

        piece = lax.dynamic_index_in_dim(pieces, lax.rem(seq + k, 4), 0, keepdims=False)
        piece = moved(piece, home).astype(F32)
        grad_query = lax.dynamic_update_index_in_dim(
            grad_query, piece[:, :cols], lax.rem(seq + 4 - k, 4), 0
        )
        grad_kv = grad_kv + piece[:, cols : cols + HD + VD]
    grad_query = grad_query.transpose(1, 0, 2).reshape(12, 4 * cols)
    grad_out = value[240:].reshape(12, 12, 128).transpose(1, 0, 2).reshape(12, width)
    grad_out = moved(grad_out, lambda z, y, c, x: (x, 2 * c + z // 2, z % 2, y)).astype(F32)
    return grad_query, grad_kv, grad_out


def rms_back(value, gain, grad):
    scale = row_scale(value)
    scaled = grad * gain
    return scale * scaled - value * (scale * scale * scale) * jnp.mean(
        value * scaled, axis=-1, keepdims=True
    )


def per_device(
    bases, skip, base_table, conv_weight, conv_gain, attn_gain, w_query, w_kv, w_out, cotangent
):
    skip = skip[0]
    cot = cotangent[0]
    rows, width = skip.shape
    half = rows // 2
    cells = bases.reshape(rows, bases.shape[1] // rows)
    seq = lax.axis_index("x")
    ends = jnp.stack([seq, 3 - seq]).astype(jnp.int32)

    def ahead(value):
        return lax.ppermute(value, "x", [(i, i + 1) for i in range(3)])

    def behind(value):
        return lax.ppermute(value, "x", [(i + 1, i) for i in range(3)])

    def edge(tokens, features):
        tokens = tokens.reshape(8, -1)
        counts = [jnp.sum((tokens == b).astype(F32), axis=1, keepdims=True) for b in range(4)]
        counts = jnp.concatenate(counts + [jnp.zeros((8, 124), F32)], axis=1)
        return jnp.concatenate([features, counts.astype(BF16)], axis=1)

    span = 8 * (bases.shape[1] // rows)
    edge_prev = ahead(edge(bases[0, bases.shape[1] - span :], skip[rows - 8 :]))
    edge_next = behind(edge(bases[0, :span], skip[:8]))
    w_rows = gather_in_x(w_query, w_kv)
    out_home = moved(w_out, lambda z, y, c, x: (y, x, c, z))
    beside = lax.ppermute(after(cot, w_rows), "x", [(i, i ^ 1) for i in range(4)])
    across = lax.ppermute(jnp.stack([cot, beside]), "x", [(i, 3 - i) for i in range(4)])
    pieces = around(w_rows, "y")
    out_rows = gathered(out_home, "y").reshape(48, width)
    side = width // 3
    joint = jnp.concatenate(
        [piece[:, :side] for piece in pieces]
        + [out_rows[:, p * side : (p + 1) * side] for p in range(3)]
        + [
            jnp.concatenate(
                [jnp.pad(piece[:, side:], ((0, 0), (0, 64))) for piece in pieces], axis=1
            )
        ],
        axis=0,
    )
    near = jnp.stack(around(joint, "z"))

    gain = conv_gain[None, :]
    pooled, normed = front(
        ends, cells, skip, edge_prev, edge_next, base_table, gain, attn_gain[None, :], conv_weight
    )
    norms = around(normed)
    far = flipped(after(near, normed, across))

    spot = [seq, lax.axis_index("c"), lax.axis_index("z"), lax.axis_index("y")]
    spot = jnp.stack(spot).astype(jnp.int32)
    d_in, heads, normed_all, cot_all, full_out, *d_parts = attend(spot, norms, (cot, beside, across), near, far)
    d_parts[1:] = [turned(d_parts[k], "x", k) for k in range(1, 4)]
    own, other = grads(spot, normed_all, d_in, heads, cot_all)
    mine = (own.astype(F32) + flipped(other).astype(F32)).astype(BF16)
    out_parts = mix(spot, after(heads, mine), full_out)
    d_normed = d_parts[0]
    for k in range(1, 4):
        d_normed = d_normed + after(d_parts[k], mine).astype(F32)
    mine = returned_along(mine, "z")

    d_pooled = cot.astype(F32) + rms_back(pooled, attn_gain, d_normed)
    grad = (d_pooled * 0.5).astype(BF16)
    grad_prev, grad_next = ahead(grad[half - 16 :]), behind(grad[:16])
    coarse = (pooled + returned(after(out_parts, grad_prev))).astype(BF16)
    skip_grad = back(cells, skip, base_table, gain, grad, grad_prev, grad_next, conv_weight)

    factor = 1.0 / 32
    mine = summed(split_rows(mine), "y")
    cols = w_query.shape[1] // 4
    grad_query, grad_kv, grad_out = finish(mine, cols, width)
    return (
        coarse[None],
        skip_grad[None],
        grad_query * factor,
        grad_kv * factor,
        grad_out * factor,
    )


def solution(mesh):
    inner = Mesh(mesh.devices.reshape(SIZES), AXES)
    dp = ("z", "y", "c")
    every = AXES
    placed = (
        P(dp, "x"),
        P(dp, "x", None),
        P(),
        P(),
        P(),
        P(),
        P(every, None),
        P(every, None),
        P(every, None),
        P(dp, "x", None),
    )
    return jax.shard_map(
        per_device,
        mesh=inner,
        in_specs=placed,
        out_specs=(
            P(dp, "x", None),
            P(dp, "x", None),
            P(every, None),
            P(every, None),
            P(every, None),
        ),
        check_vma=False,
    )
```

time: 440 us -> 209 us (0.47)
  waiting for transfers between devices: 204 us -> 48.7 us
  blocking collectives: 81.2 us -> 0 us
  matrix products: 69.7 us -> 0 us
  starting transfers between devices: 9.36 us -> 78.1 us
  Pallas kernels: 0 us -> 51.8 us
  local copies, waits for them, and re-layouts: 39.3 us -> 12.1 us
  between operations: 14.2 us -> 1.44 us
    unnamed x6 -> x0, waiting for transfers between devices: 189 us -> none
    all_gather x2 -> x0, blocking collectives: 81.2 us -> none  [the longest x1 69.8 us: per_device(): lax.all_gather(w_kv, ('dp', 'seq'), axis=0, tiled=True)]
    ppermute x4 -> x41, starting transfers between devices: 9.21 us -> 78.1 us  [the longest x27 32.8 us: turned(): return lax.ppermute(value, axis, [(i, (i + by) % 4) for i in range(4)])]
    dot_general x16 -> x0, matrix products: 66.5 us -> none  [the longest x1 14 us: conv_backward(): lax.dot_general(window, weight, (((1, 2), (0, 2)), ((), ())), preferred_e...]
    pallas_call x0 -> x5, Pallas kernels: none -> 51.8 us  [the longest x1 14.9 us: attend(): pl.pallas_call(attend_kernel, grid_spec=pltpu.PrefetchScalarGridSpec(num_...]
    ppermute x4 -> x41, waiting for transfers between devices: 0.32 us -> 48.7 us  [the longest x27 41.2 us: turned(): return lax.ppermute(value, axis, [(i, (i + by) % 4) for i in range(4)])]
    unnamed x51 -> x60, local copies, waits for them, and re-layouts: 28.5 us -> 4.6 us
    all_gather x2 -> x0, waiting for transfers between devices: 15.1 us -> none  [the longest x1 15.1 us: per_device(): lax.all_gather(w_out, ('dp', 'seq'), axis=0, tiled=True)]
  transfers between devices with their start and end apart: 8 -> 41, of which waited for: 4 -> 11; matrix products, arithmetic and copies ran while one was open for 19% -> 10% of each run, Pallas kernels for 0% -> 14%
where the time goes in v1:
time: 209 us; the launch traced here: 208 us
  starting transfers between devices  78.1 us (37%)
  Pallas kernels  51.8 us (25%)
  waiting for transfers between devices  48.7 us (23%)
  other arithmetic  15.6 us (7%)
  local copies, waits for them, and re-layouts  12.1 us (6%)
    ppermute x27, waiting for transfers between devices, turned(): return lax.ppermute(value, axis, [(i, (i + by) % 4) for i in range(4)])  41.2 us
    ppermute x27, starting transfers between devices, turned(): return lax.ppermute(value, axis, [(i, (i + by) % 4) for i in range(4)])  32.8 us
    ppermute x8, starting transfers between devices, moved(): return lax.ppermute(value, AXES, pairs)  32.5 us
    pallas_call x1, Pallas kernels, attend(): pl.pallas_call(attend_kernel, grid_spec=pltpu.PrefetchScalarGridSpec(num_...  14.9 us
    pallas_call x1, Pallas kernels, back(): pl.pallas_call(back_kernel, grid=(1,), in_specs=[whole(a) for a in small]...  12.9 us
    pallas_call x1, Pallas kernels, front(): pl.pallas_call(front_kernel, grid_spec=pltpu.PrefetchScalarGridSpec(num_s...  11.6 us
    ppermute x2, starting transfers between devices, behind(): return lax.ppermute(value, 'x', [(i + 1, i) for i in range(3)])  8.57 us
    ppermute x8, waiting for transfers between devices, moved(): return lax.ppermute(value, AXES, pairs)  7.45 us
  transfers between devices with their start and end apart: 41, of which 11 were waited for; matrix products, arithmetic and copies ran while one was open for 10% of the time, Pallas kernels for 14%

profile of v1, /device:TPU:15, one launch (start us, length us, event | category | flops | bytes accessed | tf_op | source)
XLA Modules:
  0.0 207.8 jit_solution(12125619835846689038)
XLA Ops:
  6.1 4.0 %collective-permute-start.1 = (bf16[8,1664]{1,0:T(8,128)(2,1)S(1)}, bf16[8,1664]{1,0:T(8,128)(2,1)S(1)}, u32[]{:S(2)}, u32[]{:S(2)}) collective-permute-start(bf16[8,1664]{1,0:T(8,128)(2,1)S(1)} %concatenate.34), channel_id=1, source_target_pairs={{1,0},{2,1},{3,2},{5,4},{6,5},{7,6},{9,8},{10,9},{11,10},{13,12},{... | collective-permute-start | bytes 79880 | tf_op jit(solution)/shard_map/ppermute | solution.py:613
  11.6 2.3 %collective-permute-start.6 = (bf16[12,576]{1,0:T(8,128)(2,1)S(1)}, bf16[12,576]{1,0:T(8,128)(2,1)S(1)}, u32[]{:S(2)}, u32[]{:S(2)}) collective-permute-start(bf16[12,576]{1,0:T(8,128)(2,1)S(1)} %get-tuple-element.78), channel_id=1, source_target_pairs={{0,2},{1,3},{2,0},{3,1},{4,6},{5,7},{6,4},{7,5},{8,10},{9,11},{10,... | collective-permute-start | bytes 41480 | tf_op jit(solution)/shard_map/ppermute | solution.py:498
  14.7 7.7 %collective-permute-start.13 = (bf16[12,1536]{1,0:T(8,128)(2,1)}, bf16[12,1536]{1,0:T(8,128)(2,1)S(1)}, u32[]{:S(2)}, u32[]{:S(2)}) collective-permute-start(bf16[12,1536]{1,0:T(8,128)(2,1)} %param.18), channel_id=1, source_target_pairs={{0,0},{1,8},{2,16},{3,24},{4,4},{5,12},{6,20},{7,28},{8,32},{9,40}... | collective-permute-start | bytes 110600 | tf_op jit(solution)/shard_map/ppermute | solution.py:490
  22.6 3.4 %collective-permute-start.11 = (bf16[48,576]{1,0:T(8,128)(2,1)S(1)}, bf16[48,576]{1,0:T(8,128)(2,1)S(1)}, u32[]{:S(2)}, u32[]{:S(2)}) collective-permute-start(bf16[48,576]{1,0:T(8,128)(2,1)S(1)} %reshape.106), channel_id=1, source_target_pairs={{0,16},{8,24},{16,0},{24,8},{1,17},{9,25},{17,1},{25,9},{2,18},{10... | collective-permute-start | bytes 165896 | tf_op jit(solution)/shard_map/ppermute | solution.py:498
  37.8 3.0 %collective-permute-start.18 = (bf16[384,512]{1,0:T(8,128)(2,1)S(1)}, bf16[384,512]{1,0:T(8,128)(2,1)S(1)}, u32[]{:S(2)}, u32[]{:S(2)}) collective-permute-start(bf16[384,512]{1,0:T(8,128)(2,1)S(1)} %fusion.27), channel_id=1, source_target_pairs={{0,64},{32,96},{64,0},{96,32},{1,65},{33,97},{65,1},{97,33},{2,66}... | collective-permute-start | bytes 1179656 | tf_op jit(solution)/shard_map/ppermute | solution.py:498
  46.3 11.6 %front.1 = (f32[128,1536]{1,0:T(8,128)}, bf16[128,1536]{1,0:T(8,128)(2,1)}) custom-call(s32[2]{0:T(128)} %pad_add_fusion.ends, s32[256,64]{1,0:T(8,128)} %reshape.105.cells, bf16[256,1536]{1,0:T(8,128)(2,1)} %bitcast.137, bf16[8,1664]{1,0:T(8,128)(2,1)} %copy-done.13, bf16[8,1664]{1,0:T(8,128)(2,1)} %copy-done.14, f32[4,1536]{1,0:T(4,128)} %table.3, ...), custom_call_target="tpu_custom_call" | custom-call | flops 3019898880 | bytes 26738688 | tf_op jit(solution)/shard_map/front/pallas_call | solution.py:129
  59.9 7.1 %collective-permute-start.20 = (bf16[4,384,512]{2,1,0:T(8,128)(2,1)S(1)}, bf16[4,384,512]{2,1,0:T(8,128)(2,1)}, u32[]{:S(2)}, u32[]{:S(2)}) collective-permute-start(bf16[4,384,512]{2,1,0:T(8,128)(2,1)S(1)} %pad_maximum_fusion.near), channel_id=1, source_target_pairs={{0,4},{1,5},{2,6},{3,7},{4,0},{5,1},{6,2},{7,3},{8,12},{9,13},{10,... | collective-permute-start | bytes 4718600 | tf_op jit(solution)/shard_map/ppermute | solution.py:490
  70.4 17.2 %collective-permute-done.2.norm1 = bf16[128,1536]{1,0:T(8,128)(2,1)S(1)} collective-permute-done((bf16[128,1536]{1,0:T(8,128)(2,1)}, bf16[128,1536]{1,0:T(8,128)(2,1)S(1)}, u32[]{:S(2)}, u32[]{:S(2)}) %collective-permute-start.2) | collective-permute-done | bytes 393248 | tf_op jit(solution)/shard_map/ppermute | solution.py:498
  88.7 14.9 %attend.1 = (bf16[512,640]{1,0:T(8,128)(2,1)}, bf16[2,512,192]{2,1,0:T(8,128)(2,1)}, bf16[512,1536]{1,0:T(8,128)(2,1)}, bf16[512,1536]{1,0:T(8,128)(2,1)}, bf16[...) custom-call(s32[4]{0:T(128)} %pad_add_fusion.1.place, ...), custom_call_target="tpu_custom_call" | custom-call | flops 3623878656 | bytes 9437184 | tf_op jit(solution)/shard_map/attend/pallas_call | solution.py:366
  103.6 7.2 %grads.1 = (bf16[4,1536,128]{2,1,0:T(8,128)(2,1)}, bf16[4,1536,128]{2,1,0:T(8,128)(2,1)}) custom-call(s32[4]{0:T(128)} %pad_add_fusion.1.place, bf16[512,1536]{1,0:T(8,128)(2,1)} %get-tuple-element.30.normed, bf16[512,640]{1,0:T(8,128)(2,1)} %get-tuple-element.31.d_in, bf16[2,512,192]{2,1,0:T(8,128)(2,1)} %get-tuple-element.35.heads, ...), custom_call_target="tpu_custom_call" | custom-call | flops 1610612736 | bytes 12582912 | tf_op jit(solution)/shard_map/grads/pallas_call | solution.py:424
  112.0 3.2 %collective-permute-start.23 = (bf16[128,1536]{1,0:T(8,128)(2,1)S(1)}, bf16[128,1536]{1,0:T(8,128)(2,1)S(1)}, u32[]{:S(2)}, u32[]{:S(2)}) collective-permute-start(bf16[128,1536]{1,0:T(8,128)(2,1)S(1)} %copy-done.18), channel_id=1, source_target_pairs={{0,2},{1,3},{2,0},{3,1},{4,6},{5,7},{6,4},{7,5},{8,10},{9,11},{10,... | collective-permute-start | bytes 1179656 | tf_op jit(solution)/shard_map/ppermute | solution.py:498
  116.4 2.3 %add_convert_fusion = bf16[4,1536,128]{2,1,0:T(8,128)(2,1)S(1)} fusion(bf16[4,1536,128]{2,1,0:T(8,128)(2,1)} %copy-done.5, bf16[4,1536,128]{2,1,0:T(8,128)(2,1)} %get-tuple-element.33), kind=kLoop, calls=%fused_computation | loop fusion | flops 3145728 | bytes 4718592 | tf_op jit(solution)/shard_map/convert_element_type | solution.py:655
  118.7 5.2 %collective-permute-done.24 = bf16[128,1536]{1,0:T(8,128)(2,1)S(1)} collective-permute-done((bf16[128,1536]{1,0:T(8,128)(2,1)S(1)}, bf16[128,1536]{1,0:T(8,128)(2,1)S(1)}, u32[]{:S(2)}, u32[]{:S(2)}) %collective-permute-start.24) | collective-permute-done | bytes 393248 | tf_op jit(solution)/shard_map/ppermute | solution.py:498
  123.9 9.0 %collective-permute-done.23 = bf16[128,1536]{1,0:T(8,128)(2,1)S(1)} collective-permute-done((bf16[128,1536]{1,0:T(8,128)(2,1)S(1)}, bf16[128,1536]{1,0:T(8,128)(2,1)S(1)}, u32[]{:S(2)}, u32[]{:S(2)}) %collective-permute-start.23) | collective-permute-done | bytes 393248 | tf_op jit(solution)/shard_map/ppermute | solution.py:498
  133.1 2.6 %collective-permute-start.31 = (bf16[1536,128]{1,0:T(8,128)(2,1)S(1)}, bf16[1536,128]{1,0:T(8,128)(2,1)}, u32[]{:S(2)}, u32[]{:S(2)}) collective-permute-start(bf16[1536,128]{1,0:T(8,128)(2,1)S(1)} %get-tuple-element.57), channel_id=1, source_target_pairs={{0,64},{32,96},{64,0},{96,32},{1,65},{33,97},{65,1},{97,33},{2,66}... | collective-permute-start | bytes 1179656 | tf_op jit(solution)/shard_map/ppermute | solution.py:498
  138.6 4.6 %collective-permute-start.29 = (bf16[16,1536]{1,0:T(8,128)(2,1)}, bf16[16,1536]{1,0:T(8,128)(2,1)}, u32[]{:S(2)}, u32[]{:S(2)}) collective-permute-start(bf16[16,1536]{1,0:T(8,128)(2,1)} %get-tuple-element.66), channel_id=1, source_target_pairs={{1,0},{2,1},{3,2},{5,4},{6,5},{7,6},{9,8},{10,9},{11,10},{13,12},{... | collective-permute-start | bytes 147464 | tf_op jit(solution)/shard_map/ppermute | solution.py:613
  143.2 5.2 %mix.1 = bf16[4,128,1536]{2,1,0:T(8,128)(2,1)} custom-call(s32[4]{0:T(128)} %pad_add_fusion.1.place, bf16[2,512,192]{2,1,0:T(8,128)(2,1)} %get-tuple-element.35.heads, bf16[384,1536]{1,0:T(8,128)(2,1)} %get-tuple-element.36.w_out), custom_call_target="tpu_custom_call" | custom-call | flops 603979776 | bytes 2359296 | tf_op jit(solution)/shard_map/mix/pallas_call | solution.py:455
  148.4 5.8 %collective-permute-done.30 = bf16[1536,128]{1,0:T(8,128)(2,1)} collective-permute-done((bf16[1536,128]{1,0:T(8,128)(2,1)S(1)}, bf16[1536,128]{1,0:T(8,128)(2,1)}, u32[]{:S(2)}, u32[]{:S(2)}) %collective-permute-start.30) | collective-permute-done | bytes 393248 | tf_op jit(solution)/shard_map/ppermute | solution.py:498
  159.2 3.5 %collective-permute-start.27 = (bf16[128,1536]{1,0:T(8,128)(2,1)S(1)}, bf16[128,1536]{1,0:T(8,128)(2,1)}, u32[]{:S(2)}, u32[]{:S(2)}) collective-permute-start(bf16[128,1536]{1,0:T(8,128)(2,1)S(1)} %get-tuple-element.60), channel_id=1, source_target_pairs={{0,2},{1,3},{2,0},{3,1},{4,6},{5,7},{6,4},{7,5},{8,10},{9,11},{10,... | collective-permute-start | bytes 1179656 | tf_op jit(solution)/shard_map/ppermute | solution.py:498
  165.0 12.9 %back.1 = bf16[256,1536]{1,0:T(8,128)(2,1)} custom-call(s32[256,64]{1,0:T(8,128)} %reshape.105.cells, bf16[256,1536]{1,0:T(8,128)(2,1)} %bitcast.138, f32[4,1536]{1,0:T(4,128)} %table.3, f32[1,1536]{1,0:T(1,128)} %broadcast_in_dim.103.gain, bf16[128,1536]{1,0:T(8,128)(2,1)} %copy-done.3, bf16[16,1536]{1,0:T(8,128)(2,1)} %copy-done.12, ...), custom_call_target="tpu_custom_call" | custom-call | flops 3019898880 | bytes 26738688 | tf_op jit(solution)/shard_map/back/pallas_call | solution.py:249
  182.3 5.1 %collective-permute-start.36 = (bf16[12,640]{1,0:T(8,128)(2,1)S(1)}, bf16[12,640]{1,0:T(8,128)(2,1)S(1)}, u32[]{:S(2)}, u32[]{:S(2)}) collective-permute-start(bf16[12,640]{1,0:T(8,128)(2,1)S(1)} %bitcast.161), channel_id=1, source_target_pairs={{0,0},{1,1},{2,2},{3,3},{4,64},{5,65},{6,66},{7,67},{8,4},{9,5},{1... | collective-permute-start | bytes 46088 | tf_op jit(solution)/shard_map/ppermute | solution.py:490
  187.4 7.6 %collective-permute-start.37 = (bf16[12,640]{1,0:T(8,128)(2,1)S(1)}, bf16[12,640]{1,0:T(8,128)(2,1)S(1)}, u32[]{:S(2)}, u32[]{:S(2)}) collective-permute-start(bf16[12,640]{1,0:T(8,128)(2,1)S(1)} %bitcast.160), channel_id=1, source_target_pairs={{0,1},{1,2},{2,3},{3,0},{4,65},{5,66},{6,67},{7,64},{8,5},{9,6},{1... | collective-permute-start | bytes 46088 | tf_op jit(solution)/shard_map/ppermute | solution.py:490
  198.2 3.9 %collective-permute-done.38 = bf16[12,640]{1,0:T(8,128)(2,1)S(1)} collective-permute-done((bf16[12,640]{1,0:T(8,128)(2,1)S(1)}, bf16[12,640]{1,0:T(8,128)(2,1)S(1)}, u32[]{:S(2)}, u32[]{:S(2)}) %collective-permute-start.38) | collective-permute-done | bytes 15392 | tf_op jit(solution)/shard_map/ppermute | solution.py:490
  203.6 3.5 %collective-permute-done.40 = bf16[12,1536]{1,0:T(8,128)(2,1)S(1)} collective-permute-done((bf16[12,1536]{1,0:T(8,128)(2,1)S(1)}, bf16[12,1536]{1,0:T(8,128)(2,1)S(1)}, u32[]{:S(2)}, u32[]{:S(2)}) %collective-permute-start.40) | collective-permute-done | bytes 36896 | tf_op jit(solution)/shard_map/ppermute | solution.py:490
  (219 shorter events, 53.4 us)
Async XLA Ops:
  3.5 37.3 %collective-permute-start = (bf16[8,1664]{1,0:T(8,128)(2,1)S(1)}, bf16[8,1664]{1,0:T(8,128)(2,1)S(1)}, u32[]{:S(2)}, u32[]{:S(2)}) collective-permute-start(bf16[8,1664]{1,0:T(8,128)(2,1)S(1)} %concatenate.33), channel_id=1, source_target_pairs={{0,1},{1,2},{2,3},{4,5},{5,6},{6,7},{8,9},{9,10},{10,11},{12,13},{... | collective-permute-start | bytes 79880 | tf_op jit(solution)/shard_map/ppermute | solution.py:610
  6.1 39.6 %collective-permute-start.1 = (bf16[8,1664]{1,0:T(8,128)(2,1)S(1)}, bf16[8,1664]{1,0:T(8,128)(2,1)S(1)}, u32[]{:S(2)}, u32[]{:S(2)}) collective-permute-start(bf16[8,1664]{1,0:T(8,128)(2,1)S(1)} %concatenate.34), channel_id=1, source_target_pairs={{1,0},{2,1},{3,2},{5,4},{6,5},{7,6},{9,8},{10,9},{11,10},{13,12},{... | collective-permute-start | bytes 79880 | tf_op jit(solution)/shard_map/ppermute | solution.py:613
  35.6 24.2 %collective-permute-start.9 = (bf16[2,128,1536]{2,1,0:T(8,128)(2,1)S(1)}, bf16[2,128,1536]{2,1,0:T(8,128)(2,1)}, u32[]{:S(2)}, u32[]{:S(2)}) collective-permute-start(bf16[2,128,1536]{2,1,0:T(8,128)(2,1)S(1)} %pad_maximum_fusion.1), channel_id=1, source_target_pairs={{0,3},{1,2},{2,1},{3,0},{4,7},{5,6},{6,5},{7,4},{8,11},{9,10},{10,... | collective-permute-start | bytes 2359304 | tf_op jit(solution)/shard_map/ppermute | solution.py:627
  36.4 21.4 %collective-permute-start.19 = (bf16[384,512]{1,0:T(8,128)(2,1)S(1)}, bf16[384,512]{1,0:T(8,128)(2,1)S(1)}, u32[]{:S(2)}, u32[]{:S(2)}) collective-permute-start(bf16[384,512]{1,0:T(8,128)(2,1)S(1)} %fusion.27), channel_id=1, source_target_pairs={{0,32},{32,64},{64,96},{96,0},{1,33},{33,65},{65,97},{97,1},{2,34}... | collective-permute-start | bytes 1179656 | tf_op jit(solution)/shard_map/ppermute | solution.py:498
  37.8 20.1 %collective-permute-start.18 = (bf16[384,512]{1,0:T(8,128)(2,1)S(1)}, bf16[384,512]{1,0:T(8,128)(2,1)S(1)}, u32[]{:S(2)}, u32[]{:S(2)}) collective-permute-start(bf16[384,512]{1,0:T(8,128)(2,1)S(1)} %fusion.27), channel_id=1, source_target_pairs={{0,64},{32,96},{64,0},{96,32},{1,65},{33,97},{65,1},{97,33},{2,66}... | collective-permute-start | bytes 1179656 | tf_op jit(solution)/shard_map/ppermute | solution.py:498
  40.8 17.1 %collective-permute-start.17 = (bf16[384,512]{1,0:T(8,128)(2,1)S(1)}, bf16[384,512]{1,0:T(8,128)(2,1)S(1)}, u32[]{:S(2)}, u32[]{:S(2)}) collective-permute-start(bf16[384,512]{1,0:T(8,128)(2,1)S(1)} %fusion.27), channel_id=1, source_target_pairs={{0,96},{32,0},{64,32},{96,64},{1,97},{33,1},{65,33},{97,65},{2,98}... | collective-permute-start | bytes 1179656 | tf_op jit(solution)/shard_map/ppermute | solution.py:498
  59.9 28.0 %collective-permute-start.20 = (bf16[4,384,512]{2,1,0:T(8,128)(2,1)S(1)}, bf16[4,384,512]{2,1,0:T(8,128)(2,1)}, u32[]{:S(2)}, u32[]{:S(2)}) collective-permute-start(bf16[4,384,512]{2,1,0:T(8,128)(2,1)S(1)} %pad_maximum_fusion.near), channel_id=1, source_target_pairs={{0,4},{1,5},{2,6},{3,7},{4,0},{5,1},{6,2},{7,3},{8,12},{9,13},{10,... | collective-permute-start | bytes 4718600 | tf_op jit(solution)/shard_map/ppermute | solution.py:490
  67.0 20.5 %collective-permute-start.2 = (bf16[128,1536]{1,0:T(8,128)(2,1)}, bf16[128,1536]{1,0:T(8,128)(2,1)S(1)}, u32[]{:S(2)}, u32[]{:S(2)}) collective-permute-start(bf16[128,1536]{1,0:T(8,128)(2,1)} %get-tuple-element.26.norm0), channel_id=1, source_target_pairs={{0,3},{1,0},{2,1},{3,2},{4,7},{5,4},{6,5},{7,6},{8,11},{9,8},{10,9... | collective-permute-start | bytes 1179656 | tf_op jit(solution)/shard_map/ppermute | solution.py:498
  67.0 20.5 %collective-permute-start.3 = (bf16[128,1536]{1,0:T(8,128)(2,1)}, bf16[128,1536]{1,0:T(8,128)(2,1)S(1)}, u32[]{:S(2)}, u32[]{:S(2)}) collective-permute-start(bf16[128,1536]{1,0:T(8,128)(2,1)} %get-tuple-element.26.norm0), channel_id=1, source_target_pairs={{0,2},{1,3},{2,0},{3,1},{4,6},{5,7},{6,4},{7,5},{8,10},{9,11},{10,... | collective-permute-start | bytes 1179656 | tf_op jit(solution)/shard_map/ppermute | solution.py:498
  68.0 19.9 %collective-permute-start.4 = (bf16[128,1536]{1,0:T(8,128)(2,1)}, bf16[128,1536]{1,0:T(8,128)(2,1)S(1)}, u32[]{:S(2)}, u32[]{:S(2)}) collective-permute-start(bf16[128,1536]{1,0:T(8,128)(2,1)} %get-tuple-element.26.norm0), channel_id=1, source_target_pairs={{0,1},{1,2},{2,3},{3,0},{4,5},{5,6},{6,7},{7,4},{8,9},{9,10},{10,1... | collective-permute-start | bytes 1179656 | tf_op jit(solution)/shard_map/ppermute | solution.py:498
  112.0 11.9 %collective-permute-start.24 = (bf16[128,1536]{1,0:T(8,128)(2,1)S(1)}, bf16[128,1536]{1,0:T(8,128)(2,1)S(1)}, u32[]{:S(2)}, u32[]{:S(2)}) collective-permute-start(bf16[128,1536]{1,0:T(8,128)(2,1)S(1)} %copy-done.20), channel_id=1, source_target_pairs={{0,3},{1,0},{2,1},{3,2},{4,7},{5,4},{6,5},{7,6},{8,11},{9,8},{10,9... | collective-permute-start | bytes 1179656 | tf_op jit(solution)/shard_map/ppermute | solution.py:498
  112.0 20.9 %collective-permute-start.23 = (bf16[128,1536]{1,0:T(8,128)(2,1)S(1)}, bf16[128,1536]{1,0:T(8,128)(2,1)S(1)}, u32[]{:S(2)}, u32[]{:S(2)}) collective-permute-start(bf16[128,1536]{1,0:T(8,128)(2,1)S(1)} %copy-done.18), channel_id=1, source_target_pairs={{0,2},{1,3},{2,0},{3,1},{4,6},{5,7},{6,4},{7,5},{8,10},{9,11},{10,... | collective-permute-start | bytes 1179656 | tf_op jit(solution)/shard_map/ppermute | solution.py:498
  115.3 17.7 %collective-permute-start.22 = (bf16[128,1536]{1,0:T(8,128)(2,1)S(1)}, bf16[128,1536]{1,0:T(8,128)(2,1)S(1)}, u32[]{:S(2)}, u32[]{:S(2)}) collective-permute-start(bf16[128,1536]{1,0:T(8,128)(2,1)S(1)} %copy-done.16), channel_id=1, source_target_pairs={{0,1},{1,2},{2,3},{3,0},{4,5},{5,6},{6,7},{7,4},{8,9},{9,10},{10,1... | collective-permute-start | bytes 1179656 | tf_op jit(solution)/shard_map/ppermute | solution.py:498
  133.0 15.4 %collective-permute-start.32 = (bf16[1536,128]{1,0:T(8,128)(2,1)S(1)}, bf16[1536,128]{1,0:T(8,128)(2,1)}, u32[]{:S(2)}, u32[]{:S(2)}) collective-permute-start(bf16[1536,128]{1,0:T(8,128)(2,1)S(1)} %get-tuple-element.56), channel_id=1, source_target_pairs={{0,96},{32,0},{64,32},{96,64},{1,97},{33,1},{65,33},{97,65},{2,98}... | collective-permute-start | bytes 1179656 | tf_op jit(solution)/shard_map/ppermute | solution.py:498
  133.1 15.3 %collective-permute-start.31 = (bf16[1536,128]{1,0:T(8,128)(2,1)S(1)}, bf16[1536,128]{1,0:T(8,128)(2,1)}, u32[]{:S(2)}, u32[]{:S(2)}) collective-permute-start(bf16[1536,128]{1,0:T(8,128)(2,1)S(1)} %get-tuple-element.57), channel_id=1, source_target_pairs={{0,64},{32,96},{64,0},{96,32},{1,65},{33,97},{65,1},{97,33},{2,66}... | collective-permute-start | bytes 1179656 | tf_op jit(solution)/shard_map/ppermute | solution.py:498
  135.7 18.5 %collective-permute-start.30 = (bf16[1536,128]{1,0:T(8,128)(2,1)S(1)}, bf16[1536,128]{1,0:T(8,128)(2,1)}, u32[]{:S(2)}, u32[]{:S(2)}) collective-permute-start(bf16[1536,128]{1,0:T(8,128)(2,1)S(1)} %get-tuple-element.55), channel_id=1, source_target_pairs={{0,32},{32,64},{64,96},{96,0},{1,33},{33,65},{65,97},{97,1},{2,34}... | collective-permute-start | bytes 1179656 | tf_op jit(solution)/shard_map/ppermute | solution.py:498
  138.6 24.2 %collective-permute-start.29 = (bf16[16,1536]{1,0:T(8,128)(2,1)}, bf16[16,1536]{1,0:T(8,128)(2,1)}, u32[]{:S(2)}, u32[]{:S(2)}) collective-permute-start(bf16[16,1536]{1,0:T(8,128)(2,1)} %get-tuple-element.66), channel_id=1, source_target_pairs={{1,0},{2,1},{3,2},{5,4},{6,5},{7,6},{9,8},{10,9},{11,10},{13,12},{... | collective-permute-start | bytes 147464 | tf_op jit(solution)/shard_map/ppermute | solution.py:613
  159.0 21.1 %collective-permute-start.28 = (bf16[128,1536]{1,0:T(8,128)(2,1)}, bf16[128,1536]{1,0:T(8,128)(2,1)}, u32[]{:S(2)}, u32[]{:S(2)}) collective-permute-start(bf16[128,1536]{1,0:T(8,128)(2,1)} %get-tuple-element.59), channel_id=1, source_target_pairs={{0,3},{1,0},{2,1},{3,2},{4,7},{5,4},{6,5},{7,6},{8,11},{9,8},{10,9... | collective-permute-start | bytes 1179656 | tf_op jit(solution)/shard_map/ppermute | solution.py:498
  159.2 20.9 %collective-permute-start.27 = (bf16[128,1536]{1,0:T(8,128)(2,1)S(1)}, bf16[128,1536]{1,0:T(8,128)(2,1)}, u32[]{:S(2)}, u32[]{:S(2)}) collective-permute-start(bf16[128,1536]{1,0:T(8,128)(2,1)S(1)} %get-tuple-element.60), channel_id=1, source_target_pairs={{0,2},{1,3},{2,0},{3,1},{4,6},{5,7},{6,4},{7,5},{8,10},{9,11},{10,... | collective-permute-start | bytes 1179656 | tf_op jit(solution)/shard_map/ppermute | solution.py:498
  162.8 17.3 %collective-permute-start.26 = (bf16[128,1536]{1,0:T(8,128)(2,1)S(1)}, bf16[128,1536]{1,0:T(8,128)(2,1)}, u32[]{:S(2)}, u32[]{:S(2)}) collective-permute-start(bf16[128,1536]{1,0:T(8,128)(2,1)S(1)} %get-tuple-element.58), channel_id=1, source_target_pairs={{0,1},{1,2},{2,3},{3,0},{4,5},{5,6},{6,7},{7,4},{8,9},{9,10},{10,1... | collective-permute-start | bytes 1179656 | tf_op jit(solution)/shard_map/ppermute | solution.py:498
  162.8 15.2 %collective-permute-start.34 = (bf16[384,128]{1,0:T(8,128)(2,1)S(1)}, bf16[384,128]{1,0:T(8,128)(2,1)}, u32[]{:S(2)}, u32[]{:S(2)}) collective-permute-start(bf16[384,128]{1,0:T(8,128)(2,1)S(1)} %get-tuple-element.64), channel_id=1, source_target_pairs={{0,16},{8,24},{16,0},{24,8},{1,17},{9,25},{17,1},{25,9},{2,18},{10... | collective-permute-start | bytes 294920 | tf_op jit(solution)/shard_map/ppermute | solution.py:498
  162.8 15.2 %collective-permute-start.33 = (bf16[384,128]{1,0:T(8,128)(2,1)S(1)}, bf16[384,128]{1,0:T(8,128)(2,1)S(1)}, u32[]{:S(2)}, u32[]{:S(2)}) collective-permute-start(bf16[384,128]{1,0:T(8,128)(2,1)S(1)} %get-tuple-element.63), channel_id=1, source_target_pairs={{0,8},{8,16},{16,24},{24,0},{1,9},{9,17},{17,25},{25,1},{2,10},{10... | collective-permute-start | bytes 294920 | tf_op jit(solution)/shard_map/ppermute | solution.py:498
  179.3 18.9 %collective-permute-start.39 = (bf16[12,640]{1,0:T(8,128)(2,1)S(1)}, bf16[12,640]{1,0:T(8,128)(2,1)S(1)}, u32[]{:S(2)}, u32[]{:S(2)}) collective-permute-start(bf16[12,640]{1,0:T(8,128)(2,1)S(1)} %bitcast.158), channel_id=1, source_target_pairs={{0,3},{1,0},{2,1},{3,2},{4,67},{5,64},{6,65},{7,66},{8,7},{9,4},{1... | collective-permute-start | bytes 46088 | tf_op jit(solution)/shard_map/ppermute | solution.py:490
  182.3 15.8 %collective-permute-start.36 = (bf16[12,640]{1,0:T(8,128)(2,1)S(1)}, bf16[12,640]{1,0:T(8,128)(2,1)S(1)}, u32[]{:S(2)}, u32[]{:S(2)}) collective-permute-start(bf16[12,640]{1,0:T(8,128)(2,1)S(1)} %bitcast.161), channel_id=1, source_target_pairs={{0,0},{1,1},{2,2},{3,3},{4,64},{5,65},{6,66},{7,67},{8,4},{9,5},{1... | collective-permute-start | bytes 46088 | tf_op jit(solution)/shard_map/ppermute | solution.py:490
  (39 other events, 321.1 us)

commit v2 on v1

--- a/solution.py
+++ b/solution.py
@@ -534,13 +534,6 @@
     return total
 
 
-def returned_along(pieces, axis):
-    total = pieces[0].astype(F32)
-    for k in range(1, 4):
-        total = total + turned(pieces[k], axis, k).astype(F32)
-    return total.astype(BF16)
-
-
 def gather_in_x(w_query, w_kv):
     seq = lax.axis_index("x")
     cols = w_query.shape[1] // 4
@@ -623,7 +616,7 @@
     edge_next = behind(edge(bases[0, :span], skip[:8]))
     w_rows = gather_in_x(w_query, w_kv)
     out_home = moved(w_out, lambda z, y, c, x: (y, x, c, z))
-    beside = lax.ppermute(after(cot, w_rows), "x", [(i, i ^ 1) for i in range(4)])
+    beside = lax.ppermute(cot, "x", [(i, i ^ 1) for i in range(4)])
     across = lax.ppermute(jnp.stack([cot, beside]), "x", [(i, 3 - i) for i in range(4)])
     pieces = around(w_rows, "y")
     out_rows = gathered(out_home, "y").reshape(48, width)
@@ -638,35 +631,40 @@
         ],
         axis=0,
     )
-    near = jnp.stack(around(joint, "z"))
-
+    edge_next = after(edge_next, beside, out_home)
     gain = conv_gain[None, :]
     pooled, normed = front(
         ends, cells, skip, edge_prev, edge_next, base_table, gain, attn_gain[None, :], conv_weight
     )
     norms = around(normed)
-    far = flipped(after(near, normed, across))
+    joint = after(joint, normed, across)
+    near = jnp.stack(around(joint, "z"))
+    far = flipped(after(near, *norms))
 
     spot = [seq, lax.axis_index("c"), lax.axis_index("z"), lax.axis_index("y")]
     spot = jnp.stack(spot).astype(jnp.int32)
     d_in, heads, normed_all, cot_all, full_out, *d_parts = attend(spot, norms, (cot, beside, across), near, far)
     d_parts[1:] = [turned(d_parts[k], "x", k) for k in range(1, 4)]
     own, other = grads(spot, normed_all, d_in, heads, cot_all)
+    out_parts = mix(spot, heads, full_out)
     mine = (own.astype(F32) + flipped(other).astype(F32)).astype(BF16)
-    out_parts = mix(spot, after(heads, mine), full_out)
+    total = mine[0].astype(F32)
+    for k in range(1, 4):
+        total = total + turned(mine[k], "z", k).astype(F32)
+    mine = total.astype(BF16)
     d_normed = d_parts[0]
     for k in range(1, 4):
         d_normed = d_normed + after(d_parts[k], mine).astype(F32)
-    mine = returned_along(mine, "z")
+    mine = summed(split_rows(mine), "y")
 
     d_pooled = cot.astype(F32) + rms_back(pooled, attn_gain, d_normed)
     grad = (d_pooled * 0.5).astype(BF16)
     grad_prev, grad_next = ahead(grad[half - 16 :]), behind(grad[:16])
+    grad_next = after(grad_next, mine)
     coarse = (pooled + returned(after(out_parts, grad_prev))).astype(BF16)
     skip_grad = back(cells, skip, base_table, gain, grad, grad_prev, grad_next, conv_weight)
 
     factor = 1.0 / 32
-    mine = summed(split_rows(mine), "y")
     cols = w_query.shape[1] // 4
     grad_query, grad_kv, grad_out = finish(mine, cols, width)
     return (

time: 209 us -> 209 us (level)
  waiting for transfers between devices: 48.7 us -> 38.3 us
  starting transfers between devices: 78.1 us -> 88.2 us
    ppermute x27, waiting for transfers between devices: 41.2 us -> 27.1 us  [turned(): return lax.ppermute(value, axis, [(i, (i + by) % 4) for i in range(4)])]
    ppermute x8, starting transfers between devices: 32.5 us -> 38.2 us  [moved(): return lax.ppermute(value, AXES, pairs)]
    ppermute x27, starting transfers between devices: 32.8 us -> 36.8 us  [turned(): return lax.ppermute(value, axis, [(i, (i + by) % 4) for i in range(4)])]
    ppermute x8, waiting for transfers between devices: 7.45 us -> 11.2 us  [moved(): return lax.ppermute(value, AXES, pairs)]
    unnamed x60 -> x48, local copies, waits for them, and re-layouts: 4.6 us -> 4.2 us
  transfers between devices with their start and end apart: 41 -> 41, of which waited for: 11 -> 16; matrix products, arithmetic and copies ran while one was open for 10% -> 8% of each run, Pallas kernels for 14% -> 14%
where the time goes in v2:
time: 209 us; the launch traced here: 207 us
  starting transfers between devices  88.2 us (42%)
  Pallas kernels  51.6 us (25%)
  waiting for transfers between devices  38.3 us (18%)
  local copies, waits for them, and re-layouts  14 us (7%)
  other arithmetic  14 us (7%)
    ppermute x8, starting transfers between devices, moved(): return lax.ppermute(value, AXES, pairs)  38.2 us
    ppermute x27, starting transfers between devices, turned(): return lax.ppermute(value, axis, [(i, (i + by) % 4) for i in range(4)])  36.8 us
    ppermute x27, waiting for transfers between devices, turned(): return lax.ppermute(value, axis, [(i, (i + by) % 4) for i in range(4)])  27.1 us
    pallas_call x1, Pallas kernels, attend(): pl.pallas_call(attend_kernel, grid_spec=pltpu.PrefetchScalarGridSpec(num_...  14.9 us
    pallas_call x1, Pallas kernels, back(): pl.pallas_call(back_kernel, grid=(1,), in_specs=[whole(a) for a in small]...  12.9 us
    pallas_call x1, Pallas kernels, front(): pl.pallas_call(front_kernel, grid_spec=pltpu.PrefetchScalarGridSpec(num_s...  11.6 us
    ppermute x8, waiting for transfers between devices, moved(): return lax.ppermute(value, AXES, pairs)  11.2 us
    ppermute x2, starting transfers between devices, behind(): return lax.ppermute(value, 'x', [(i + 1, i) for i in range(3)])  8.58 us
  transfers between devices with their start and end apart: 41, of which 16 were waited for; matrix products, arithmetic and copies ran while one was open for 8% of the time, Pallas kernels for 14%

profile of v2, /device:TPU:15, one launch (start us, length us, event | category | flops | bytes accessed | tf_op | source)
XLA Modules:
  0.0 207.4 jit_solution(7080175482646092073)
XLA Ops:
  6.1 4.0 %collective-permute-start.1 = (bf16[8,1664]{1,0:T(8,128)(2,1)S(1)}, bf16[8,1664]{1,0:T(8,128)(2,1)S(1)}, u32[]{:S(2)}, u32[]{:S(2)}) collective-permute-start(bf16[8,1664]{1,0:T(8,128)(2,1)S(1)} %concatenate.34), channel_id=1, source_target_pairs={{1,0},{2,1},{3,2},{5,4},{6,5},{7,6},{9,8},{10,9},{11,10},{13,12},{... | collective-permute-start | bytes 79880 | tf_op jit(solution)/shard_map/ppermute | solution.py:606
  10.7 5.8 %collective-permute-start.3 = (bf16[12,1536]{1,0:T(8,128)(2,1)}, bf16[12,1536]{1,0:T(8,128)(2,1)S(1)}, u32[]{:S(2)}, u32[]{:S(2)}) collective-permute-start(bf16[12,1536]{1,0:T(8,128)(2,1)} %param.18), channel_id=1, source_target_pairs={{0,0},{1,8},{2,16},{3,24},{4,4},{5,12},{6,20},{7,28},{8,32},{9,40}... | collective-permute-start | bytes 110600 | tf_op jit(solution)/shard_map/ppermute | solution.py:490
  26.6 2.5 %collective-permute-done.9 = bf16[12,576]{1,0:T(8,128)(2,1)S(1)} collective-permute-done((bf16[12,576]{1,0:T(8,128)(2,1)S(1)}, bf16[12,576]{1,0:T(8,128)(2,1)S(1)}, u32[]{:S(2)}, u32[]{:S(2)}) %collective-permute-start.9) | collective-permute-done | bytes 13856 | tf_op jit(solution)/shard_map/ppermute | solution.py:498
  30.5 2.4 %collective-permute-done.10 = bf16[12,576]{1,0:T(8,128)(2,1)S(1)} collective-permute-done((bf16[12,576]{1,0:T(8,128)(2,1)S(1)}, bf16[12,576]{1,0:T(8,128)(2,1)S(1)}, u32[]{:S(2)}, u32[]{:S(2)}) %collective-permute-start.10) | collective-permute-done | bytes 13856 | tf_op jit(solution)/shard_map/ppermute | solution.py:498
  33.1 3.4 %collective-permute-start.12 = (bf16[48,576]{1,0:T(8,128)(2,1)S(1)}, bf16[48,576]{1,0:T(8,128)(2,1)S(1)}, u32[]{:S(2)}, u32[]{:S(2)}) collective-permute-start(bf16[48,576]{1,0:T(8,128)(2,1)S(1)} %reshape.106), channel_id=1, source_target_pairs={{0,16},{8,24},{16,0},{24,8},{1,17},{9,25},{17,1},{25,9},{2,18},{10... | collective-permute-start | bytes 165896 | tf_op jit(solution)/shard_map/ppermute | solution.py:498
  48.5 11.6 %front.1 = (f32[128,1536]{1,0:T(8,128)}, bf16[128,1536]{1,0:T(8,128)(2,1)}) custom-call(s32[2]{0:T(128)} %pad_add_fusion.ends, s32[256,64]{1,0:T(8,128)} %reshape.105.cells, bf16[256,1536]{1,0:T(8,128)(2,1)} %bitcast.137, bf16[8,1664]{1,0:T(8,128)(2,1)} %copy-done.10, bf16[8,1664]{1,0:T(8,128)(2,1)} %copy-done.11, f32[4,1536]{1,0:T(4,128)} %table.3, ...), custom_call_target="tpu_custom_call" | custom-call | flops 3019898880 | bytes 26738688 | tf_op jit(solution)/shard_map/front/pallas_call | solution.py:129
  64.5 3.8 %collective-permute-start.5 = (bf16[128,1536]{1,0:T(8,128)(2,1)}, bf16[128,1536]{1,0:T(8,128)(2,1)S(1)}, u32[]{:S(2)}, u32[]{:S(2)}) collective-permute-start(bf16[128,1536]{1,0:T(8,128)(2,1)} %get-tuple-element.28.norm0), channel_id=1, source_target_pairs={{0,2},{1,3},{2,0},{3,1},{4,6},{5,7},{6,4},{7,5},{8,10},{9,11},{10,... | collective-permute-start | bytes 1179656 | tf_op jit(solution)/shard_map/ppermute | solution.py:498
  68.4 4.0 %collective-permute-done.19 = bf16[384,512]{1,0:T(8,128)(2,1)S(1)} collective-permute-done((bf16[384,512]{1,0:T(8,128)(2,1)S(1)}, bf16[384,512]{1,0:T(8,128)(2,1)S(1)}, u32[]{:S(2)}, u32[]{:S(2)}) %collective-permute-start.19) | collective-permute-done | bytes 393248 | tf_op jit(solution)/shard_map/ppermute | solution.py:498
  73.5 4.5 %collective-permute-done.5.norm2 = bf16[128,1536]{1,0:T(8,128)(2,1)S(1)} collective-permute-done((bf16[128,1536]{1,0:T(8,128)(2,1)}, bf16[128,1536]{1,0:T(8,128)(2,1)S(1)}, u32[]{:S(2)}, u32[]{:S(2)}) %collective-permute-start.5) | collective-permute-done | bytes 393248 | tf_op jit(solution)/shard_map/ppermute | solution.py:498
  79.4 11.6 %collective-permute-start.20 = (bf16[4,384,512]{2,1,0:T(8,128)(2,1)S(1)}, bf16[4,384,512]{2,1,0:T(8,128)(2,1)S(1)}, u32[]{:S(2)}, u32[]{:S(2)}) collective-permute-start(bf16[4,384,512]{2,1,0:T(8,128)(2,1)S(1)} %pad_maximum_fusion.near), channel_id=1, source_target_pairs={{0,4},{1,5},{2,6},{3,7},{4,0},{5,1},{6,2},{7,3},{8,12},{9,13},{10,... | collective-permute-start | bytes 4718600 | tf_op jit(solution)/shard_map/ppermute | solution.py:490
  95.3 14.9 %attend.1 = (bf16[512,640]{1,0:T(8,128)(2,1)}, bf16[2,512,192]{2,1,0:T(8,128)(2,1)}, bf16[512,1536]{1,0:T(8,128)(2,1)}, bf16[512,1536]{1,0:T(8,128)(2,1)}, bf16[...) custom-call(s32[4]{0:T(128)} %pad_add_fusion.1.place, ...), custom_call_target="tpu_custom_call" | custom-call | flops 3623878656 | bytes 9437184 | tf_op jit(solution)/shard_map/attend/pallas_call | solution.py:366
  110.2 7.0 %grads.1 = (bf16[4,1536,128]{2,1,0:T(8,128)(2,1)}, bf16[4,1536,128]{2,1,0:T(8,128)(2,1)}) custom-call(s32[4]{0:T(128)} %pad_add_fusion.1.place, bf16[512,1536]{1,0:T(8,128)(2,1)} %get-tuple-element.35.normed, bf16[512,640]{1,0:T(8,128)(2,1)} %get-tuple-element.36.d_in, bf16[2,512,192]{2,1,0:T(8,128)(2,1)} %get-tuple-element.31.heads, ...), custom_call_target="tpu_custom_call" | custom-call | flops 1610612736 | bytes 12582912 | tf_op jit(solution)/shard_map/grads/pallas_call | solution.py:424
  117.6 3.2 %collective-permute-done.22 = bf16[4,1536,128]{2,1,0:T(8,128)(2,1)S(1)} collective-permute-done((bf16[4,1536,128]{2,1,0:T(8,128)(2,1)}, bf16[4,1536,128]{2,1,0:T(8,128)(2,1)S(1)}, u32[]{:S(2)}, u32[]{:S(2)}) %collective-permute-start.22) | collective-permute-done | bytes 1572896 | tf_op jit(solution)/shard_map/ppermute | solution.py:490
  123.6 2.7 %collective-permute-start.24 = (bf16[1536,128]{1,0:T(8,128)(2,1)}, bf16[1536,128]{1,0:T(8,128)(2,1)}, u32[]{:S(2)}, u32[]{:S(2)}) collective-permute-start(bf16[1536,128]{1,0:T(8,128)(2,1)} %get-tuple-element.62), channel_id=1, source_target_pairs={{0,64},{32,96},{64,0},{96,32},{1,65},{33,97},{65,1},{97,33},{2,66}... | collective-permute-start | bytes 1179656 | tf_op jit(solution)/shard_map/ppermute | solution.py:498
  127.2 2.6 %collective-permute-start.26 = (bf16[128,1536]{1,0:T(8,128)(2,1)}, bf16[128,1536]{1,0:T(8,128)(2,1)S(1)}, u32[]{:S(2)}, u32[]{:S(2)}) collective-permute-start(bf16[128,1536]{1,0:T(8,128)(2,1)} %get-tuple-element.41), channel_id=1, source_target_pairs={{0,2},{1,3},{2,0},{3,1},{4,6},{5,7},{6,4},{7,5},{8,10},{9,11},{10,... | collective-permute-start | bytes 1179656 | tf_op jit(solution)/shard_map/ppermute | solution.py:498
  129.9 5.2 %mix.1 = bf16[4,128,1536]{2,1,0:T(8,128)(2,1)} custom-call(s32[4]{0:T(128)} %pad_add_fusion.1.place, bf16[2,512,192]{2,1,0:T(8,128)(2,1)} %get-tuple-element.31.heads, bf16[384,1536]{1,0:T(8,128)(2,1)} %get-tuple-element.32.w_out), custom_call_target="tpu_custom_call" | custom-call | flops 603979776 | bytes 2359296 | tf_op jit(solution)/shard_map/mix/pallas_call | solution.py:455
  136.4 8.6 %collective-permute-done.23 = bf16[1536,128]{1,0:T(8,128)(2,1)} collective-permute-done((bf16[1536,128]{1,0:T(8,128)(2,1)S(1)}, bf16[1536,128]{1,0:T(8,128)(2,1)}, u32[]{:S(2)}, u32[]{:S(2)}) %collective-permute-start.23) | collective-permute-done | bytes 393248 | tf_op jit(solution)/shard_map/ppermute | solution.py:498
  149.9 4.6 %collective-permute-start.32 = (bf16[16,1536]{1,0:T(8,128)(2,1)}, bf16[16,1536]{1,0:T(8,128)(2,1)}, u32[]{:S(2)}, u32[]{:S(2)}) collective-permute-start(bf16[16,1536]{1,0:T(8,128)(2,1)} %get-tuple-element.68), channel_id=1, source_target_pairs={{1,0},{2,1},{3,2},{5,4},{6,5},{7,6},{9,8},{10,9},{11,10},{13,12},{... | collective-permute-start | bytes 147464 | tf_op jit(solution)/shard_map/ppermute | solution.py:606
  165.6 12.9 %back.1 = bf16[256,1536]{1,0:T(8,128)(2,1)} custom-call(s32[256,64]{1,0:T(8,128)} %reshape.105.cells, bf16[256,1536]{1,0:T(8,128)(2,1)} %bitcast.138, f32[4,1536]{1,0:T(4,128)} %table.3, f32[1,1536]{1,0:T(1,128)} %broadcast_in_dim.103.gain, bf16[128,1536]{1,0:T(8,128)(2,1)} %copy-done.3, bf16[16,1536]{1,0:T(8,128)(2,1)} %collective-permute-done.28.grad_prev, ...), custom_call_target="tpu_custom_call" | custom-call | flops 3019898880 | bytes 26738688 | tf_op jit(solution)/shard_map/back/pallas_call | solution.py:249
  178.6 7.3 %collective-permute-start.36 = (bf16[12,640]{1,0:T(8,128)(2,1)S(1)}, bf16[12,640]{1,0:T(8,128)(2,1)S(1)}, u32[]{:S(2)}, u32[]{:S(2)}) collective-permute-start(bf16[12,640]{1,0:T(8,128)(2,1)S(1)} %bitcast.161), channel_id=1, source_target_pairs={{0,0},{1,1},{2,2},{3,3},{4,64},{5,65},{6,66},{7,67},{8,4},{9,5},{1... | collective-permute-start | bytes 46088 | tf_op jit(solution)/shard_map/ppermute | solution.py:490
  186.1 4.5 %collective-permute-start.37 = (bf16[12,640]{1,0:T(8,128)(2,1)S(1)}, bf16[12,640]{1,0:T(8,128)(2,1)S(1)}, u32[]{:S(2)}, u32[]{:S(2)}) collective-permute-start(bf16[12,640]{1,0:T(8,128)(2,1)S(1)} %bitcast.159), channel_id=1, source_target_pairs={{0,1},{1,2},{2,3},{3,0},{4,65},{5,66},{6,67},{7,64},{8,5},{9,6},{1... | collective-permute-start | bytes 46088 | tf_op jit(solution)/shard_map/ppermute | solution.py:490
  190.5 2.8 %collective-permute-start.38 = (bf16[12,640]{1,0:T(8,128)(2,1)S(1)}, bf16[12,640]{1,0:T(8,128)(2,1)S(1)}, u32[]{:S(2)}, u32[]{:S(2)}) collective-permute-start(bf16[12,640]{1,0:T(8,128)(2,1)S(1)} %bitcast.158), channel_id=1, source_target_pairs={{0,2},{1,3},{2,0},{3,1},{4,66},{5,67},{6,64},{7,65},{8,6},{9,7},{1... | collective-permute-start | bytes 46088 | tf_op jit(solution)/shard_map/ppermute | solution.py:490
  193.4 4.1 %collective-permute-start.40 = (bf16[12,1536]{1,0:T(8,128)(2,1)S(1)}, bf16[12,1536]{1,0:T(8,128)(2,1)S(1)}, u32[]{:S(2)}, u32[]{:S(2)}) collective-permute-start(bf16[12,1536]{1,0:T(8,128)(2,1)S(1)} %bitcast.157), channel_id=1, source_target_pairs={{0,0},{1,32},{2,64},{3,96},{4,16},{5,48},{6,80},{7,112},{8,1},{9,3... | collective-permute-start | bytes 110600 | tf_op jit(solution)/shard_map/ppermute | solution.py:490
  199.3 5.3 %collective-permute-done.40 = bf16[12,1536]{1,0:T(8,128)(2,1)S(1)} collective-permute-done((bf16[12,1536]{1,0:T(8,128)(2,1)S(1)}, bf16[12,1536]{1,0:T(8,128)(2,1)S(1)}, u32[]{:S(2)}, u32[]{:S(2)}) %collective-permute-start.40) | collective-permute-done | bytes 36896 | tf_op jit(solution)/shard_map/ppermute | solution.py:490
  (209 shorter events, 66.7 us)
Async XLA Ops:
  3.5 44.4 %collective-permute-start = (bf16[8,1664]{1,0:T(8,128)(2,1)S(1)}, bf16[8,1664]{1,0:T(8,128)(2,1)S(1)}, u32[]{:S(2)}, u32[]{:S(2)}) collective-permute-start(bf16[8,1664]{1,0:T(8,128)(2,1)S(1)} %concatenate.33), channel_id=1, source_target_pairs={{0,1},{1,2},{2,3},{4,5},{5,6},{6,7},{8,9},{9,10},{10,11},{12,13},{... | collective-permute-start | bytes 79880 | tf_op jit(solution)/shard_map/ppermute | solution.py:603
  6.1 41.8 %collective-permute-start.1 = (bf16[8,1664]{1,0:T(8,128)(2,1)S(1)}, bf16[8,1664]{1,0:T(8,128)(2,1)S(1)}, u32[]{:S(2)}, u32[]{:S(2)}) collective-permute-start(bf16[8,1664]{1,0:T(8,128)(2,1)S(1)} %concatenate.34), channel_id=1, source_target_pairs={{1,0},{2,1},{3,2},{5,4},{6,5},{7,6},{9,8},{10,9},{11,10},{13,12},{... | collective-permute-start | bytes 79880 | tf_op jit(solution)/shard_map/ppermute | solution.py:606
  10.0 36.3 %collective-permute-start.2 = (bf16[128,1536]{1,0:T(8,128)(2,1)}, bf16[128,1536]{1,0:T(8,128)(2,1)S(1)}, u32[]{:S(2)}, u32[]{:S(2)}) collective-permute-start(bf16[128,1536]{1,0:T(8,128)(2,1)} %bitcast.141), channel_id=1, source_target_pairs={{0,1},{1,0},{2,3},{3,2},{4,5},{5,4},{6,7},{7,6},{8,9},{9,8},{10,11... | collective-permute-start | bytes 1179656 | tf_op jit(solution)/shard_map/ppermute | solution.py:619
  10.7 22.4 %collective-permute-start.3 = (bf16[12,1536]{1,0:T(8,128)(2,1)}, bf16[12,1536]{1,0:T(8,128)(2,1)S(1)}, u32[]{:S(2)}, u32[]{:S(2)}) collective-permute-start(bf16[12,1536]{1,0:T(8,128)(2,1)} %param.18), channel_id=1, source_target_pairs={{0,0},{1,8},{2,16},{3,24},{4,4},{5,12},{6,20},{7,28},{8,32},{9,40}... | collective-permute-start | bytes 110600 | tf_op jit(solution)/shard_map/ppermute | solution.py:490
  46.4 13.7 %collective-permute-start.7 = (bf16[2,128,1536]{2,1,0:T(8,128)(2,1)S(1)}, bf16[2,128,1536]{2,1,0:T(8,128)(2,1)S(1)}, u32[]{:S(2)}, u32[]{:S(2)}) collective-permute-start(bf16[2,128,1536]{2,1,0:T(8,128)(2,1)S(1)} %pad_maximum_fusion.1), channel_id=1, source_target_pairs={{0,3},{1,2},{2,1},{3,0},{4,7},{5,6},{6,5},{7,4},{8,11},{9,10},{10,... | collective-permute-start | bytes 2359304 | tf_op jit(solution)/shard_map/ppermute | solution.py:620
  60.2 12.1 %collective-permute-start.19 = (bf16[384,512]{1,0:T(8,128)(2,1)S(1)}, bf16[384,512]{1,0:T(8,128)(2,1)S(1)}, u32[]{:S(2)}, u32[]{:S(2)}) collective-permute-start(bf16[384,512]{1,0:T(8,128)(2,1)S(1)} %fusion.27), channel_id=1, source_target_pairs={{0,32},{32,64},{64,96},{96,0},{1,33},{33,65},{65,97},{97,1},{2,34}... | collective-permute-start | bytes 1179656 | tf_op jit(solution)/shard_map/ppermute | solution.py:498
  60.3 12.0 %collective-permute-start.18 = (bf16[384,512]{1,0:T(8,128)(2,1)S(1)}, bf16[384,512]{1,0:T(8,128)(2,1)S(1)}, u32[]{:S(2)}, u32[]{:S(2)}) collective-permute-start(bf16[384,512]{1,0:T(8,128)(2,1)S(1)} %fusion.27), channel_id=1, source_target_pairs={{0,64},{32,96},{64,0},{96,32},{1,65},{33,97},{65,1},{97,33},{2,66}... | collective-permute-start | bytes 1179656 | tf_op jit(solution)/shard_map/ppermute | solution.py:498
  62.7 10.6 %collective-permute-start.17 = (bf16[384,512]{1,0:T(8,128)(2,1)S(1)}, bf16[384,512]{1,0:T(8,128)(2,1)S(1)}, u32[]{:S(2)}, u32[]{:S(2)}) collective-permute-start(bf16[384,512]{1,0:T(8,128)(2,1)S(1)} %fusion.27), channel_id=1, source_target_pairs={{0,96},{32,0},{64,32},{96,64},{1,97},{33,1},{65,33},{97,65},{2,98}... | collective-permute-start | bytes 1179656 | tf_op jit(solution)/shard_map/ppermute | solution.py:498
  64.5 13.4 %collective-permute-start.5 = (bf16[128,1536]{1,0:T(8,128)(2,1)}, bf16[128,1536]{1,0:T(8,128)(2,1)S(1)}, u32[]{:S(2)}, u32[]{:S(2)}) collective-permute-start(bf16[128,1536]{1,0:T(8,128)(2,1)} %get-tuple-element.28.norm0), channel_id=1, source_target_pairs={{0,2},{1,3},{2,0},{3,1},{4,6},{5,7},{6,4},{7,5},{8,10},{9,11},{10,... | collective-permute-start | bytes 1179656 | tf_op jit(solution)/shard_map/ppermute | solution.py:498
  79.4 14.6 %collective-permute-start.20 = (bf16[4,384,512]{2,1,0:T(8,128)(2,1)S(1)}, bf16[4,384,512]{2,1,0:T(8,128)(2,1)S(1)}, u32[]{:S(2)}, u32[]{:S(2)}) collective-permute-start(bf16[4,384,512]{2,1,0:T(8,128)(2,1)S(1)} %pad_maximum_fusion.near), channel_id=1, source_target_pairs={{0,4},{1,5},{2,6},{3,7},{4,0},{5,1},{6,2},{7,3},{8,12},{9,13},{10,... | collective-permute-start | bytes 4718600 | tf_op jit(solution)/shard_map/ppermute | solution.py:490
  123.6 11.4 %collective-permute-start.25 = (bf16[1536,128]{1,0:T(8,128)(2,1)}, bf16[1536,128]{1,0:T(8,128)(2,1)}, u32[]{:S(2)}, u32[]{:S(2)}) collective-permute-start(bf16[1536,128]{1,0:T(8,128)(2,1)} %get-tuple-element.61), channel_id=1, source_target_pairs={{0,96},{32,0},{64,32},{96,64},{1,97},{33,1},{65,33},{97,65},{2,98}... | collective-permute-start | bytes 1179656 | tf_op jit(solution)/shard_map/ppermute | solution.py:498
  123.6 12.7 %collective-permute-start.24 = (bf16[1536,128]{1,0:T(8,128)(2,1)}, bf16[1536,128]{1,0:T(8,128)(2,1)}, u32[]{:S(2)}, u32[]{:S(2)}) collective-permute-start(bf16[1536,128]{1,0:T(8,128)(2,1)} %get-tuple-element.62), channel_id=1, source_target_pairs={{0,64},{32,96},{64,0},{96,32},{1,65},{33,97},{65,1},{97,33},{2,66}... | collective-permute-start | bytes 1179656 | tf_op jit(solution)/shard_map/ppermute | solution.py:498
  126.4 18.5 %collective-permute-start.23 = (bf16[1536,128]{1,0:T(8,128)(2,1)S(1)}, bf16[1536,128]{1,0:T(8,128)(2,1)}, u32[]{:S(2)}, u32[]{:S(2)}) collective-permute-start(bf16[1536,128]{1,0:T(8,128)(2,1)S(1)} %get-tuple-element.60), channel_id=1, source_target_pairs={{0,32},{32,64},{64,96},{96,0},{1,33},{33,65},{65,97},{97,1},{2,34}... | collective-permute-start | bytes 1179656 | tf_op jit(solution)/shard_map/ppermute | solution.py:498
  127.2 19.1 %collective-permute-start.27 = (bf16[128,1536]{1,0:T(8,128)(2,1)}, bf16[128,1536]{1,0:T(8,128)(2,1)S(1)}, u32[]{:S(2)}, u32[]{:S(2)}) collective-permute-start(bf16[128,1536]{1,0:T(8,128)(2,1)} %get-tuple-element.43), channel_id=1, source_target_pairs={{0,3},{1,0},{2,1},{3,2},{4,7},{5,4},{6,5},{7,6},{8,11},{9,8},{10,9... | collective-permute-start | bytes 1179656 | tf_op jit(solution)/shard_map/ppermute | solution.py:498
  127.2 19.2 %collective-permute-start.26 = (bf16[128,1536]{1,0:T(8,128)(2,1)}, bf16[128,1536]{1,0:T(8,128)(2,1)S(1)}, u32[]{:S(2)}, u32[]{:S(2)}) collective-permute-start(bf16[128,1536]{1,0:T(8,128)(2,1)} %get-tuple-element.41), channel_id=1, source_target_pairs={{0,2},{1,3},{2,0},{3,1},{4,6},{5,7},{6,4},{7,5},{8,10},{9,11},{10,... | collective-permute-start | bytes 1179656 | tf_op jit(solution)/shard_map/ppermute | solution.py:498
  135.1 11.7 %collective-permute-start.21 = (bf16[128,1536]{1,0:T(8,128)(2,1)}, bf16[128,1536]{1,0:T(8,128)(2,1)S(1)}, u32[]{:S(2)}, u32[]{:S(2)}) collective-permute-start(bf16[128,1536]{1,0:T(8,128)(2,1)} %get-tuple-element.34), channel_id=1, source_target_pairs={{0,1},{1,2},{2,3},{3,0},{4,5},{5,6},{6,7},{7,4},{8,9},{9,10},{10,1... | collective-permute-start | bytes 1179656 | tf_op jit(solution)/shard_map/ppermute | solution.py:498
  148.6 10.0 %collective-permute-start.28 = (bf16[16,1536]{1,0:T(8,128)(2,1)S(1)}, bf16[16,1536]{1,0:T(8,128)(2,1)}, u32[]{:S(2)}, u32[]{:S(2)}) collective-permute-start(bf16[16,1536]{1,0:T(8,128)(2,1)S(1)} %get-tuple-element.69), channel_id=1, source_target_pairs={{0,1},{1,2},{2,3},{4,5},{5,6},{6,7},{8,9},{9,10},{10,11},{12,13},{... | collective-permute-start | bytes 147464 | tf_op jit(solution)/shard_map/ppermute | solution.py:603
  149.9 13.8 %collective-permute-start.32 = (bf16[16,1536]{1,0:T(8,128)(2,1)}, bf16[16,1536]{1,0:T(8,128)(2,1)}, u32[]{:S(2)}, u32[]{:S(2)}) collective-permute-start(bf16[16,1536]{1,0:T(8,128)(2,1)} %get-tuple-element.68), channel_id=1, source_target_pairs={{1,0},{2,1},{3,2},{5,4},{6,5},{7,6},{9,8},{10,9},{11,10},{13,12},{... | collective-permute-start | bytes 147464 | tf_op jit(solution)/shard_map/ppermute | solution.py:606
  159.6 45.6 %collective-permute-start.31 = (bf16[128,1536]{1,0:T(8,128)(2,1)}, bf16[128,1536]{1,0:T(8,128)(2,1)}, u32[]{:S(2)}, u32[]{:S(2)}) collective-permute-start(bf16[128,1536]{1,0:T(8,128)(2,1)} %get-tuple-element.58), channel_id=1, source_target_pairs={{0,3},{1,0},{2,1},{3,2},{4,7},{5,4},{6,5},{7,6},{8,11},{9,8},{10,9... | collective-permute-start | bytes 1179656 | tf_op jit(solution)/shard_map/ppermute | solution.py:498
  159.6 45.6 %collective-permute-start.30 = (bf16[128,1536]{1,0:T(8,128)(2,1)}, bf16[128,1536]{1,0:T(8,128)(2,1)}, u32[]{:S(2)}, u32[]{:S(2)}) collective-permute-start(bf16[128,1536]{1,0:T(8,128)(2,1)} %get-tuple-element.59), channel_id=1, source_target_pairs={{0,2},{1,3},{2,0},{3,1},{4,6},{5,7},{6,4},{7,5},{8,10},{9,11},{10,... | collective-permute-start | bytes 1179656 | tf_op jit(solution)/shard_map/ppermute | solution.py:498
  161.6 43.6 %collective-permute-start.29 = (bf16[128,1536]{1,0:T(8,128)(2,1)S(1)}, bf16[128,1536]{1,0:T(8,128)(2,1)}, u32[]{:S(2)}, u32[]{:S(2)}) collective-permute-start(bf16[128,1536]{1,0:T(8,128)(2,1)S(1)} %get-tuple-element.57), channel_id=1, source_target_pairs={{0,1},{1,2},{2,3},{3,0},{4,5},{5,6},{6,7},{7,4},{8,9},{9,10},{10,1... | collective-permute-start | bytes 1179656 | tf_op jit(solution)/shard_map/ppermute | solution.py:498
  164.0 22.1 %collective-permute-start.39 = (bf16[12,640]{1,0:T(8,128)(2,1)S(1)}, bf16[12,640]{1,0:T(8,128)(2,1)S(1)}, u32[]{:S(2)}, u32[]{:S(2)}) collective-permute-start(bf16[12,640]{1,0:T(8,128)(2,1)S(1)} %bitcast.160), channel_id=1, source_target_pairs={{0,3},{1,0},{2,1},{3,2},{4,67},{5,64},{6,65},{7,66},{8,7},{9,4},{1... | collective-permute-start | bytes 46088 | tf_op jit(solution)/shard_map/ppermute | solution.py:490
  178.6 12.0 %collective-permute-start.36 = (bf16[12,640]{1,0:T(8,128)(2,1)S(1)}, bf16[12,640]{1,0:T(8,128)(2,1)S(1)}, u32[]{:S(2)}, u32[]{:S(2)}) collective-permute-start(bf16[12,640]{1,0:T(8,128)(2,1)S(1)} %bitcast.161), channel_id=1, source_target_pairs={{0,0},{1,1},{2,2},{3,3},{4,64},{5,65},{6,66},{7,67},{8,4},{9,5},{1... | collective-permute-start | bytes 46088 | tf_op jit(solution)/shard_map/ppermute | solution.py:490
  193.4 11.1 %collective-permute-start.40 = (bf16[12,1536]{1,0:T(8,128)(2,1)S(1)}, bf16[12,1536]{1,0:T(8,128)(2,1)S(1)}, u32[]{:S(2)}, u32[]{:S(2)}) collective-permute-start(bf16[12,1536]{1,0:T(8,128)(2,1)S(1)} %bitcast.157), channel_id=1, source_target_pairs={{0,0},{1,32},{2,64},{3,96},{4,16},{5,48},{6,80},{7,112},{8,1},{9,3... | collective-permute-start | bytes 110600 | tf_op jit(solution)/shard_map/ppermute | solution.py:490
  (35 other events, 283.0 us)

commit v3 on v2

--- a/solution.py
+++ b/solution.py
@@ -49,9 +49,10 @@
 
 
 def front_kernel(
-    ends, cells, skip, edge_prev, edge_next, table, gain, attn_gain,
+    ends, cells, skip, edge_prev, edge_next, table,
     weight, pooled, normed, state_buf, active_buf, lhs, weight_buf, arrived,
 ):
+    gain, attn_gain = table.at[4:5], table.at[5:6]
     rows = skip.shape[0]
     half = rows // 2
     width = skip.shape[1]
@@ -121,11 +122,11 @@
     lax.fori_loop(0, half // 64, finish_rows, 0)
 
 
-def front(ends, cells, skip, edge_prev, edge_next, table, gain, attn_gain, weight, block=256):
+def front(ends, cells, skip, edge_prev, edge_next, table, weight, block=256):
     rows, width = skip.shape
     half = rows // 2
     whole = lambda array: pl.BlockSpec(array.shape, lambda n, s: (0,) * array.ndim)
-    small = (cells, skip, edge_prev, edge_next, table, gain, attn_gain)
+    small = (cells, skip, edge_prev, edge_next, table)
     return pl.pallas_call(
         front_kernel,
         grid_spec=pltpu.PrefetchScalarGridSpec(
@@ -157,9 +158,10 @@
 
 
 def back_kernel(
-    cells, skip, table, gain, grad, grad_prev, grad_next, weight, out,
+    cells, skip, table, grad, grad_prev, grad_next, weight, out,
     state_buf, scaled_buf, grad_buf, turned_buf, level_buf, scale_buf, sum_buf, weight_buf, arrived,
 ):
+    gain = table.at[4:5]
     rows, width = skip.shape
     half = rows // 2
     steps, _, block, _ = weight_buf.shape
@@ -241,11 +243,11 @@
         out[:, lanes] = (level_buf[0] + (scale * scaled - state * coef)).astype(BF16)
 
 
-def back(cells, skip, table, gain, grad, grad_prev, grad_next, weight, block=256):
+def back(cells, skip, table, grad, grad_prev, grad_next, weight, block=256):
     rows, width = skip.shape
     half = rows // 2
     whole = lambda array: pl.BlockSpec(array.shape, lambda n: (0,) * array.ndim)
-    small = (cells, skip, table, gain, grad, grad_prev, grad_next)
+    small = (cells, skip, table, grad, grad_prev, grad_next)
     return pl.pallas_call(
         back_kernel,
         grid=(1,),
@@ -537,14 +539,15 @@
 def gather_in_x(w_query, w_kv):
     seq = lax.axis_index("x")
     cols = w_query.shape[1] // 4
-    rows = jnp.zeros((4, w_query.shape[0], cols + w_kv.shape[1]), BF16)
+    rows = jnp.zeros((4, w_query.shape[0], cols + w_kv.shape[1] + 64), BF16)
+    w_kv = jnp.pad(w_kv, ((0, 0), (0, 64)))
     for k in range(4):
         head_cols = lax.dynamic_slice_in_dim(w_query, lax.rem(seq + k, 4) * cols, cols, 1)
         piece = jnp.concatenate([head_cols, w_kv], axis=1)
         if k:
             piece = turned(piece, "x", k)
         rows = lax.dynamic_update_index_in_dim(rows, piece, lax.rem(seq + 4 - k, 4), 0)
-    return rows.reshape(48, rows.shape[2])
+    return rows
 
 
 def after(value, *others):
@@ -616,37 +619,36 @@
     edge_next = behind(edge(bases[0, :span], skip[:8]))
     w_rows = gather_in_x(w_query, w_kv)
     out_home = moved(w_out, lambda z, y, c, x: (y, x, c, z))
-    beside = lax.ppermute(cot, "x", [(i, i ^ 1) for i in range(4)])
+    beside = lax.ppermute(after(cot, w_rows), "x", [(i, i ^ 1) for i in range(4)])
     across = lax.ppermute(jnp.stack([cot, beside]), "x", [(i, 3 - i) for i in range(4)])
-    pieces = around(w_rows, "y")
-    out_rows = gathered(out_home, "y").reshape(48, width)
     side = width // 3
+    cols = w_rows.shape[2]
+    chunks = out_home.reshape(12, 4, width // 4).transpose(1, 0, 2)
+    pieces = jnp.stack(around(jnp.concatenate([w_rows, chunks], axis=2), "y"))
+    out_rows = jnp.roll(pieces[:, :, :, cols:], lax.axis_index("y"), axis=0)
+    out_rows = out_rows.transpose(0, 2, 1, 3).reshape(48, width)
+    rest = pieces[:, :, :, side:cols].reshape(4, 48, cols - side)
     joint = jnp.concatenate(
-        [piece[:, :side] for piece in pieces]
-        + [out_rows[:, p * side : (p + 1) * side] for p in range(3)]
-        + [
-            jnp.concatenate(
-                [jnp.pad(piece[:, side:], ((0, 0), (0, 64))) for piece in pieces], axis=1
-            )
+        [
+            pieces[:, :, :, :side].reshape(192, side),
+            out_rows.reshape(48, 3, side).transpose(1, 0, 2).reshape(144, side),
+            rest.transpose(1, 0, 2).reshape(48, side),
         ],
         axis=0,
     )
-    edge_next = after(edge_next, beside, out_home)
-    gain = conv_gain[None, :]
+    near = jnp.stack(around(joint, "z"))
+    table = jnp.concatenate([base_table, conv_gain[None, :], attn_gain[None, :]], axis=0)
     pooled, normed = front(
-        ends, cells, skip, edge_prev, edge_next, base_table, gain, attn_gain[None, :], conv_weight
+        ends, cells, skip, edge_prev, edge_next, table, conv_weight
     )
     norms = around(normed)
-    joint = after(joint, normed, across)
-    near = jnp.stack(around(joint, "z"))
-    far = flipped(after(near, *norms))
+    far = flipped(after(near, normed, across))
 
     spot = [seq, lax.axis_index("c"), lax.axis_index("z"), lax.axis_index("y")]
     spot = jnp.stack(spot).astype(jnp.int32)
     d_in, heads, normed_all, cot_all, full_out, *d_parts = attend(spot, norms, (cot, beside, across), near, far)
     d_parts[1:] = [turned(d_parts[k], "x", k) for k in range(1, 4)]
     own, other = grads(spot, normed_all, d_in, heads, cot_all)
-    out_parts = mix(spot, heads, full_out)
     mine = (own.astype(F32) + flipped(other).astype(F32)).astype(BF16)
     total = mine[0].astype(F32)
     for k in range(1, 4):
@@ -659,10 +661,11 @@
 
     d_pooled = cot.astype(F32) + rms_back(pooled, attn_gain, d_normed)
     grad = (d_pooled * 0.5).astype(BF16)
+    out_parts = mix(spot, after(heads, grad), full_out)
     grad_prev, grad_next = ahead(grad[half - 16 :]), behind(grad[:16])
     grad_next = after(grad_next, mine)
     coarse = (pooled + returned(after(out_parts, grad_prev))).astype(BF16)
-    skip_grad = back(cells, skip, base_table, gain, grad, grad_prev, grad_next, conv_weight)
+    skip_grad = back(cells, skip, table, grad, grad_prev, grad_next, conv_weight)
 
     factor = 1.0 / 32
     cols = w_query.shape[1] // 4

time: 209 us -> 203 us (0.971)
  starting transfers between devices: 88.2 us -> 78.8 us
    ppermute x27 -> x24, starting transfers between devices: 36.8 us -> 31.4 us  [turned(): return lax.ppermute(value, axis, [(i, (i + by) % 4) for i in range(4)])]
    ppermute x27 -> x24, waiting for transfers between devices: 27.1 us -> 31.9 us  [turned(): return lax.ppermute(value, axis, [(i, (i + by) % 4) for i in range(4)])]
    ppermute x8, waiting for transfers between devices: 11.2 us -> 8.33 us  [moved(): return lax.ppermute(value, AXES, pairs)]
    ppermute x2, starting transfers between devices: 8.58 us -> 5.91 us  [behind(): return lax.ppermute(value, 'x', [(i + 1, i) for i in range(3)])]
    ppermute x8, starting transfers between devices: 38.2 us -> 36 us  [moved(): return lax.ppermute(value, AXES, pairs)]
    unnamed x48 -> x40, local copies, waits for them, and re-layouts: 4.2 us -> 3.57 us
  transfers between devices with their start and end apart: 41 -> 38, of which waited for: 16 -> 8; matrix products, arithmetic and copies ran while one was open for 8% -> 9% of each run, Pallas kernels for 14% -> 15%
where the time goes in v3:
time: 203 us; the launch traced here: 201 us
  starting transfers between devices  78.8 us (39%)
  Pallas kernels  51.6 us (25%)
  waiting for transfers between devices  40.3 us (20%)
  other arithmetic  15.5 us (8%)
  local copies, waits for them, and re-layouts  12.9 us (6%)
    ppermute x8, starting transfers between devices, moved(): return lax.ppermute(value, AXES, pairs)  36 us
    ppermute x24, waiting for transfers between devices, turned(): return lax.ppermute(value, axis, [(i, (i + by) % 4) for i in range(4)])  31.9 us
    ppermute x24, starting transfers between devices, turned(): return lax.ppermute(value, axis, [(i, (i + by) % 4) for i in range(4)])  31.4 us
    pallas_call x1, Pallas kernels, attend(): pl.pallas_call(attend_kernel, grid_spec=pltpu.PrefetchScalarGridSpec(num_...  14.9 us
    pallas_call x1, Pallas kernels, back(): pl.pallas_call(back_kernel, grid=(1,), in_specs=[whole(a) for a in small]...  12.8 us
    pallas_call x1, Pallas kernels, front(): pl.pallas_call(front_kernel, grid_spec=pltpu.PrefetchScalarGridSpec(num_s...  11.6 us
    ppermute x8, waiting for transfers between devices, moved(): return lax.ppermute(value, AXES, pairs)  8.33 us
    pallas_call x1, Pallas kernels, grads(): pl.pallas_call(grads_kernel, grid_spec=pltpu.PrefetchScalarGridSpec(num_s...  7.05 us
  transfers between devices with their start and end apart: 38, of which 8 were waited for; matrix products, arithmetic and copies ran while one was open for 9% of the time, Pallas kernels for 15%

profile of v3, /device:TPU:15, one launch (start us, length us, event | category | flops | bytes accessed | tf_op | source)
XLA Modules:
  0.0 200.6 jit_solution(124860791903170372)
XLA Ops:
  2.5 2.1 %collective-permute-start.6 = (bf16[12,640]{1,0:T(8,128)(2,1)S(1)}, bf16[12,640]{1,0:T(8,128)(2,1)S(1)}, u32[]{:S(2)}, u32[]{:S(2)}) collective-permute-start(bf16[12,640]{1,0:T(8,128)(2,1)S(1)} %get-tuple-element.85), channel_id=1, source_target_pairs={{0,2},{1,3},{2,0},{3,1},{4,6},{5,7},{6,4},{7,5},{8,10},{9,11},{10,... | collective-permute-start | bytes 46088 | tf_op jit(solution)/shard_map/ppermute | solution.py:500
  4.6 7.7 %collective-permute-start.10 = (bf16[12,1536]{1,0:T(8,128)(2,1)}, bf16[12,1536]{1,0:T(8,128)(2,1)S(1)}, u32[]{:S(2)}, u32[]{:S(2)}) collective-permute-start(bf16[12,1536]{1,0:T(8,128)(2,1)} %param.18), channel_id=1, source_target_pairs={{0,0},{1,8},{2,16},{3,24},{4,4},{5,12},{6,20},{7,28},{8,32},{9,40}... | collective-permute-start | bytes 110600 | tf_op jit(solution)/shard_map/ppermute | solution.py:492
  18.6 2.2 %collective-permute-start.8 = (bf16[128,1536]{1,0:T(8,128)(2,1)}, bf16[128,1536]{1,0:T(8,128)(2,1)S(1)}, u32[]{:S(2)}, u32[]{:S(2)}) collective-permute-start(bf16[128,1536]{1,0:T(8,128)(2,1)} %bitcast.146), channel_id=1, source_target_pairs={{0,1},{1,0},{2,3},{3,2},{4,5},{5,4},{6,7},{7,6},{8,9},{9,8},{10,11... | collective-permute-start | bytes 1179656 | tf_op jit(solution)/shard_map/ppermute | solution.py:622
  20.9 2.3 %collective-permute-start.13 = (bf16[4,12,1024]{2,0,1:T(4,128)(2,1)S(1)}, bf16[4,12,1024]{2,0,1:T(4,128)(2,1)S(1)}, u32[]{:S(2)}, u32[]{:S(2)}) collective-permute-start(bf16[4,12,1024]{2,0,1:T(4,128)(2,1)S(1)} %get-tuple-element.73), channel_id=1, source_target_pairs={{0,8},{8,16},{16,24},{24,0},{1,9},{9,17},{17,25},{25,1},{2,10},{10... | collective-permute-start | bytes 294920 | tf_op jit(solution)/shard_map/ppermute | solution.py:500
  32.6 2.5 %collective-permute-start.14 = (bf16[384,512]{1,0:T(8,128)(2,1)S(1)}, bf16[384,512]{1,0:T(8,128)(2,1)}, u32[]{:S(2)}, u32[]{:S(2)}) collective-permute-start(bf16[384,512]{1,0:T(8,128)(2,1)S(1)} %get-tuple-element.71), channel_id=1, source_target_pairs={{0,96},{32,0},{64,32},{96,64},{1,97},{33,1},{65,33},{97,65},{2,98}... | collective-permute-start | bytes 1179656 | tf_op jit(solution)/shard_map/ppermute | solution.py:500
  38.4 11.6 %front.1 = (f32[128,1536]{1,0:T(8,128)}, bf16[128,1536]{1,0:T(8,128)(2,1)}) custom-call(s32[2]{0:T(128)} %pad_add_fusion.ends, s32[256,64]{1,0:T(8,128)} %reshape.114.cells, bf16[256,1536]{1,0:T(8,128)(2,1)} %bitcast.142, bf16[8,1664]{1,0:T(8,128)(2,1)} %copy-done.11, bf16[8,1664]{1,0:T(8,128)(2,1)} %copy-done.12, f32[6,1536]{1,0:T(8,128)} %pad_maximum_fusion.6.table, ...), custom_call_target="tpu_custom_call" | custom-call | flops 3019898880 | bytes 26738688 | tf_op jit(solution)/shard_map/front/pallas_call | solution.py:130
  50.0 2.3 %collective-permute-done.14 = bf16[384,512]{1,0:T(8,128)(2,1)} collective-permute-done((bf16[384,512]{1,0:T(8,128)(2,1)S(1)}, bf16[384,512]{1,0:T(8,128)(2,1)}, u32[]{:S(2)}, u32[]{:S(2)}) %collective-permute-start.14) | collective-permute-done | bytes 393248 | tf_op jit(solution)/shard_map/ppermute | solution.py:500
  60.8 6.7 %collective-permute-done.2.norm1 = bf16[128,1536]{1,0:T(8,128)(2,1)S(1)} collective-permute-done((bf16[128,1536]{1,0:T(8,128)(2,1)}, bf16[128,1536]{1,0:T(8,128)(2,1)S(1)}, u32[]{:S(2)}, u32[]{:S(2)}) %collective-permute-start.2) | collective-permute-done | bytes 393248 | tf_op jit(solution)/shard_map/ppermute | solution.py:500
  67.4 9.2 %collective-permute-done.3.norm2 = bf16[128,1536]{1,0:T(8,128)(2,1)} collective-permute-done((bf16[128,1536]{1,0:T(8,128)(2,1)}, bf16[128,1536]{1,0:T(8,128)(2,1)}, u32[]{:S(2)}, u32[]{:S(2)}) %collective-permute-start.3) | collective-permute-done | bytes 393248 | tf_op jit(solution)/shard_map/ppermute | solution.py:500
  77.8 14.9 %attend.1 = (bf16[512,640]{1,0:T(8,128)(2,1)}, bf16[2,512,192]{2,1,0:T(8,128)(2,1)}, bf16[512,1536]{1,0:T(8,128)(2,1)}, bf16[512,1536]{1,0:T(8,128)(2,1)}, bf16[...) custom-call(s32[4]{0:T(128)} %pad_add_fusion.1.place, ...), custom_call_target="tpu_custom_call" | custom-call | flops 3623878656 | bytes 9437184 | tf_op jit(solution)/shard_map/attend/pallas_call | solution.py:368
  92.7 7.1 %grads.1 = (bf16[4,1536,128]{2,1,0:T(8,128)(2,1)}, bf16[4,1536,128]{2,1,0:T(8,128)(2,1)}) custom-call(s32[4]{0:T(128)} %pad_add_fusion.1.place, bf16[512,1536]{1,0:T(8,128)(2,1)} %get-tuple-element.33.normed, bf16[512,640]{1,0:T(8,128)(2,1)} %get-tuple-element.34.d_in, bf16[2,512,192]{2,1,0:T(8,128)(2,1)} %get-tuple-element.43.heads, ...), custom_call_target="tpu_custom_call" | custom-call | flops 1610612736 | bytes 12582912 | tf_op jit(solution)/shard_map/grads/pallas_call | solution.py:426
  100.6 3.2 %collective-permute-done.19 = bf16[4,1536,128]{2,1,0:T(8,128)(2,1)S(1)} collective-permute-done((bf16[4,1536,128]{2,1,0:T(8,128)(2,1)}, bf16[4,1536,128]{2,1,0:T(8,128)(2,1)S(1)}, u32[]{:S(2)}, u32[]{:S(2)}) %collective-permute-start.19) | collective-permute-done | bytes 1572896 | tf_op jit(solution)/shard_map/ppermute | solution.py:492
  106.7 2.3 %collective-permute-start.22 = (bf16[1536,128]{1,0:T(8,128)(2,1)}, bf16[1536,128]{1,0:T(8,128)(2,1)}, u32[]{:S(2)}, u32[]{:S(2)}) collective-permute-start(bf16[1536,128]{1,0:T(8,128)(2,1)} %get-tuple-element.61), channel_id=1, source_target_pairs={{0,96},{32,0},{64,32},{96,64},{1,97},{33,1},{65,33},{97,65},{2,98}... | collective-permute-start | bytes 1179656 | tf_op jit(solution)/shard_map/ppermute | solution.py:500
  113.5 4.6 %collective-permute-done.22 = bf16[1536,128]{1,0:T(8,128)(2,1)} collective-permute-done((bf16[1536,128]{1,0:T(8,128)(2,1)}, bf16[1536,128]{1,0:T(8,128)(2,1)}, u32[]{:S(2)}, u32[]{:S(2)}) %collective-permute-start.22) | collective-permute-done | bytes 393248 | tf_op jit(solution)/shard_map/ppermute | solution.py:500
  118.0 2.4 %collective-permute-start.18 = (bf16[128,1536]{1,0:T(8,128)(2,1)}, bf16[128,1536]{1,0:T(8,128)(2,1)S(1)}, u32[]{:S(2)}, u32[]{:S(2)}) collective-permute-start(bf16[128,1536]{1,0:T(8,128)(2,1)} %get-tuple-element.32), channel_id=1, source_target_pairs={{0,1},{1,2},{2,3},{3,0},{4,5},{5,6},{6,7},{7,4},{8,9},{9,10},{10,1... | collective-permute-start | bytes 1179656 | tf_op jit(solution)/shard_map/ppermute | solution.py:500
  120.9 8.7 %collective-permute-done.20 = bf16[1536,128]{1,0:T(8,128)(2,1)} collective-permute-done((bf16[1536,128]{1,0:T(8,128)(2,1)S(1)}, bf16[1536,128]{1,0:T(8,128)(2,1)}, u32[]{:S(2)}, u32[]{:S(2)}) %collective-permute-start.20) | collective-permute-done | bytes 393248 | tf_op jit(solution)/shard_map/ppermute | solution.py:500
  133.9 4.0 %collective-permute-start.29 = (bf16[16,1536]{1,0:T(8,128)(2,1)S(1)}, bf16[16,1536]{1,0:T(8,128)(2,1)S(1)}, u32[]{:S(2)}, u32[]{:S(2)}) collective-permute-start(bf16[16,1536]{1,0:T(8,128)(2,1)S(1)} %get-tuple-element.68), channel_id=1, source_target_pairs={{1,0},{2,1},{3,2},{5,4},{6,5},{7,6},{9,8},{10,9},{11,10},{13,12},{... | collective-permute-start | bytes 147464 | tf_op jit(solution)/shard_map/ppermute | solution.py:609
  142.0 5.2 %mix.1 = bf16[4,128,1536]{2,1,0:T(8,128)(2,1)} custom-call(s32[4]{0:T(128)} %pad_add_fusion.1.place, bf16[2,512,192]{2,1,0:T(8,128)(2,1)} %get-tuple-element.43.heads, bf16[384,1536]{1,0:T(8,128)(2,1)} %get-tuple-element.44.w_out), custom_call_target="tpu_custom_call" | custom-call | flops 603979776 | bytes 2359296 | tf_op jit(solution)/shard_map/mix/pallas_call | solution.py:457
  153.4 12.8 %back.1 = bf16[256,1536]{1,0:T(8,128)(2,1)} custom-call(s32[256,64]{1,0:T(8,128)} %reshape.114.cells, bf16[256,1536]{1,0:T(8,128)(2,1)} %bitcast.143, f32[6,1536]{1,0:T(8,128)} %pad_maximum_fusion.6.table, bf16[128,1536]{1,0:T(8,128)(2,1)} %copy-done.2, bf16[16,1536]{1,0:T(8,128)(2,1)} %copy-done.9, bf16[16,1536]{1,0:T(8,128)(2,1)} %copy-done.10, ...), custom_call_target="tpu_custom_call" | custom-call | flops 3019898880 | bytes 26738688 | tf_op jit(solution)/shard_map/back/pallas_call | solution.py:251
  166.3 12.7 %collective-permute-start.33 = (bf16[12,640]{1,0:T(8,128)(2,1)S(1)}, bf16[12,640]{1,0:T(8,128)(2,1)S(1)}, u32[]{:S(2)}, u32[]{:S(2)}) collective-permute-start(bf16[12,640]{1,0:T(8,128)(2,1)S(1)} %bitcast.178), channel_id=1, source_target_pairs={{0,0},{1,1},{2,2},{3,3},{4,64},{5,65},{6,66},{7,67},{8,4},{9,5},{1... | collective-permute-start | bytes 46088 | tf_op jit(solution)/shard_map/ppermute | solution.py:492
  179.1 3.3 %collective-permute-start.34 = (bf16[12,640]{1,0:T(8,128)(2,1)S(1)}, bf16[12,640]{1,0:T(8,128)(2,1)S(1)}, u32[]{:S(2)}, u32[]{:S(2)}) collective-permute-start(bf16[12,640]{1,0:T(8,128)(2,1)S(1)} %bitcast.176), channel_id=1, source_target_pairs={{0,1},{1,2},{2,3},{3,0},{4,65},{5,66},{6,67},{7,64},{8,5},{9,6},{1... | collective-permute-start | bytes 46088 | tf_op jit(solution)/shard_map/ppermute | solution.py:492
  182.4 3.5 %collective-permute-start.35 = (bf16[12,640]{1,0:T(8,128)(2,1)S(1)}, bf16[12,640]{1,0:T(8,128)(2,1)S(1)}, u32[]{:S(2)}, u32[]{:S(2)}) collective-permute-start(bf16[12,640]{1,0:T(8,128)(2,1)S(1)} %bitcast.175), channel_id=1, source_target_pairs={{0,2},{1,3},{2,0},{3,1},{4,66},{5,67},{6,64},{7,65},{8,6},{9,7},{1... | collective-permute-start | bytes 46088 | tf_op jit(solution)/shard_map/ppermute | solution.py:492
  186.0 5.2 %collective-permute-start.37 = (bf16[12,1536]{1,0:T(8,128)(2,1)S(1)}, bf16[12,1536]{1,0:T(8,128)(2,1)S(1)}, u32[]{:S(2)}, u32[]{:S(2)}) collective-permute-start(bf16[12,1536]{1,0:T(8,128)(2,1)S(1)} %bitcast.171), channel_id=1, source_target_pairs={{0,0},{1,32},{2,64},{3,96},{4,16},{5,48},{6,80},{7,112},{8,1},{9,3... | collective-permute-start | bytes 110600 | tf_op jit(solution)/shard_map/ppermute | solution.py:492
  192.8 5.1 %collective-permute-done.37 = bf16[12,1536]{1,0:T(8,128)(2,1)S(1)} collective-permute-done((bf16[12,1536]{1,0:T(8,128)(2,1)S(1)}, bf16[12,1536]{1,0:T(8,128)(2,1)S(1)}, u32[]{:S(2)}, u32[]{:S(2)}) %collective-permute-start.37) | collective-permute-done | bytes 36896 | tf_op jit(solution)/shard_map/ppermute | solution.py:492
  (199 shorter events, 57.6 us)
Async XLA Ops:
  2.2 15.8 %collective-permute-start.5 = (bf16[12,640]{1,0:T(8,128)(2,1)S(1)}, bf16[12,640]{1,0:T(8,128)(2,1)S(1)}, u32[]{:S(2)}, u32[]{:S(2)}) collective-permute-start(bf16[12,640]{1,0:T(8,128)(2,1)S(1)} %get-tuple-element.84), channel_id=1, source_target_pairs={{0,1},{1,2},{2,3},{3,0},{4,5},{5,6},{6,7},{7,4},{8,9},{9,10},{10,1... | collective-permute-start | bytes 46088 | tf_op jit(solution)/shard_map/ppermute | solution.py:500
  2.5 15.6 %collective-permute-start.6 = (bf16[12,640]{1,0:T(8,128)(2,1)S(1)}, bf16[12,640]{1,0:T(8,128)(2,1)S(1)}, u32[]{:S(2)}, u32[]{:S(2)}) collective-permute-start(bf16[12,640]{1,0:T(8,128)(2,1)S(1)} %get-tuple-element.85), channel_id=1, source_target_pairs={{0,2},{1,3},{2,0},{3,1},{4,6},{5,7},{6,4},{7,5},{8,10},{9,11},{10,... | collective-permute-start | bytes 46088 | tf_op jit(solution)/shard_map/ppermute | solution.py:500
  4.6 13.5 %collective-permute-start.7 = (bf16[12,640]{1,0:T(8,128)(2,1)S(1)}, bf16[12,640]{1,0:T(8,128)(2,1)S(1)}, u32[]{:S(2)}, u32[]{:S(2)}) collective-permute-start(bf16[12,640]{1,0:T(8,128)(2,1)S(1)} %get-tuple-element.82), channel_id=1, source_target_pairs={{0,3},{1,0},{2,1},{3,2},{4,7},{5,4},{6,5},{7,6},{8,11},{9,8},{10,9... | collective-permute-start | bytes 46088 | tf_op jit(solution)/shard_map/ppermute | solution.py:500
  4.6 16.2 %collective-permute-start.10 = (bf16[12,1536]{1,0:T(8,128)(2,1)}, bf16[12,1536]{1,0:T(8,128)(2,1)S(1)}, u32[]{:S(2)}, u32[]{:S(2)}) collective-permute-start(bf16[12,1536]{1,0:T(8,128)(2,1)} %param.18), channel_id=1, source_target_pairs={{0,0},{1,8},{2,16},{3,24},{4,4},{5,12},{6,20},{7,28},{8,32},{9,40}... | collective-permute-start | bytes 110600 | tf_op jit(solution)/shard_map/ppermute | solution.py:492
  15.1 17.5 %collective-permute-start = (bf16[8,1664]{1,0:T(8,128)(2,1)S(1)}, bf16[8,1664]{1,0:T(8,128)(2,1)S(1)}, u32[]{:S(2)}, u32[]{:S(2)}) collective-permute-start(bf16[8,1664]{1,0:T(8,128)(2,1)S(1)} %concatenate.40), channel_id=1, source_target_pairs={{0,1},{1,2},{2,3},{4,5},{5,6},{6,7},{8,9},{9,10},{10,11},{12,13},{... | collective-permute-start | bytes 79880 | tf_op jit(solution)/shard_map/ppermute | solution.py:606
  30.5 23.0 %collective-permute-start.9 = (bf16[2,128,1536]{2,1,0:T(8,128)(2,1)S(1)}, bf16[2,128,1536]{2,1,0:T(8,128)(2,1)}, u32[]{:S(2)}, u32[]{:S(2)}) collective-permute-start(bf16[2,128,1536]{2,1,0:T(8,128)(2,1)S(1)} %pad_maximum_fusion.1), channel_id=1, source_target_pairs={{0,3},{1,2},{2,1},{3,0},{4,7},{5,6},{6,5},{7,4},{8,11},{9,10},{10,... | collective-permute-start | bytes 2359304 | tf_op jit(solution)/shard_map/ppermute | solution.py:623
  32.0 17.9 %collective-permute-start.16 = (bf16[384,512]{1,0:T(8,128)(2,1)S(1)}, bf16[384,512]{1,0:T(8,128)(2,1)S(1)}, u32[]{:S(2)}, u32[]{:S(2)}) collective-permute-start(bf16[384,512]{1,0:T(8,128)(2,1)S(1)} %get-tuple-element.71), channel_id=1, source_target_pairs={{0,32},{32,64},{64,96},{96,0},{1,33},{33,65},{65,97},{97,1},{2,34}... | collective-permute-start | bytes 1179656 | tf_op jit(solution)/shard_map/ppermute | solution.py:500
  32.6 17.4 %collective-permute-start.15 = (bf16[384,512]{1,0:T(8,128)(2,1)S(1)}, bf16[384,512]{1,0:T(8,128)(2,1)S(1)}, u32[]{:S(2)}, u32[]{:S(2)}) collective-permute-start(bf16[384,512]{1,0:T(8,128)(2,1)S(1)} %get-tuple-element.71), channel_id=1, source_target_pairs={{0,64},{32,96},{64,0},{96,32},{1,65},{33,97},{65,1},{97,33},{2,66}... | collective-permute-start | bytes 1179656 | tf_op jit(solution)/shard_map/ppermute | solution.py:500
  32.6 19.7 %collective-permute-start.14 = (bf16[384,512]{1,0:T(8,128)(2,1)S(1)}, bf16[384,512]{1,0:T(8,128)(2,1)}, u32[]{:S(2)}, u32[]{:S(2)}) collective-permute-start(bf16[384,512]{1,0:T(8,128)(2,1)S(1)} %get-tuple-element.71), channel_id=1, source_target_pairs={{0,96},{32,0},{64,32},{96,64},{1,97},{33,1},{65,33},{97,65},{2,98}... | collective-permute-start | bytes 1179656 | tf_op jit(solution)/shard_map/ppermute | solution.py:500
  53.5 23.1 %collective-permute-start.17 = (bf16[4,384,512]{2,1,0:T(8,128)(2,1)S(1)}, bf16[4,384,512]{2,1,0:T(8,128)(2,1)S(1)}, u32[]{:S(2)}, u32[]{:S(2)}) collective-permute-start(bf16[4,384,512]{2,1,0:T(8,128)(2,1)S(1)} %pad_maximum_fusion.near), channel_id=1, source_target_pairs={{0,4},{1,5},{2,6},{3,7},{4,0},{5,1},{6,2},{7,3},{8,12},{9,13},{10,... | collective-permute-start | bytes 4718600 | tf_op jit(solution)/shard_map/ppermute | solution.py:492
  55.3 12.1 %collective-permute-start.2 = (bf16[128,1536]{1,0:T(8,128)(2,1)}, bf16[128,1536]{1,0:T(8,128)(2,1)S(1)}, u32[]{:S(2)}, u32[]{:S(2)}) collective-permute-start(bf16[128,1536]{1,0:T(8,128)(2,1)} %get-tuple-element.27.norm0), channel_id=1, source_target_pairs={{0,3},{1,0},{2,1},{3,2},{4,7},{5,4},{6,5},{7,6},{8,11},{9,8},{10,9... | collective-permute-start | bytes 1179656 | tf_op jit(solution)/shard_map/ppermute | solution.py:500
  56.9 19.7 %collective-permute-start.3 = (bf16[128,1536]{1,0:T(8,128)(2,1)}, bf16[128,1536]{1,0:T(8,128)(2,1)}, u32[]{:S(2)}, u32[]{:S(2)}) collective-permute-start(bf16[128,1536]{1,0:T(8,128)(2,1)} %get-tuple-element.27.norm0), channel_id=1, source_target_pairs={{0,2},{1,3},{2,0},{3,1},{4,6},{5,7},{6,4},{7,5},{8,10},{9,11},{10,... | collective-permute-start | bytes 1179656 | tf_op jit(solution)/shard_map/ppermute | solution.py:500
  58.7 17.9 %collective-permute-start.4 = (bf16[128,1536]{1,0:T(8,128)(2,1)}, bf16[128,1536]{1,0:T(8,128)(2,1)}, u32[]{:S(2)}, u32[]{:S(2)}) collective-permute-start(bf16[128,1536]{1,0:T(8,128)(2,1)} %get-tuple-element.27.norm0), channel_id=1, source_target_pairs={{0,1},{1,2},{2,3},{3,0},{4,5},{5,6},{6,7},{7,4},{8,9},{9,10},{10,1... | collective-permute-start | bytes 1179656 | tf_op jit(solution)/shard_map/ppermute | solution.py:500
  109.2 20.4 %collective-permute-start.20 = (bf16[1536,128]{1,0:T(8,128)(2,1)S(1)}, bf16[1536,128]{1,0:T(8,128)(2,1)}, u32[]{:S(2)}, u32[]{:S(2)}) collective-permute-start(bf16[1536,128]{1,0:T(8,128)(2,1)S(1)} %get-tuple-element.60), channel_id=1, source_target_pairs={{0,32},{32,64},{64,96},{96,0},{1,33},{33,65},{65,97},{97,1},{2,34}... | collective-permute-start | bytes 1179656 | tf_op jit(solution)/shard_map/ppermute | solution.py:500
  110.0 21.1 %collective-permute-start.24 = (bf16[128,1536]{1,0:T(8,128)(2,1)}, bf16[128,1536]{1,0:T(8,128)(2,1)S(1)}, u32[]{:S(2)}, u32[]{:S(2)}) collective-permute-start(bf16[128,1536]{1,0:T(8,128)(2,1)} %get-tuple-element.41), channel_id=1, source_target_pairs={{0,3},{1,0},{2,1},{3,2},{4,7},{5,4},{6,5},{7,6},{8,11},{9,8},{10,9... | collective-permute-start | bytes 1179656 | tf_op jit(solution)/shard_map/ppermute | solution.py:500
  111.4 19.7 %collective-permute-start.23 = (bf16[128,1536]{1,0:T(8,128)(2,1)}, bf16[128,1536]{1,0:T(8,128)(2,1)S(1)}, u32[]{:S(2)}, u32[]{:S(2)}) collective-permute-start(bf16[128,1536]{1,0:T(8,128)(2,1)} %get-tuple-element.39), channel_id=1, source_target_pairs={{0,2},{1,3},{2,0},{3,1},{4,6},{5,7},{6,4},{7,5},{8,10},{9,11},{10,... | collective-permute-start | bytes 1179656 | tf_op jit(solution)/shard_map/ppermute | solution.py:500
  118.0 13.1 %collective-permute-start.18 = (bf16[128,1536]{1,0:T(8,128)(2,1)}, bf16[128,1536]{1,0:T(8,128)(2,1)S(1)}, u32[]{:S(2)}, u32[]{:S(2)}) collective-permute-start(bf16[128,1536]{1,0:T(8,128)(2,1)} %get-tuple-element.32), channel_id=1, source_target_pairs={{0,1},{1,2},{2,3},{3,0},{4,5},{5,6},{6,7},{7,4},{8,9},{9,10},{10,1... | collective-permute-start | bytes 1179656 | tf_op jit(solution)/shard_map/ppermute | solution.py:500
  132.6 14.6 %collective-permute-start.25 = (bf16[16,1536]{1,0:T(8,128)(2,1)S(1)}, bf16[16,1536]{1,0:T(8,128)(2,1)S(1)}, u32[]{:S(2)}, u32[]{:S(2)}) collective-permute-start(bf16[16,1536]{1,0:T(8,128)(2,1)S(1)} %get-tuple-element.69), channel_id=1, source_target_pairs={{0,1},{1,2},{2,3},{4,5},{5,6},{6,7},{8,9},{9,10},{10,11},{12,13},{... | collective-permute-start | bytes 147464 | tf_op jit(solution)/shard_map/ppermute | solution.py:606
  133.9 18.3 %collective-permute-start.29 = (bf16[16,1536]{1,0:T(8,128)(2,1)S(1)}, bf16[16,1536]{1,0:T(8,128)(2,1)S(1)}, u32[]{:S(2)}, u32[]{:S(2)}) collective-permute-start(bf16[16,1536]{1,0:T(8,128)(2,1)S(1)} %get-tuple-element.68), channel_id=1, source_target_pairs={{1,0},{2,1},{3,2},{5,4},{6,5},{7,6},{9,8},{10,9},{11,10},{13,12},{... | collective-permute-start | bytes 147464 | tf_op jit(solution)/shard_map/ppermute | solution.py:609
  148.5 50.0 %collective-permute-start.28 = (bf16[128,1536]{1,0:T(8,128)(2,1)S(1)}, bf16[128,1536]{1,0:T(8,128)(2,1)S(1)}, u32[]{:S(2)}, u32[]{:S(2)}) collective-permute-start(bf16[128,1536]{1,0:T(8,128)(2,1)S(1)} %get-tuple-element.58), channel_id=1, source_target_pairs={{0,3},{1,0},{2,1},{3,2},{4,7},{5,4},{6,5},{7,6},{8,11},{9,8},{10,9... | collective-permute-start | bytes 1179656 | tf_op jit(solution)/shard_map/ppermute | solution.py:500
  149.0 49.5 %collective-permute-start.27 = (bf16[128,1536]{1,0:T(8,128)(2,1)S(1)}, bf16[128,1536]{1,0:T(8,128)(2,1)S(1)}, u32[]{:S(2)}, u32[]{:S(2)}) collective-permute-start(bf16[128,1536]{1,0:T(8,128)(2,1)S(1)} %get-tuple-element.59), channel_id=1, source_target_pairs={{0,2},{1,3},{2,0},{3,1},{4,6},{5,7},{6,4},{7,5},{8,10},{9,11},{10,... | collective-permute-start | bytes 1179656 | tf_op jit(solution)/shard_map/ppermute | solution.py:500
  150.2 48.3 %collective-permute-start.26 = (bf16[128,1536]{1,0:T(8,128)(2,1)S(1)}, bf16[128,1536]{1,0:T(8,128)(2,1)}, u32[]{:S(2)}, u32[]{:S(2)}) collective-permute-start(bf16[128,1536]{1,0:T(8,128)(2,1)S(1)} %get-tuple-element.57), channel_id=1, source_target_pairs={{0,1},{1,2},{2,3},{3,0},{4,5},{5,6},{6,7},{7,4},{8,9},{9,10},{10,1... | collective-permute-start | bytes 1179656 | tf_op jit(solution)/shard_map/ppermute | solution.py:500
  152.5 26.6 %collective-permute-start.36 = (bf16[12,640]{1,0:T(8,128)(2,1)S(1)}, bf16[12,640]{1,0:T(8,128)(2,1)S(1)}, u32[]{:S(2)}, u32[]{:S(2)}) collective-permute-start(bf16[12,640]{1,0:T(8,128)(2,1)S(1)} %bitcast.177), channel_id=1, source_target_pairs={{0,3},{1,0},{2,1},{3,2},{4,67},{5,64},{6,65},{7,66},{8,7},{9,4},{1... | collective-permute-start | bytes 46088 | tf_op jit(solution)/shard_map/ppermute | solution.py:492
  166.3 16.1 %collective-permute-start.33 = (bf16[12,640]{1,0:T(8,128)(2,1)S(1)}, bf16[12,640]{1,0:T(8,128)(2,1)S(1)}, u32[]{:S(2)}, u32[]{:S(2)}) collective-permute-start(bf16[12,640]{1,0:T(8,128)(2,1)S(1)} %bitcast.178), channel_id=1, source_target_pairs={{0,0},{1,1},{2,2},{3,3},{4,64},{5,65},{6,66},{7,67},{8,4},{9,5},{1... | collective-permute-start | bytes 46088 | tf_op jit(solution)/shard_map/ppermute | solution.py:492
  (29 other events, 290.8 us)

commit v4 on v3

--- a/solution.py
+++ b/solution.py
@@ -275,7 +275,8 @@
 
 def attend_kernel(
     place, norm0, norm1, norm2, norm3, cot0, cot1, cot2, near, far,
-    d_in, heads, normed, cot, w_out, own, part1, part2, part3, w_in, query_kv, acc,
+    heads, w_out, own, part1, part2, part3, near_sum, far_sum,
+    d_in, normed, cot, w_in, query_kv, acc, rows_in, rows_out,
 ):
     head = pl.program_id(0)
     seq, core, depth, level = place[0], place[1], place[2], place[3]
@@ -321,7 +322,7 @@
     expo = jnp.exp(scores - jnp.max(scores, axis=1, keepdims=True))
     probs = expo * (1.0 / jnp.sum(expo, axis=1, keepdims=True))
     weights = probs.astype(BF16)
-    heads[0] = ndot(weights, values).astype(BF16)
+    heads[head] = ndot(weights, values).astype(BF16)
     d_probs = rdot(d_heads, values)
     inner = jnp.sum(probs * d_probs, axis=1, keepdims=True)
     d_scores = (probs * (d_probs - inner) * inv).astype(BF16)
@@ -346,6 +347,26 @@
         for piece, out in enumerate((own, part1, part2, part3)):
             rows = d_in[rows_of(lax.rem(seq + piece, 4)), :]
             out[...] = rdot(rows, w_in[...]).astype(out.dtype)
+        width = cot.shape[1]
+        blocks = cols // 128
+        for half_core, out in ((1 - core, far_sum), (core, near_sum)):
+            tall = width // 2
+            lanes = pl.ds(pl.multiple_of(half_core * tall, tall), tall)
+            rows_in[...] = tdot(normed[:, lanes], d_in[...]).astype(BF16)
+            rows_out[...] = tdot(heads[half_core], cot[...]).astype(BF16)
+            for turn in range(4):
+                quarter = lax.rem(depth + turn, 4)
+                count = tall // 4
+                at = pl.ds(pl.multiple_of(quarter * count, count), count)
+                for b in range(blocks):
+                    out[turn, b * count : (b + 1) * count, :] = rows_in[at, b * 128 : (b + 1) * 128]
+                base = blocks * count
+                count = VD // 4
+                at = pl.ds(pl.multiple_of(quarter * count, count), count)
+                for b in range(width // 128):
+                    out[turn, base + b * count : base + (b + 1) * count, :] = rows_out[
+                        at, b * 128 : (b + 1) * 128
+                    ]
 
 
 def attend(place, norms, cots, near, far):
@@ -354,16 +375,17 @@
     cols = near.shape[2] + 128
     heads = 2
     whole = lambda array: pl.BlockSpec(array.shape, lambda h, s: (0,) * array.ndim)
-    outs = [
-        jax.ShapeDtypeStruct((rows, cols), BF16),
-        jax.ShapeDtypeStruct((heads, rows, VD), BF16),
-        jax.ShapeDtypeStruct((rows, width), BF16),
-        jax.ShapeDtypeStruct((rows, width), BF16),
-        jax.ShapeDtypeStruct((heads * VD, width), BF16),
-        jax.ShapeDtypeStruct((half, width), F32),
-    ] + [jax.ShapeDtypeStruct((half, width), BF16)] * 3
+    length = cols // 128 * (width // 8) + width // 128 * (VD // 4)
+    outs = (
+        [
+            jax.ShapeDtypeStruct((heads, rows, VD), BF16),
+            jax.ShapeDtypeStruct((heads * VD, width), BF16),
+            jax.ShapeDtypeStruct((half, width), F32),
+        ]
+        + [jax.ShapeDtypeStruct((half, width), BF16)] * 3
+        + [jax.ShapeDtypeStruct((4, length, 128), BF16)] * 2
+    )
     specs = [whole(out) for out in outs]
-    specs[1] = pl.BlockSpec((1, rows, VD), lambda h, s: (h, 0, 0))
     ins = (*norms, *cots, near, far)
     return pl.pallas_call(
         attend_kernel,
@@ -373,76 +395,24 @@
             in_specs=[whole(a) for a in ins],
             out_specs=specs,
             scratch_shapes=[
+                pltpu.VMEM((rows, cols), BF16),
+                pltpu.VMEM((rows, width), BF16),
+                pltpu.VMEM((rows, width), BF16),
                 pltpu.VMEM((width, cols), BF16),
                 pltpu.VMEM((rows, cols), BF16),
                 pltpu.VMEM((rows, HD + VD), F32),
+                pltpu.VMEM((width // 2, cols), BF16),
+                pltpu.VMEM((VD, width), BF16),
             ],
         ),
         out_shape=outs,
         compiler_params=pltpu.CompilerParams(vmem_limit_bytes=VMEM_LIMIT),
         cost_estimate=pl.CostEstimate(
-            flops=2 * rows * heads * (VD * width + 3 * rows * (HD + VD)) + 4 * rows * cols * width,
+            flops=2 * rows * heads * (2 * VD * width + 3 * rows * (HD + VD)) + 6 * rows * cols * width,
             bytes_accessed=8 * rows * width + 2 * heads * VD * width + 2 * cols * width,
             transcendentals=rows * heads * rows,
         ),
         name="attend",
-    )(place, *ins)
-
-
-def grads_kernel(place, normed, d_in, heads, cot, own, other, rows_in, rows_out):
-    core, depth = place[1], place[2]
-    width = cot.shape[1]
-    cols = d_in.shape[1]
-    side = width // 2
-    blocks = rows_in.shape[1] // 128
-    for turn, out in enumerate((other, own)):
-        half = core if turn else 1 - core
-        lanes = pl.ds(pl.multiple_of(half * side, side), side)
-        rows_in[:, 0:cols] = tdot(normed[:, lanes], d_in[...]).astype(BF16)
-        rows_out[...] = tdot(heads[half], cot[...]).astype(BF16)
-        for k in range(4):
-            quarter = lax.rem(depth + k, 4)
-            count = side // 4
-            at = pl.ds(pl.multiple_of(quarter * count, count), count)
-            for b in range(blocks):
-                out[k, b * count : (b + 1) * count, :] = rows_in[at, b * 128 : (b + 1) * 128]
-            base = blocks * count
-            count = VD // 4
-            at = pl.ds(pl.multiple_of(quarter * count, count), count)
-            for b in range(width // 128):
-                out[k, base + b * count : base + (b + 1) * count, :] = rows_out[
-                    at, b * 128 : (b + 1) * 128
-                ]
-
-
-def grads(place, normed, d_in, heads, cot):
-    rows, width = cot.shape
-    cols = d_in.shape[1]
-    blocks = (cols + 127) // 128
-    length = blocks * (width // 8) + width // 128 * (VD // 4)
-    whole = lambda array: pl.BlockSpec(array.shape, lambda n, s: (0,) * array.ndim)
-    outs = [jax.ShapeDtypeStruct((4, length, 128), BF16)] * 2
-    ins = (normed, d_in, heads, cot)
-    return pl.pallas_call(
-        grads_kernel,
-        grid_spec=pltpu.PrefetchScalarGridSpec(
-            num_scalar_prefetch=1,
-            grid=(1,),
-            in_specs=[whole(a) for a in ins],
-            out_specs=[whole(a) for a in outs],
-            scratch_shapes=[
-                pltpu.VMEM((width // 2, blocks * 128), BF16),
-                pltpu.VMEM((VD, width), BF16),
-            ],
-        ),
-        out_shape=outs,
-        compiler_params=pltpu.CompilerParams(vmem_limit_bytes=VMEM_LIMIT),
-        cost_estimate=pl.CostEstimate(
-            flops=2 * rows * width * (cols + 2 * VD),
-            bytes_accessed=16 * rows * width,
-            transcendentals=0,
-        ),
-        name="grads",
     )(place, *ins)
 
 
@@ -646,9 +616,8 @@
 
     spot = [seq, lax.axis_index("c"), lax.axis_index("z"), lax.axis_index("y")]
     spot = jnp.stack(spot).astype(jnp.int32)
-    d_in, heads, normed_all, cot_all, full_out, *d_parts = attend(spot, norms, (cot, beside, across), near, far)
+    heads, full_out, *d_parts, own, other = attend(spot, norms, (cot, beside, across), near, far)
     d_parts[1:] = [turned(d_parts[k], "x", k) for k in range(1, 4)]
-    own, other = grads(spot, normed_all, d_in, heads, cot_all)
     mine = (own.astype(F32) + flipped(other).astype(F32)).astype(BF16)
     total = mine[0].astype(F32)
     for k in range(1, 4):
@@ -661,7 +630,7 @@
 
     d_pooled = cot.astype(F32) + rms_back(pooled, attn_gain, d_normed)
     grad = (d_pooled * 0.5).astype(BF16)
-    out_parts = mix(spot, after(heads, grad), full_out)
+    out_parts = mix(spot, heads, full_out)
     grad_prev, grad_next = ahead(grad[half - 16 :]), behind(grad[:16])
     grad_next = after(grad_next, mine)
     coarse = (pooled + returned(after(out_parts, grad_prev))).astype(BF16)
@@ -670,6 +639,7 @@
     factor = 1.0 / 32
     cols = w_query.shape[1] // 4
     grad_query, grad_kv, grad_out = finish(mine, cols, width)
+    grad_query = after(grad_query, coarse)
     return (
         coarse[None],
         skip_grad[None],

time: 203 us -> 195 us (0.961)
  Pallas kernels: 51.6 us -> 46.8 us
  waiting for transfers between devices: 40.3 us -> 37.9 us
    pallas_call x1 -> x0, Pallas kernels: 7.05 us -> none  [grads(): pl.pallas_call(grads_kernel, grid_spec=pltpu.PrefetchScalarGridSpec(num_s...]
    ppermute x24, waiting for transfers between devices: 31.9 us -> 27.5 us  [turned(): return lax.ppermute(value, axis, [(i, (i + by) % 4) for i in range(4)])]
    pallas_call x1, Pallas kernels: 14.9 us -> 17.2 us  [attend(): pl.pallas_call(attend_kernel, grid_spec=pltpu.PrefetchScalarGridSpec(num_...]
    convert_element_type x0 -> x1, other arithmetic: none -> 2.2 us  [per_device(): coarse = (pooled + returned(after(out_parts, grad_prev))).astype(BF16)]
    broadcast_in_dim x1 -> x0, other arithmetic: 2.08 us -> none  [per_device(): coarse[None]]
    ppermute x8, waiting for transfers between devices: 8.33 us -> 10.4 us  [moved(): return lax.ppermute(value, AXES, pairs)]
where the time goes in v4:
time: 195 us; the launch traced here: 194 us
  starting transfers between devices  78.2 us (40%)
  Pallas kernels  46.8 us (24%)
  waiting for transfers between devices  37.9 us (19%)
  other arithmetic  16.1 us (8%)
  local copies, waits for them, and re-layouts  13.4 us (7%)
    ppermute x8, starting transfers between devices, moved(): return lax.ppermute(value, AXES, pairs)  35.5 us
    ppermute x24, starting transfers between devices, turned(): return lax.ppermute(value, axis, [(i, (i + by) % 4) for i in range(4)])  30.7 us
    ppermute x24, waiting for transfers between devices, turned(): return lax.ppermute(value, axis, [(i, (i + by) % 4) for i in range(4)])  27.5 us
    pallas_call x1, Pallas kernels, attend(): pl.pallas_call(attend_kernel, grid_spec=pltpu.PrefetchScalarGridSpec(num_...  17.2 us
    pallas_call x1, Pallas kernels, back(): pl.pallas_call(back_kernel, grid=(1,), in_specs=[whole(a) for a in small]...  12.8 us
    pallas_call x1, Pallas kernels, front(): pl.pallas_call(front_kernel, grid_spec=pltpu.PrefetchScalarGridSpec(num_s...  11.6 us
    ppermute x8, waiting for transfers between devices, moved(): return lax.ppermute(value, AXES, pairs)  10.4 us
    ppermute x2, starting transfers between devices, behind(): return lax.ppermute(value, 'x', [(i + 1, i) for i in range(3)])  6.53 us
  transfers between devices with their start and end apart: 38, of which 8 were waited for; matrix products, arithmetic and copies ran while one was open for 9% of the time, Pallas kernels for 15%

profile of v4, /device:TPU:15, one launch (start us, length us, event | category | flops | bytes accessed | tf_op | source)
XLA Modules:
  0.0 193.9 jit_solution(134208369444314670)
XLA Ops:
  2.5 2.1 %collective-permute-start.6 = (bf16[12,640]{1,0:T(8,128)(2,1)S(1)}, bf16[12,640]{1,0:T(8,128)(2,1)S(1)}, u32[]{:S(2)}, u32[]{:S(2)}) collective-permute-start(bf16[12,640]{1,0:T(8,128)(2,1)S(1)} %get-tuple-element.79), channel_id=1, source_target_pairs={{0,2},{1,3},{2,0},{3,1},{4,6},{5,7},{6,4},{7,5},{8,10},{9,11},{10,... | collective-permute-start | bytes 46088 | tf_op jit(solution)/shard_map/ppermute | solution.py:470
  4.6 7.7 %collective-permute-start.10 = (bf16[12,1536]{1,0:T(8,128)(2,1)}, bf16[12,1536]{1,0:T(8,128)(2,1)S(1)}, u32[]{:S(2)}, u32[]{:S(2)}) collective-permute-start(bf16[12,1536]{1,0:T(8,128)(2,1)} %param.18), channel_id=1, source_target_pairs={{0,0},{1,8},{2,16},{3,24},{4,4},{5,12},{6,20},{7,28},{8,32},{9,40}... | collective-permute-start | bytes 110600 | tf_op jit(solution)/shard_map/ppermute | solution.py:462
  18.6 2.2 %collective-permute-start.8 = (bf16[128,1536]{1,0:T(8,128)(2,1)}, bf16[128,1536]{1,0:T(8,128)(2,1)S(1)}, u32[]{:S(2)}, u32[]{:S(2)}) collective-permute-start(bf16[128,1536]{1,0:T(8,128)(2,1)} %bitcast.144), channel_id=1, source_target_pairs={{0,1},{1,0},{2,3},{3,2},{4,5},{5,4},{6,7},{7,6},{8,9},{9,8},{10,11... | collective-permute-start | bytes 1179656 | tf_op jit(solution)/shard_map/ppermute | solution.py:592
  20.9 2.3 %collective-permute-start.13 = (bf16[4,12,1024]{2,0,1:T(4,128)(2,1)S(1)}, bf16[4,12,1024]{2,0,1:T(4,128)(2,1)S(1)}, u32[]{:S(2)}, u32[]{:S(2)}) collective-permute-start(bf16[4,12,1024]{2,0,1:T(4,128)(2,1)S(1)} %get-tuple-element.67), channel_id=1, source_target_pairs={{0,8},{8,16},{16,24},{24,0},{1,9},{9,17},{17,25},{25,1},{2,10},{10... | collective-permute-start | bytes 294920 | tf_op jit(solution)/shard_map/ppermute | solution.py:470
  23.4 2.0 %collective-permute-start.11 = (bf16[4,12,1024]{2,0,1:T(4,128)(2,1)S(1)}, bf16[4,12,1024]{2,0,1:T(4,128)(2,1)S(1)}, u32[]{:S(2)}, u32[]{:S(2)}) collective-permute-start(bf16[4,12,1024]{2,0,1:T(4,128)(2,1)S(1)} %get-tuple-element.67), channel_id=1, source_target_pairs={{0,24},{8,0},{16,8},{24,16},{1,25},{9,1},{17,9},{25,17},{2,26},{10... | collective-permute-start | bytes 294920 | tf_op jit(solution)/shard_map/ppermute | solution.py:470
  32.6 2.5 %collective-permute-start.14 = (bf16[384,512]{1,0:T(8,128)(2,1)S(1)}, bf16[384,512]{1,0:T(8,128)(2,1)S(1)}, u32[]{:S(2)}, u32[]{:S(2)}) collective-permute-start(bf16[384,512]{1,0:T(8,128)(2,1)S(1)} %get-tuple-element.65), channel_id=1, source_target_pairs={{0,96},{32,0},{64,32},{96,64},{1,97},{33,1},{65,33},{97,65},{2,98}... | collective-permute-start | bytes 1179656 | tf_op jit(solution)/shard_map/ppermute | solution.py:470
  38.4 11.6 %front.1 = (f32[128,1536]{1,0:T(8,128)}, bf16[128,1536]{1,0:T(8,128)(2,1)}) custom-call(s32[2]{0:T(128)} %pad_add_fusion.ends, s32[256,64]{1,0:T(8,128)} %reshape.114.cells, bf16[256,1536]{1,0:T(8,128)(2,1)} %bitcast.140, bf16[8,1664]{1,0:T(8,128)(2,1)} %copy-done.12, bf16[8,1664]{1,0:T(8,128)(2,1)} %copy-done.13, f32[6,1536]{1,0:T(8,128)} %pad_maximum_fusion.6.table, ...), custom_call_target="tpu_custom_call" | custom-call | flops 3019898880 | bytes 26738688 | tf_op jit(solution)/shard_map/front/pallas_call | solution.py:130
  50.0 2.3 %collective-permute-done.14 = bf16[384,512]{1,0:T(8,128)(2,1)S(1)} collective-permute-done((bf16[384,512]{1,0:T(8,128)(2,1)S(1)}, bf16[384,512]{1,0:T(8,128)(2,1)S(1)}, u32[]{:S(2)}, u32[]{:S(2)}) %collective-permute-start.14) | collective-permute-done | bytes 393248 | tf_op jit(solution)/shard_map/ppermute | solution.py:470
  61.5 6.6 %collective-permute-done.2.norm1 = bf16[128,1536]{1,0:T(8,128)(2,1)S(1)} collective-permute-done((bf16[128,1536]{1,0:T(8,128)(2,1)}, bf16[128,1536]{1,0:T(8,128)(2,1)S(1)}, u32[]{:S(2)}, u32[]{:S(2)}) %collective-permute-start.2) | collective-permute-done | bytes 393248 | tf_op jit(solution)/shard_map/ppermute | solution.py:470
  68.1 9.3 %collective-permute-done.3.norm2 = bf16[128,1536]{1,0:T(8,128)(2,1)} collective-permute-done((bf16[128,1536]{1,0:T(8,128)(2,1)}, bf16[128,1536]{1,0:T(8,128)(2,1)}, u32[]{:S(2)}, u32[]{:S(2)}) %collective-permute-start.3) | collective-permute-done | bytes 393248 | tf_op jit(solution)/shard_map/ppermute | solution.py:470
  78.5 17.2 %attend.1 = (bf16[2,512,192]{2,1,0:T(8,128)(2,1)}, bf16[384,1536]{1,0:T(8,128)(2,1)}, f32[128,1536]{1,0:T(8,128)}, bf16[128,1536]{1,0:T(8,128)(2,1)}, bf16[128,1...) custom-call(s32[4]{0:T(128)} %pad_add_fusion.1.place, ...), custom_call_target="tpu_custom_call" | custom-call | flops 5234491392 | bytes 9437184 | tf_op jit(solution)/shard_map/attend/pallas_call | solution.py:390
  96.6 3.2 %collective-permute-done.19 = bf16[4,1536,128]{2,1,0:T(8,128)(2,1)S(1)} collective-permute-done((bf16[4,1536,128]{2,1,0:T(8,128)(2,1)}, bf16[4,1536,128]{2,1,0:T(8,128)(2,1)S(1)}, u32[]{:S(2)}, u32[]{:S(2)}) %collective-permute-start.19) | collective-permute-done | bytes 1572896 | tf_op jit(solution)/shard_map/ppermute | solution.py:462
  102.6 2.2 %collective-permute-start.22 = (bf16[1536,128]{1,0:T(8,128)(2,1)}, bf16[1536,128]{1,0:T(8,128)(2,1)}, u32[]{:S(2)}, u32[]{:S(2)}) collective-permute-start(bf16[1536,128]{1,0:T(8,128)(2,1)} %get-tuple-element.55), channel_id=1, source_target_pairs={{0,96},{32,0},{64,32},{96,64},{1,97},{33,1},{65,33},{97,65},{2,98}... | collective-permute-start | bytes 1179656 | tf_op jit(solution)/shard_map/ppermute | solution.py:470
  107.3 2.1 %collective-permute-start.23 = (bf16[128,1536]{1,0:T(8,128)(2,1)}, bf16[128,1536]{1,0:T(8,128)(2,1)S(1)}, u32[]{:S(2)}, u32[]{:S(2)}) collective-permute-start(bf16[128,1536]{1,0:T(8,128)(2,1)} %get-tuple-element.34), channel_id=1, source_target_pairs={{0,2},{1,3},{2,0},{3,1},{4,6},{5,7},{6,4},{7,5},{8,10},{9,11},{10,... | collective-permute-start | bytes 1179656 | tf_op jit(solution)/shard_map/ppermute | solution.py:470
  109.4 5.2 %mix.1 = bf16[4,128,1536]{2,1,0:T(8,128)(2,1)} custom-call(s32[4]{0:T(128)} %pad_add_fusion.1.place, bf16[2,512,192]{2,1,0:T(8,128)(2,1)} %get-tuple-element.27.heads, bf16[384,1536]{1,0:T(8,128)(2,1)} %get-tuple-element.28.w_out), custom_call_target="tpu_custom_call" | custom-call | flops 603979776 | bytes 2359296 | tf_op jit(solution)/shard_map/mix/pallas_call | solution.py:427
  116.7 8.7 %collective-permute-done.20 = bf16[1536,128]{1,0:T(8,128)(2,1)} collective-permute-done((bf16[1536,128]{1,0:T(8,128)(2,1)S(1)}, bf16[1536,128]{1,0:T(8,128)(2,1)}, u32[]{:S(2)}, u32[]{:S(2)}) %collective-permute-start.20) | collective-permute-done | bytes 393248 | tf_op jit(solution)/shard_map/ppermute | solution.py:470
  130.5 4.6 %collective-permute-start.29 = (bf16[16,1536]{1,0:T(8,128)(2,1)}, bf16[16,1536]{1,0:T(8,128)(2,1)}, u32[]{:S(2)}, u32[]{:S(2)}) collective-permute-start(bf16[16,1536]{1,0:T(8,128)(2,1)} %get-tuple-element.62), channel_id=1, source_target_pairs={{1,0},{2,1},{3,2},{5,4},{6,5},{7,6},{9,8},{10,9},{11,10},{13,12},{... | collective-permute-start | bytes 147464 | tf_op jit(solution)/shard_map/ppermute | solution.py:579
  144.1 2.6 %collective-permute-start.36 = (bf16[12,640]{1,0:T(8,128)(2,1)S(1)}, bf16[12,640]{1,0:T(8,128)(2,1)S(1)}, u32[]{:S(2)}, u32[]{:S(2)}) collective-permute-start(bf16[12,640]{1,0:T(8,128)(2,1)S(1)} %bitcast.178), channel_id=1, source_target_pairs={{0,3},{1,0},{2,1},{3,2},{4,67},{5,64},{6,65},{7,66},{8,7},{9,4},{1... | collective-permute-start | bytes 46088 | tf_op jit(solution)/shard_map/ppermute | solution.py:462
  146.7 12.8 %back.1 = bf16[256,1536]{1,0:T(8,128)(2,1)} custom-call(s32[256,64]{1,0:T(8,128)} %reshape.114.cells, bf16[256,1536]{1,0:T(8,128)(2,1)} %bitcast.141, f32[6,1536]{1,0:T(8,128)} %pad_maximum_fusion.6.table, bf16[128,1536]{1,0:T(8,128)(2,1)} %copy-done.3, bf16[16,1536]{1,0:T(8,128)(2,1)} %collective-permute-done.25.grad_prev, ...), custom_call_target="tpu_custom_call" | custom-call | flops 3019898880 | bytes 26738688 | tf_op jit(solution)/shard_map/back/pallas_call | solution.py:251
  159.5 12.4 %collective-permute-start.33 = (bf16[12,640]{1,0:T(8,128)(2,1)S(1)}, bf16[12,640]{1,0:T(8,128)(2,1)S(1)}, u32[]{:S(2)}, u32[]{:S(2)}) collective-permute-start(bf16[12,640]{1,0:T(8,128)(2,1)S(1)} %bitcast.179), channel_id=1, source_target_pairs={{0,0},{1,1},{2,2},{3,3},{4,64},{5,65},{6,66},{7,67},{8,4},{9,5},{1... | collective-permute-start | bytes 46088 | tf_op jit(solution)/shard_map/ppermute | solution.py:462
  173.8 4.9 %collective-permute-start.35 = (bf16[12,640]{1,0:T(8,128)(2,1)S(1)}, bf16[12,640]{1,0:T(8,128)(2,1)S(1)}, u32[]{:S(2)}, u32[]{:S(2)}) collective-permute-start(bf16[12,640]{1,0:T(8,128)(2,1)S(1)} %bitcast.176), channel_id=1, source_target_pairs={{0,2},{1,3},{2,0},{3,1},{4,66},{5,67},{6,64},{7,65},{8,6},{9,7},{1... | collective-permute-start | bytes 46088 | tf_op jit(solution)/shard_map/ppermute | solution.py:462
  178.8 3.6 %collective-permute-start.37 = (bf16[12,1536]{1,0:T(8,128)(2,1)S(1)}, bf16[12,1536]{1,0:T(8,128)(2,1)S(1)}, u32[]{:S(2)}, u32[]{:S(2)}) collective-permute-start(bf16[12,1536]{1,0:T(8,128)(2,1)S(1)} %bitcast.172), channel_id=1, source_target_pairs={{0,0},{1,32},{2,64},{3,96},{4,16},{5,48},{6,80},{7,112},{8,1},{9,3... | collective-permute-start | bytes 110600 | tf_op jit(solution)/shard_map/ppermute | solution.py:462
  183.3 7.1 %collective-permute-done.37 = bf16[12,1536]{1,0:T(8,128)(2,1)S(1)} collective-permute-done((bf16[12,1536]{1,0:T(8,128)(2,1)S(1)}, bf16[12,1536]{1,0:T(8,128)(2,1)S(1)}, u32[]{:S(2)}, u32[]{:S(2)}) %collective-permute-start.37) | collective-permute-done | bytes 36896 | tf_op jit(solution)/shard_map/ppermute | solution.py:462
  191.1 2.2 %fusion.3 = bf16[128,1536]{1,0:T(8,128)(2,1)} fusion(f32[128,1536]{1,0:T(8,128)S(1)} %copy-done, bf16[128,1536]{1,0:T(8,128)(2,1)} %collective-permute-done.28, bf16[128,1536]{1,0:T(8,128)(2,1)} %collective-permute-done.27, bf16[128,1536]{1,0:T(8,128)(2,1)} %collective-permute-done.26, bf16[4,128,1536]{2,1,0:T(8,128)(2,1)S(1)} %copy-done.1), kind=kLoop, calls=%fused_computation.7 | loop fusion | flops 1769472 | bytes 2752512 | tf_op jit(solution)/shard_map/convert_element_type | solution.py:636
  (202 shorter events, 55.0 us)
Async XLA Ops:
  2.2 15.8 %collective-permute-start.5 = (bf16[12,640]{1,0:T(8,128)(2,1)S(1)}, bf16[12,640]{1,0:T(8,128)(2,1)S(1)}, u32[]{:S(2)}, u32[]{:S(2)}) collective-permute-start(bf16[12,640]{1,0:T(8,128)(2,1)S(1)} %get-tuple-element.78), channel_id=1, source_target_pairs={{0,1},{1,2},{2,3},{3,0},{4,5},{5,6},{6,7},{7,4},{8,9},{9,10},{10,1... | collective-permute-start | bytes 46088 | tf_op jit(solution)/shard_map/ppermute | solution.py:470
  2.5 15.6 %collective-permute-start.6 = (bf16[12,640]{1,0:T(8,128)(2,1)S(1)}, bf16[12,640]{1,0:T(8,128)(2,1)S(1)}, u32[]{:S(2)}, u32[]{:S(2)}) collective-permute-start(bf16[12,640]{1,0:T(8,128)(2,1)S(1)} %get-tuple-element.79), channel_id=1, source_target_pairs={{0,2},{1,3},{2,0},{3,1},{4,6},{5,7},{6,4},{7,5},{8,10},{9,11},{10,... | collective-permute-start | bytes 46088 | tf_op jit(solution)/shard_map/ppermute | solution.py:470
  4.6 13.5 %collective-permute-start.7 = (bf16[12,640]{1,0:T(8,128)(2,1)S(1)}, bf16[12,640]{1,0:T(8,128)(2,1)S(1)}, u32[]{:S(2)}, u32[]{:S(2)}) collective-permute-start(bf16[12,640]{1,0:T(8,128)(2,1)S(1)} %get-tuple-element.76), channel_id=1, source_target_pairs={{0,3},{1,0},{2,1},{3,2},{4,7},{5,4},{6,5},{7,6},{8,11},{9,8},{10,9... | collective-permute-start | bytes 46088 | tf_op jit(solution)/shard_map/ppermute | solution.py:470
  4.6 16.2 %collective-permute-start.10 = (bf16[12,1536]{1,0:T(8,128)(2,1)}, bf16[12,1536]{1,0:T(8,128)(2,1)S(1)}, u32[]{:S(2)}, u32[]{:S(2)}) collective-permute-start(bf16[12,1536]{1,0:T(8,128)(2,1)} %param.18), channel_id=1, source_target_pairs={{0,0},{1,8},{2,16},{3,24},{4,4},{5,12},{6,20},{7,28},{8,32},{9,40}... | collective-permute-start | bytes 110600 | tf_op jit(solution)/shard_map/ppermute | solution.py:462
  15.1 17.5 %collective-permute-start = (bf16[8,1664]{1,0:T(8,128)(2,1)S(1)}, bf16[8,1664]{1,0:T(8,128)(2,1)S(1)}, u32[]{:S(2)}, u32[]{:S(2)}) collective-permute-start(bf16[8,1664]{1,0:T(8,128)(2,1)S(1)} %concatenate.40), channel_id=1, source_target_pairs={{0,1},{1,2},{2,3},{4,5},{5,6},{6,7},{8,9},{9,10},{10,11},{12,13},{... | collective-permute-start | bytes 79880 | tf_op jit(solution)/shard_map/ppermute | solution.py:576
  30.5 23.8 %collective-permute-start.9 = (bf16[2,128,1536]{2,1,0:T(8,128)(2,1)S(1)}, bf16[2,128,1536]{2,1,0:T(8,128)(2,1)}, u32[]{:S(2)}, u32[]{:S(2)}) collective-permute-start(bf16[2,128,1536]{2,1,0:T(8,128)(2,1)S(1)} %pad_maximum_fusion.1), channel_id=1, source_target_pairs={{0,3},{1,2},{2,1},{3,0},{4,7},{5,6},{6,5},{7,4},{8,11},{9,10},{10,... | collective-permute-start | bytes 2359304 | tf_op jit(solution)/shard_map/ppermute | solution.py:593
  32.0 17.9 %collective-permute-start.16 = (bf16[384,512]{1,0:T(8,128)(2,1)S(1)}, bf16[384,512]{1,0:T(8,128)(2,1)S(1)}, u32[]{:S(2)}, u32[]{:S(2)}) collective-permute-start(bf16[384,512]{1,0:T(8,128)(2,1)S(1)} %get-tuple-element.65), channel_id=1, source_target_pairs={{0,32},{32,64},{64,96},{96,0},{1,33},{33,65},{65,97},{97,1},{2,34}... | collective-permute-start | bytes 1179656 | tf_op jit(solution)/shard_map/ppermute | solution.py:470
  32.6 17.4 %collective-permute-start.15 = (bf16[384,512]{1,0:T(8,128)(2,1)S(1)}, bf16[384,512]{1,0:T(8,128)(2,1)S(1)}, u32[]{:S(2)}, u32[]{:S(2)}) collective-permute-start(bf16[384,512]{1,0:T(8,128)(2,1)S(1)} %get-tuple-element.65), channel_id=1, source_target_pairs={{0,64},{32,96},{64,0},{96,32},{1,65},{33,97},{65,1},{97,33},{2,66}... | collective-permute-start | bytes 1179656 | tf_op jit(solution)/shard_map/ppermute | solution.py:470
  32.6 19.7 %collective-permute-start.14 = (bf16[384,512]{1,0:T(8,128)(2,1)S(1)}, bf16[384,512]{1,0:T(8,128)(2,1)S(1)}, u32[]{:S(2)}, u32[]{:S(2)}) collective-permute-start(bf16[384,512]{1,0:T(8,128)(2,1)S(1)} %get-tuple-element.65), channel_id=1, source_target_pairs={{0,96},{32,0},{64,32},{96,64},{1,97},{33,1},{65,33},{97,65},{2,98}... | collective-permute-start | bytes 1179656 | tf_op jit(solution)/shard_map/ppermute | solution.py:470
  54.3 23.1 %collective-permute-start.17 = (bf16[4,384,512]{2,1,0:T(8,128)(2,1)S(1)}, bf16[4,384,512]{2,1,0:T(8,128)(2,1)S(1)}, u32[]{:S(2)}, u32[]{:S(2)}) collective-permute-start(bf16[4,384,512]{2,1,0:T(8,128)(2,1)S(1)} %pad_maximum_fusion.near), channel_id=1, source_target_pairs={{0,4},{1,5},{2,6},{3,7},{4,0},{5,1},{6,2},{7,3},{8,12},{9,13},{10,... | collective-permute-start | bytes 4718600 | tf_op jit(solution)/shard_map/ppermute | solution.py:462
  56.0 12.1 %collective-permute-start.2 = (bf16[128,1536]{1,0:T(8,128)(2,1)}, bf16[128,1536]{1,0:T(8,128)(2,1)S(1)}, u32[]{:S(2)}, u32[]{:S(2)}) collective-permute-start(bf16[128,1536]{1,0:T(8,128)(2,1)} %get-tuple-element.24.norm0), channel_id=1, source_target_pairs={{0,3},{1,0},{2,1},{3,2},{4,7},{5,4},{6,5},{7,6},{8,11},{9,8},{10,9... | collective-permute-start | bytes 1179656 | tf_op jit(solution)/shard_map/ppermute | solution.py:470
  57.7 19.7 %collective-permute-start.3 = (bf16[128,1536]{1,0:T(8,128)(2,1)}, bf16[128,1536]{1,0:T(8,128)(2,1)}, u32[]{:S(2)}, u32[]{:S(2)}) collective-permute-start(bf16[128,1536]{1,0:T(8,128)(2,1)} %get-tuple-element.24.norm0), channel_id=1, source_target_pairs={{0,2},{1,3},{2,0},{3,1},{4,6},{5,7},{6,4},{7,5},{8,10},{9,11},{10,... | collective-permute-start | bytes 1179656 | tf_op jit(solution)/shard_map/ppermute | solution.py:470
  59.4 17.9 %collective-permute-start.4 = (bf16[128,1536]{1,0:T(8,128)(2,1)}, bf16[128,1536]{1,0:T(8,128)(2,1)}, u32[]{:S(2)}, u32[]{:S(2)}) collective-permute-start(bf16[128,1536]{1,0:T(8,128)(2,1)} %get-tuple-element.24.norm0), channel_id=1, source_target_pairs={{0,1},{1,2},{2,3},{3,0},{4,5},{5,6},{6,7},{7,4},{8,9},{9,10},{10,1... | collective-permute-start | bytes 1179656 | tf_op jit(solution)/shard_map/ppermute | solution.py:470
  102.6 12.0 %collective-permute-start.22 = (bf16[1536,128]{1,0:T(8,128)(2,1)}, bf16[1536,128]{1,0:T(8,128)(2,1)}, u32[]{:S(2)}, u32[]{:S(2)}) collective-permute-start(bf16[1536,128]{1,0:T(8,128)(2,1)} %get-tuple-element.55), channel_id=1, source_target_pairs={{0,96},{32,0},{64,32},{96,64},{1,97},{33,1},{65,33},{97,65},{2,98}... | collective-permute-start | bytes 1179656 | tf_op jit(solution)/shard_map/ppermute | solution.py:470
  105.0 20.5 %collective-permute-start.20 = (bf16[1536,128]{1,0:T(8,128)(2,1)S(1)}, bf16[1536,128]{1,0:T(8,128)(2,1)}, u32[]{:S(2)}, u32[]{:S(2)}) collective-permute-start(bf16[1536,128]{1,0:T(8,128)(2,1)S(1)} %get-tuple-element.54), channel_id=1, source_target_pairs={{0,32},{32,64},{64,96},{96,0},{1,33},{33,65},{65,97},{97,1},{2,34}... | collective-permute-start | bytes 1179656 | tf_op jit(solution)/shard_map/ppermute | solution.py:470
  105.9 21.1 %collective-permute-start.24 = (bf16[128,1536]{1,0:T(8,128)(2,1)}, bf16[128,1536]{1,0:T(8,128)(2,1)S(1)}, u32[]{:S(2)}, u32[]{:S(2)}) collective-permute-start(bf16[128,1536]{1,0:T(8,128)(2,1)} %get-tuple-element.36), channel_id=1, source_target_pairs={{0,3},{1,0},{2,1},{3,2},{4,7},{5,4},{6,5},{7,6},{8,11},{9,8},{10,9... | collective-permute-start | bytes 1179656 | tf_op jit(solution)/shard_map/ppermute | solution.py:470
  107.3 19.6 %collective-permute-start.23 = (bf16[128,1536]{1,0:T(8,128)(2,1)}, bf16[128,1536]{1,0:T(8,128)(2,1)S(1)}, u32[]{:S(2)}, u32[]{:S(2)}) collective-permute-start(bf16[128,1536]{1,0:T(8,128)(2,1)} %get-tuple-element.34), channel_id=1, source_target_pairs={{0,2},{1,3},{2,0},{3,1},{4,6},{5,7},{6,4},{7,5},{8,10},{9,11},{10,... | collective-permute-start | bytes 1179656 | tf_op jit(solution)/shard_map/ppermute | solution.py:470
  114.6 12.3 %collective-permute-start.18 = (bf16[128,1536]{1,0:T(8,128)(2,1)}, bf16[128,1536]{1,0:T(8,128)(2,1)S(1)}, u32[]{:S(2)}, u32[]{:S(2)}) collective-permute-start(bf16[128,1536]{1,0:T(8,128)(2,1)} %get-tuple-element.30), channel_id=1, source_target_pairs={{0,1},{1,2},{2,3},{3,0},{4,5},{5,6},{6,7},{7,4},{8,9},{9,10},{10,1... | collective-permute-start | bytes 1179656 | tf_op jit(solution)/shard_map/ppermute | solution.py:470
  130.5 13.3 %collective-permute-start.29 = (bf16[16,1536]{1,0:T(8,128)(2,1)}, bf16[16,1536]{1,0:T(8,128)(2,1)}, u32[]{:S(2)}, u32[]{:S(2)}) collective-permute-start(bf16[16,1536]{1,0:T(8,128)(2,1)} %get-tuple-element.62), channel_id=1, source_target_pairs={{1,0},{2,1},{3,2},{5,4},{6,5},{7,6},{9,8},{10,9},{11,10},{13,12},{... | collective-permute-start | bytes 147464 | tf_op jit(solution)/shard_map/ppermute | solution.py:579
  140.2 50.9 %collective-permute-start.28 = (bf16[128,1536]{1,0:T(8,128)(2,1)}, bf16[128,1536]{1,0:T(8,128)(2,1)}, u32[]{:S(2)}, u32[]{:S(2)}) collective-permute-start(bf16[128,1536]{1,0:T(8,128)(2,1)} %get-tuple-element.52), channel_id=1, source_target_pairs={{0,3},{1,0},{2,1},{3,2},{4,7},{5,4},{6,5},{7,6},{8,11},{9,8},{10,9... | collective-permute-start | bytes 1179656 | tf_op jit(solution)/shard_map/ppermute | solution.py:470
  140.2 50.9 %collective-permute-start.27 = (bf16[128,1536]{1,0:T(8,128)(2,1)}, bf16[128,1536]{1,0:T(8,128)(2,1)}, u32[]{:S(2)}, u32[]{:S(2)}) collective-permute-start(bf16[128,1536]{1,0:T(8,128)(2,1)} %get-tuple-element.53), channel_id=1, source_target_pairs={{0,2},{1,3},{2,0},{3,1},{4,6},{5,7},{6,4},{7,5},{8,10},{9,11},{10,... | collective-permute-start | bytes 1179656 | tf_op jit(solution)/shard_map/ppermute | solution.py:470
  142.2 48.9 %collective-permute-start.26 = (bf16[128,1536]{1,0:T(8,128)(2,1)S(1)}, bf16[128,1536]{1,0:T(8,128)(2,1)}, u32[]{:S(2)}, u32[]{:S(2)}) collective-permute-start(bf16[128,1536]{1,0:T(8,128)(2,1)S(1)} %get-tuple-element.51), channel_id=1, source_target_pairs={{0,1},{1,2},{2,3},{3,0},{4,5},{5,6},{6,7},{7,4},{8,9},{9,10},{10,1... | collective-permute-start | bytes 1179656 | tf_op jit(solution)/shard_map/ppermute | solution.py:470
  144.1 27.9 %collective-permute-start.36 = (bf16[12,640]{1,0:T(8,128)(2,1)S(1)}, bf16[12,640]{1,0:T(8,128)(2,1)S(1)}, u32[]{:S(2)}, u32[]{:S(2)}) collective-permute-start(bf16[12,640]{1,0:T(8,128)(2,1)S(1)} %bitcast.178), channel_id=1, source_target_pairs={{0,3},{1,0},{2,1},{3,2},{4,67},{5,64},{6,65},{7,66},{8,7},{9,4},{1... | collective-permute-start | bytes 46088 | tf_op jit(solution)/shard_map/ppermute | solution.py:462
  159.5 14.3 %collective-permute-start.33 = (bf16[12,640]{1,0:T(8,128)(2,1)S(1)}, bf16[12,640]{1,0:T(8,128)(2,1)S(1)}, u32[]{:S(2)}, u32[]{:S(2)}) collective-permute-start(bf16[12,640]{1,0:T(8,128)(2,1)S(1)} %bitcast.179), channel_id=1, source_target_pairs={{0,0},{1,1},{2,2},{3,3},{4,64},{5,65},{6,66},{7,67},{8,4},{9,5},{1... | collective-permute-start | bytes 46088 | tf_op jit(solution)/shard_map/ppermute | solution.py:462
  (32 other events, 262.3 us)

commit v5 on v4

--- a/solution.py
+++ b/solution.py
@@ -273,51 +273,91 @@
     )(*small, weight)
 
 
+def prep_kernel(place, cot0, cot1, cot2, near, far, w_in, w_out, cot, d_heads):
+    seq, core, depth, level = place[0], place[1], place[2], place[3]
+    half = cot0.shape[0]
+    side = near.shape[2]
+    cols = w_in.shape[1]
+
+    def rows_of(index):
+        return pl.ds(pl.multiple_of(index * half, half), half)
+
+    for source, side_core in ((near, core), (far, 1 - core)):
+        for turn in range(4):
+            z = lax.rem(depth + turn, 4)
+            for other in range(4):
+                y = lax.rem(level + other, 4)
+                at = pl.ds(pl.multiple_of((z * 4 + y) * 96 + side_core * 48, 16), 48)
+                w_in[at, 0:side] = source[turn, other * 48 : (other + 1) * 48, :]
+                w_in[at, side:cols] = source[turn, 336:384, other * 128 : (other + 1) * 128]
+            at = pl.ds(pl.multiple_of(z * 96 + side_core * 48, 16), 48)
+            for b in range(3):
+                w_out[at, b * side : (b + 1) * side] = source[
+                    turn, 192 + b * 48 : 240 + b * 48, :
+                ]
+    beside = seq + 1 - 2 * lax.rem(seq, 2)
+    cot[rows_of(seq), :] = cot0[...]
+    cot[rows_of(beside), :] = cot1[...]
+    cot[rows_of(3 - seq), :] = cot2[0]
+    cot[rows_of(3 - beside), :] = cot2[1]
+    for head in range(d_heads.shape[0]):
+        d_heads[head] = rdot(cot[...], w_out[head * VD : (head + 1) * VD, :]).astype(BF16)
+
+
+def prep(place, cots, near, far):
+    half, width = cots[0].shape
+    rows = 4 * half
+    whole = lambda array: pl.BlockSpec(array.shape, lambda n, s: (0,) * array.ndim)
+    outs = [
+        jax.ShapeDtypeStruct((width, near.shape[2] + 128), BF16),
+        jax.ShapeDtypeStruct((2 * VD, width), BF16),
+        jax.ShapeDtypeStruct((rows, width), BF16),
+        jax.ShapeDtypeStruct((2, rows, VD), BF16),
+    ]
+    ins = (*cots, near, far)
+    return pl.pallas_call(
+        prep_kernel,
+        grid_spec=pltpu.PrefetchScalarGridSpec(
+            num_scalar_prefetch=1,
+            grid=(1,),
+            in_specs=[whole(a) for a in ins],
+            out_specs=[whole(a) for a in outs],
+        ),
+        out_shape=outs,
+        compiler_params=pltpu.CompilerParams(vmem_limit_bytes=VMEM_LIMIT),
+        cost_estimate=pl.CostEstimate(
+            flops=4 * rows * VD * width, bytes_accessed=10 * width * width, transcendentals=0
+        ),
+        name="prep",
+    )(place, *ins)
+
+
 def attend_kernel(
-    place, norm0, norm1, norm2, norm3, cot0, cot1, cot2, near, far,
-    heads, w_out, own, part1, part2, part3, near_sum, far_sum,
-    d_in, normed, cot, w_in, query_kv, acc, rows_in, rows_out,
+    place, norm0, norm1, norm2, norm3, w_in, cot, d_heads_all,
+    heads, own, part1, part2, part3, near_sum, far_sum,
+    d_in, normed, query_kv, acc, rows_in, rows_out,
 ):
     head = pl.program_id(0)
-    seq, core, depth, level = place[0], place[1], place[2], place[3]
+    seq, core, depth = place[0], place[1], place[2]
     inv = 1.0 / HD**0.5
     half = own.shape[0]
     cols = w_in.shape[1]
-    side = near.shape[2]
-    first = cols - side + HD
+    first = cols - 128 - HD - HD
 
     def rows_of(index):
         return pl.ds(pl.multiple_of(index * half, half), half)
 
     @pl.when(head == 0)
     def _():
-        for source, side_core in ((near, core), (far, 1 - core)):
-            for turn in range(4):
-                z = lax.rem(depth + turn, 4)
-                for other in range(4):
-                    y = lax.rem(level + other, 4)
-                    at = pl.ds(pl.multiple_of((z * 4 + y) * 96 + side_core * 48, 16), 48)
-                    w_in[at, 0:side] = source[turn, other * 48 : (other + 1) * 48, :]
-                    w_in[at, side:cols] = source[turn, 336:384, other * 128 : (other + 1) * 128]
-                at = pl.ds(pl.multiple_of(z * 96 + side_core * 48, 16), 48)
-                for b in range(3):
-                    w_out[at, b * side : (b + 1) * side] = source[
-                        turn, 192 + b * 48 : 240 + b * 48, :
-                    ]
         for piece, value in enumerate((norm0, norm1, norm2, norm3)):
             normed[rows_of(lax.rem(seq + piece, 4)), :] = value[...]
-        beside = seq + 1 - 2 * lax.rem(seq, 2)
-        cot[rows_of(seq), :] = cot0[...]
-        cot[rows_of(beside), :] = cot1[...]
-        cot[rows_of(3 - seq), :] = cot2[0]
-        cot[rows_of(3 - beside), :] = cot2[1]
         query_kv[...] = ndot(normed[...], w_in[...]).astype(BF16)
 
     keys = query_kv[:, first : first + HD]
     values = query_kv[:, first + HD : first + HD + VD]
     lanes = pl.ds(pl.multiple_of(head * HD, HD), HD)
     q = query_kv[:, lanes]
-    d_heads = rdot(cot[...], w_out[pl.ds(pl.multiple_of(head * VD, VD), VD), :]).astype(BF16)
+    d_heads = d_heads_all[head]
     scores = rdot(q, keys) * inv
     expo = jnp.exp(scores - jnp.max(scores, axis=1, keepdims=True))
     probs = expo * (1.0 / jnp.sum(expo, axis=1, keepdims=True))
@@ -369,24 +409,23 @@
                     ]
 
 
-def attend(place, norms, cots, near, far):
+def attend(place, norms, w_in, cot, d_heads):
     half, width = norms[0].shape
     rows = 4 * half
-    cols = near.shape[2] + 128
-    heads = 2
+    cols = w_in.shape[1]
+    heads = d_heads.shape[0]
     whole = lambda array: pl.BlockSpec(array.shape, lambda h, s: (0,) * array.ndim)
     length = cols // 128 * (width // 8) + width // 128 * (VD // 4)
     outs = (
         [
             jax.ShapeDtypeStruct((heads, rows, VD), BF16),
-            jax.ShapeDtypeStruct((heads * VD, width), BF16),
             jax.ShapeDtypeStruct((half, width), F32),
         ]
         + [jax.ShapeDtypeStruct((half, width), BF16)] * 3
         + [jax.ShapeDtypeStruct((4, length, 128), BF16)] * 2
     )
     specs = [whole(out) for out in outs]
-    ins = (*norms, *cots, near, far)
+    ins = (*norms, w_in, cot, d_heads)
     return pl.pallas_call(
         attend_kernel,
         grid_spec=pltpu.PrefetchScalarGridSpec(
@@ -397,8 +436,6 @@
             scratch_shapes=[
                 pltpu.VMEM((rows, cols), BF16),
                 pltpu.VMEM((rows, width), BF16),
-                pltpu.VMEM((rows, width), BF16),
-                pltpu.VMEM((width, cols), BF16),
                 pltpu.VMEM((rows, cols), BF16),
                 pltpu.VMEM((rows, HD + VD), F32),
                 pltpu.VMEM((width // 2, cols), BF16),
@@ -616,7 +653,9 @@
 
     spot = [seq, lax.axis_index("c"), lax.axis_index("z"), lax.axis_index("y")]
     spot = jnp.stack(spot).astype(jnp.int32)
-    heads, full_out, *d_parts, own, other = attend(spot, norms, (cot, beside, across), near, far)
+    w_in, full_out, cot_all, d_heads = prep(spot, (cot, beside, across), near, far)
+    norms = [after(norm, w_in) for norm in norms]
+    heads, *d_parts, own, other = attend(spot, norms, w_in, cot_all, d_heads)
     d_parts[1:] = [turned(d_parts[k], "x", k) for k in range(1, 4)]
     mine = (own.astype(F32) + flipped(other).astype(F32)).astype(BF16)
     total = mine[0].astype(F32)

time: 195 us -> 192 us (0.985); the launches traced: 194 us -> 189 us
  waiting for transfers between devices: 37.9 us -> 28.2 us
  Pallas kernels: 46.8 us -> 50.9 us
  starting transfers between devices: 78.2 us -> 75.1 us
    ppermute x24, waiting for transfers between devices: 27.5 us -> 19.2 us  [turned(): return lax.ppermute(value, axis, [(i, (i + by) % 4) for i in range(4)])]
    pallas_call x0 -> x1, Pallas kernels: none -> 5.65 us  [prep(): pl.pallas_call(prep_kernel, grid_spec=pltpu.PrefetchScalarGridSpec(num_sc...]
    ppermute x8, starting transfers between devices: 35.5 us -> 32.5 us  [moved(): return lax.ppermute(value, AXES, pairs)]
  transfers between devices with their start and end apart: 38 -> 38, of which waited for: 8 -> 8; matrix products, arithmetic and copies ran while one was open for 9% -> 11% of each run, Pallas kernels for 15% -> 19%
where the time goes in v5:
time: 192 us; the launch traced here: 189 us
  starting transfers between devices  75.1 us (39%)
  Pallas kernels  50.9 us (27%)
  waiting for transfers between devices  28.2 us (15%)
  other arithmetic  17.8 us (9%)
  local copies, waits for them, and re-layouts  15.2 us (8%)
    ppermute x8, starting transfers between devices, moved(): return lax.ppermute(value, AXES, pairs)  32.5 us
    ppermute x24, starting transfers between devices, turned(): return lax.ppermute(value, axis, [(i, (i + by) % 4) for i in range(4)])  29.5 us
    ppermute x24, waiting for transfers between devices, turned(): return lax.ppermute(value, axis, [(i, (i + by) % 4) for i in range(4)])  19.2 us
    pallas_call x1, Pallas kernels, attend(): pl.pallas_call(attend_kernel, grid_spec=pltpu.PrefetchScalarGridSpec(num_...  15.7 us
    pallas_call x1, Pallas kernels, back(): pl.pallas_call(back_kernel, grid=(1,), in_specs=[whole(a) for a in small]...  12.8 us
    pallas_call x1, Pallas kernels, front(): pl.pallas_call(front_kernel, grid_spec=pltpu.PrefetchScalarGridSpec(num_s...  11.6 us
    ppermute x8, waiting for transfers between devices, moved(): return lax.ppermute(value, AXES, pairs)  9.01 us
    ppermute x2, starting transfers between devices, behind(): return lax.ppermute(value, 'x', [(i + 1, i) for i in range(3)])  8.12 us
  transfers between devices with their start and end apart: 38, of which 8 were waited for; matrix products, arithmetic and copies ran while one was open for 11% of the time, Pallas kernels for 19%

profile of v5, /device:TPU:15, one launch (start us, length us, event | category | flops | bytes accessed | tf_op | source)
XLA Modules:
  0.0 188.7 jit_solution(7926046433753206830)
XLA Ops:
  4.6 7.7 %collective-permute-start.7 = (bf16[12,1536]{1,0:T(8,128)(2,1)}, bf16[12,1536]{1,0:T(8,128)(2,1)S(1)}, u32[]{:S(2)}, u32[]{:S(2)}) collective-permute-start(bf16[12,1536]{1,0:T(8,128)(2,1)} %param.18), channel_id=1, source_target_pairs={{0,0},{1,8},{2,16},{3,24},{4,4},{5,12},{6,20},{7,28},{8,32},{9,40}... | collective-permute-start | bytes 110600 | tf_op jit(solution)/shard_map/ppermute | solution.py:499
  18.6 2.2 %collective-permute-start.5 = (bf16[128,1536]{1,0:T(8,128)(2,1)}, bf16[128,1536]{1,0:T(8,128)(2,1)S(1)}, u32[]{:S(2)}, u32[]{:S(2)}) collective-permute-start(bf16[128,1536]{1,0:T(8,128)(2,1)} %bitcast.140), channel_id=1, source_target_pairs={{0,1},{1,0},{2,3},{3,2},{4,5},{5,4},{6,7},{7,6},{8,9},{9,8},{10,11... | collective-permute-start | bytes 1179656 | tf_op jit(solution)/shard_map/ppermute | solution.py:629
  20.9 2.3 %collective-permute-start.10 = (bf16[4,12,1024]{2,0,1:T(4,128)(2,1)S(1)}, bf16[4,12,1024]{2,0,1:T(4,128)(2,1)S(1)}, u32[]{:S(2)}, u32[]{:S(2)}) collective-permute-start(bf16[4,12,1024]{2,0,1:T(4,128)(2,1)S(1)} %get-tuple-element.81), channel_id=1, source_target_pairs={{0,8},{8,16},{16,24},{24,0},{1,9},{9,17},{17,25},{25,1},{2,10},{10... | collective-permute-start | bytes 294920 | tf_op jit(solution)/shard_map/ppermute | solution.py:507
  28.7 2.5 %collective-permute-start.1 = (bf16[8,1664]{1,0:T(8,128)(2,1)}, bf16[8,1664]{1,0:T(8,128)(2,1)}, u32[]{:S(2)}, u32[]{:S(2)}) collective-permute-start(bf16[8,1664]{1,0:T(8,128)(2,1)} %concatenate.41), channel_id=1, source_target_pairs={{1,0},{2,1},{3,2},{5,4},{6,5},{7,6},{9,8},{10,9},{11,10},{13,12},{... | collective-permute-start | bytes 79880 | tf_op jit(solution)/shard_map/ppermute | solution.py:616
  33.3 2.5 %collective-permute-start.11 = (bf16[384,512]{1,0:T(8,128)(2,1)S(1)}, bf16[384,512]{1,0:T(8,128)(2,1)S(1)}, u32[]{:S(2)}, u32[]{:S(2)}) collective-permute-start(bf16[384,512]{1,0:T(8,128)(2,1)S(1)} %get-tuple-element.79), channel_id=1, source_target_pairs={{0,96},{32,0},{64,32},{96,64},{1,97},{33,1},{65,33},{97,65},{2,98}... | collective-permute-start | bytes 1179656 | tf_op jit(solution)/shard_map/ppermute | solution.py:507
  37.0 2.3 %reduce.35 = s32[16384]{0:T(1024)} reduce(s32[1,16384]{1,0:T(1,128)} %param.10, s32[]{:T(128)} %broadcast.165), dimensions={0}, to_apply=%param.10.reduce_sub_computation.3 | reduce | bytes 131076 | tf_op args[0]
  40.8 11.6 %front.1 = (f32[128,1536]{1,0:T(8,128)}, bf16[128,1536]{1,0:T(8,128)(2,1)}) custom-call(s32[2]{0:T(128)} %pad_add_fusion.ends, s32[256,64]{1,0:T(8,128)} %reshape.114.cells, bf16[256,1536]{1,0:T(8,128)(2,1)} %bitcast.142, bf16[8,1664]{1,0:T(8,128)(2,1)} %collective-permute-done.edge_prev, bf16[8,1664]{1,0:T(8,128)(2,1)} %collective-permute-done.1.edge_next, ...), custom_call_target="tpu_custom_call" | custom-call | flops 3019898880 | bytes 26738688 | tf_op jit(solution)/shard_map/front/pallas_call | solution.py:130
  56.2 3.5 %collective-permute-start.14 = (bf16[4,384,512]{2,1,0:T(8,128)(2,1)S(1)}, bf16[4,384,512]{2,1,0:T(8,128)(2,1)S(1)}, u32[]{:S(2)}, u32[]{:S(2)}) collective-permute-start(bf16[4,384,512]{2,1,0:T(8,128)(2,1)S(1)} %pad_maximum_fusion.near), channel_id=1, source_target_pairs={{0,4},{1,5},{2,6},{3,7},{4,0},{5,1},{6,2},{7,3},{8,12},{9,13},{10,... | collective-permute-start | bytes 4718600 | tf_op jit(solution)/shard_map/ppermute | solution.py:499
  61.3 2.4 %collective-permute-start.16 = (bf16[128,1536]{1,0:T(8,128)(2,1)}, bf16[128,1536]{1,0:T(8,128)(2,1)}, u32[]{:S(2)}, u32[]{:S(2)}) collective-permute-start(bf16[128,1536]{1,0:T(8,128)(2,1)} %get-tuple-element.35.norm0), channel_id=1, source_target_pairs={{0,2},{1,3},{2,0},{3,1},{4,6},{5,7},{6,4},{7,5},{8,10},{9,11},{10,... | collective-permute-start | bytes 1179656 | tf_op jit(solution)/shard_map/ppermute | solution.py:507
  66.8 5.6 %prep.1 = (bf16[1536,640]{1,0:T(8,128)(2,1)}, bf16[384,1536]{1,0:T(8,128)(2,1)}, bf16[512,1536]{1,0:T(8,128)(2,1)}, bf16[2,512,192]{2,1,0:T(8,128)(2,1)}) custom-call(s32[4]{0:T(128)} %pad_add_fusion.1.place, bf16[128,1536]{1,0:T(8,128)(2,1)} %bitcast.141, bf16[128,1536]{1,0:T(8,128)(2,1)} %copy-done.8, bf16[2,128,1536]{2,1,0:T(8,128)(2,1)} %copy-done.10, ...), custom_call_target="tpu_custom_call" | custom-call | flops 603979776 | bytes 23592960 | tf_op jit(solution)/shard_map/prep/pallas_call | solution.py:318
  72.5 9.2 %collective-permute-done.16.norm2 = bf16[128,1536]{1,0:T(8,128)(2,1)} collective-permute-done((bf16[128,1536]{1,0:T(8,128)(2,1)}, bf16[128,1536]{1,0:T(8,128)(2,1)}, u32[]{:S(2)}, u32[]{:S(2)}) %collective-permute-start.16) | collective-permute-done | bytes 393248 | tf_op jit(solution)/shard_map/ppermute | solution.py:507
  81.7 15.7 %attend.1 = (bf16[2,512,192]{2,1,0:T(8,128)(2,1)}, f32[128,1536]{1,0:T(8,128)}, bf16[128,1536]{1,0:T(8,128)(2,1)}, bf16[128,1536]{1,0:T(8,128)(2,1)}, bf16[128,1...) custom-call(s32[4]{0:T(128)} %pad_add_fusion.1.place, ...), custom_call_target="tpu_custom_call" | custom-call | flops 5234491392 | bytes 9437184 | tf_op jit(solution)/shard_map/attend/pallas_call | solution.py:429
  98.2 3.2 %collective-permute-done.19 = bf16[4,1536,128]{2,1,0:T(8,128)(2,1)S(1)} collective-permute-done((bf16[4,1536,128]{2,1,0:T(8,128)(2,1)}, bf16[4,1536,128]{2,1,0:T(8,128)(2,1)S(1)}, u32[]{:S(2)}, u32[]{:S(2)}) %collective-permute-start.19) | collective-permute-done | bytes 1572896 | tf_op jit(solution)/shard_map/ppermute | solution.py:499
  110.4 5.2 %mix.1 = bf16[4,128,1536]{2,1,0:T(8,128)(2,1)} custom-call(s32[4]{0:T(128)} %pad_add_fusion.1.place, bf16[2,512,192]{2,1,0:T(8,128)(2,1)} %get-tuple-element.41.heads, bf16[384,1536]{1,0:T(8,128)(2,1)} %get-tuple-element.42.w_out), custom_call_target="tpu_custom_call" | custom-call | flops 603979776 | bytes 2359296 | tf_op jit(solution)/shard_map/mix/pallas_call | solution.py:464
  117.7 8.9 %collective-permute-done.20 = bf16[1536,128]{1,0:T(8,128)(2,1)} collective-permute-done((bf16[1536,128]{1,0:T(8,128)(2,1)S(1)}, bf16[1536,128]{1,0:T(8,128)(2,1)}, u32[]{:S(2)}, u32[]{:S(2)}) %collective-permute-start.20) | collective-permute-done | bytes 393248 | tf_op jit(solution)/shard_map/ppermute | solution.py:507
  131.5 5.6 %collective-permute-start.29 = (bf16[16,1536]{1,0:T(8,128)(2,1)}, bf16[16,1536]{1,0:T(8,128)(2,1)}, u32[]{:S(2)}, u32[]{:S(2)}) collective-permute-start(bf16[16,1536]{1,0:T(8,128)(2,1)} %get-tuple-element.76), channel_id=1, source_target_pairs={{1,0},{2,1},{3,2},{5,4},{6,5},{7,6},{9,8},{10,9},{11,10},{13,12},{... | collective-permute-start | bytes 147464 | tf_op jit(solution)/shard_map/ppermute | solution.py:616
  145.1 3.1 %collective-permute-start.36 = (bf16[12,640]{1,0:T(8,128)(2,1)S(1)}, bf16[12,640]{1,0:T(8,128)(2,1)S(1)}, u32[]{:S(2)}, u32[]{:S(2)}) collective-permute-start(bf16[12,640]{1,0:T(8,128)(2,1)S(1)} %bitcast.178), channel_id=1, source_target_pairs={{0,3},{1,0},{2,1},{3,2},{4,67},{5,64},{6,65},{7,66},{8,7},{9,4},{1... | collective-permute-start | bytes 46088 | tf_op jit(solution)/shard_map/ppermute | solution.py:499
  148.1 12.8 %back.1 = bf16[256,1536]{1,0:T(8,128)(2,1)} custom-call(s32[256,64]{1,0:T(8,128)} %reshape.114.cells, bf16[256,1536]{1,0:T(8,128)(2,1)} %bitcast.143, f32[6,1536]{1,0:T(8,128)} %pad_maximum_fusion.6.table, bf16[128,1536]{1,0:T(8,128)(2,1)} %copy-done.6, bf16[16,1536]{1,0:T(8,128)(2,1)} %collective-permute-done.25.grad_prev, ...), custom_call_target="tpu_custom_call" | custom-call | flops 3019898880 | bytes 26738688 | tf_op jit(solution)/shard_map/back/pallas_call | solution.py:251
  161.0 5.8 %collective-permute-start.33 = (bf16[12,640]{1,0:T(8,128)(2,1)S(1)}, bf16[12,640]{1,0:T(8,128)(2,1)S(1)}, u32[]{:S(2)}, u32[]{:S(2)}) collective-permute-start(bf16[12,640]{1,0:T(8,128)(2,1)S(1)} %bitcast.179), channel_id=1, source_target_pairs={{0,0},{1,1},{2,2},{3,3},{4,64},{5,65},{6,66},{7,67},{8,4},{9,5},{1... | collective-permute-start | bytes 46088 | tf_op jit(solution)/shard_map/ppermute | solution.py:499
  166.9 4.5 %collective-permute-start.34 = (bf16[12,640]{1,0:T(8,128)(2,1)S(1)}, bf16[12,640]{1,0:T(8,128)(2,1)S(1)}, u32[]{:S(2)}, u32[]{:S(2)}) collective-permute-start(bf16[12,640]{1,0:T(8,128)(2,1)S(1)} %bitcast.177), channel_id=1, source_target_pairs={{0,1},{1,2},{2,3},{3,0},{4,65},{5,66},{6,67},{7,64},{8,5},{9,6},{1... | collective-permute-start | bytes 46088 | tf_op jit(solution)/shard_map/ppermute | solution.py:499
  171.4 2.6 %collective-permute-start.35 = (bf16[12,640]{1,0:T(8,128)(2,1)S(1)}, bf16[12,640]{1,0:T(8,128)(2,1)S(1)}, u32[]{:S(2)}, u32[]{:S(2)}) collective-permute-start(bf16[12,640]{1,0:T(8,128)(2,1)S(1)} %bitcast.176), channel_id=1, source_target_pairs={{0,2},{1,3},{2,0},{3,1},{4,66},{5,67},{6,64},{7,65},{8,6},{9,7},{1... | collective-permute-start | bytes 46088 | tf_op jit(solution)/shard_map/ppermute | solution.py:499
  174.1 4.5 %collective-permute-start.37 = (bf16[12,1536]{1,0:T(8,128)(2,1)S(1)}, bf16[12,1536]{1,0:T(8,128)(2,1)S(1)}, u32[]{:S(2)}, u32[]{:S(2)}) collective-permute-start(bf16[12,1536]{1,0:T(8,128)(2,1)S(1)} %bitcast.172), channel_id=1, source_target_pairs={{0,0},{1,32},{2,64},{3,96},{4,16},{5,48},{6,80},{7,112},{8,1},{9,3... | collective-permute-start | bytes 110600 | tf_op jit(solution)/shard_map/ppermute | solution.py:499
  179.5 5.7 %collective-permute-done.37 = bf16[12,1536]{1,0:T(8,128)(2,1)S(1)} collective-permute-done((bf16[12,1536]{1,0:T(8,128)(2,1)S(1)}, bf16[12,1536]{1,0:T(8,128)(2,1)S(1)}, u32[]{:S(2)}, u32[]{:S(2)}) %collective-permute-start.37) | collective-permute-done | bytes 36896 | tf_op jit(solution)/shard_map/ppermute | solution.py:499
  185.9 2.2 %fusion.3 = bf16[128,1536]{1,0:T(8,128)(2,1)} fusion(f32[128,1536]{1,0:T(8,128)S(1)} %copy-done, bf16[128,1536]{1,0:T(8,128)(2,1)} %collective-permute-done.28, bf16[128,1536]{1,0:T(8,128)(2,1)} %collective-permute-done.27, bf16[128,1536]{1,0:T(8,128)(2,1)} %collective-permute-done.26, bf16[4,128,1536]{2,1,0:T(8,128)(2,1)S(1)} %copy-done.2), kind=kLoop, calls=%fused_computation.7 | loop fusion | flops 1769472 | bytes 2752512 | tf_op jit(solution)/shard_map/convert_element_type | solution.py:675
  (203 shorter events, 55.7 us)
Async XLA Ops:
  2.2 15.8 %collective-permute-start.2 = (bf16[12,640]{1,0:T(8,128)(2,1)S(1)}, bf16[12,640]{1,0:T(8,128)(2,1)S(1)}, u32[]{:S(2)}, u32[]{:S(2)}) collective-permute-start(bf16[12,640]{1,0:T(8,128)(2,1)S(1)} %get-tuple-element.92), channel_id=1, source_target_pairs={{0,1},{1,2},{2,3},{3,0},{4,5},{5,6},{6,7},{7,4},{8,9},{9,10},{10,1... | collective-permute-start | bytes 46088 | tf_op jit(solution)/shard_map/ppermute | solution.py:507
  2.5 15.6 %collective-permute-start.3 = (bf16[12,640]{1,0:T(8,128)(2,1)S(1)}, bf16[12,640]{1,0:T(8,128)(2,1)S(1)}, u32[]{:S(2)}, u32[]{:S(2)}) collective-permute-start(bf16[12,640]{1,0:T(8,128)(2,1)S(1)} %get-tuple-element.93), channel_id=1, source_target_pairs={{0,2},{1,3},{2,0},{3,1},{4,6},{5,7},{6,4},{7,5},{8,10},{9,11},{10,... | collective-permute-start | bytes 46088 | tf_op jit(solution)/shard_map/ppermute | solution.py:507
  4.6 13.5 %collective-permute-start.4 = (bf16[12,640]{1,0:T(8,128)(2,1)S(1)}, bf16[12,640]{1,0:T(8,128)(2,1)S(1)}, u32[]{:S(2)}, u32[]{:S(2)}) collective-permute-start(bf16[12,640]{1,0:T(8,128)(2,1)S(1)} %get-tuple-element.90), channel_id=1, source_target_pairs={{0,3},{1,0},{2,1},{3,2},{4,7},{5,4},{6,5},{7,6},{8,11},{9,8},{10,9... | collective-permute-start | bytes 46088 | tf_op jit(solution)/shard_map/ppermute | solution.py:507
  4.6 16.2 %collective-permute-start.7 = (bf16[12,1536]{1,0:T(8,128)(2,1)}, bf16[12,1536]{1,0:T(8,128)(2,1)S(1)}, u32[]{:S(2)}, u32[]{:S(2)}) collective-permute-start(bf16[12,1536]{1,0:T(8,128)(2,1)} %param.18), channel_id=1, source_target_pairs={{0,0},{1,8},{2,16},{3,24},{4,4},{5,12},{6,20},{7,28},{8,32},{9,40}... | collective-permute-start | bytes 110600 | tf_op jit(solution)/shard_map/ppermute | solution.py:499
  15.1 18.3 %collective-permute-start = (bf16[8,1664]{1,0:T(8,128)(2,1)S(1)}, bf16[8,1664]{1,0:T(8,128)(2,1)}, u32[]{:S(2)}, u32[]{:S(2)}) collective-permute-start(bf16[8,1664]{1,0:T(8,128)(2,1)S(1)} %concatenate.40), channel_id=1, source_target_pairs={{0,1},{1,2},{2,3},{4,5},{5,6},{6,7},{8,9},{9,10},{10,11},{12,13},{... | collective-permute-start | bytes 79880 | tf_op jit(solution)/shard_map/ppermute | solution.py:613
  18.6 13.0 %collective-permute-start.5 = (bf16[128,1536]{1,0:T(8,128)(2,1)}, bf16[128,1536]{1,0:T(8,128)(2,1)S(1)}, u32[]{:S(2)}, u32[]{:S(2)}) collective-permute-start(bf16[128,1536]{1,0:T(8,128)(2,1)} %bitcast.140), channel_id=1, source_target_pairs={{0,1},{1,0},{2,3},{3,2},{4,5},{5,4},{6,7},{7,6},{8,9},{9,8},{10,11... | collective-permute-start | bytes 1179656 | tf_op jit(solution)/shard_map/ppermute | solution.py:629
  28.7 12.2 %collective-permute-start.1 = (bf16[8,1664]{1,0:T(8,128)(2,1)}, bf16[8,1664]{1,0:T(8,128)(2,1)}, u32[]{:S(2)}, u32[]{:S(2)}) collective-permute-start(bf16[8,1664]{1,0:T(8,128)(2,1)} %concatenate.41), channel_id=1, source_target_pairs={{1,0},{2,1},{3,2},{5,4},{6,5},{7,6},{9,8},{10,9},{11,10},{13,12},{... | collective-permute-start | bytes 79880 | tf_op jit(solution)/shard_map/ppermute | solution.py:616
  31.7 23.5 %collective-permute-start.6 = (bf16[2,128,1536]{2,1,0:T(8,128)(2,1)S(1)}, bf16[2,128,1536]{2,1,0:T(8,128)(2,1)S(1)}, u32[]{:S(2)}, u32[]{:S(2)}) collective-permute-start(bf16[2,128,1536]{2,1,0:T(8,128)(2,1)S(1)} %pad_maximum_fusion.1), channel_id=1, source_target_pairs={{0,3},{1,2},{2,1},{3,0},{4,7},{5,6},{6,5},{7,4},{8,11},{9,10},{10,... | collective-permute-start | bytes 2359304 | tf_op jit(solution)/shard_map/ppermute | solution.py:630
  32.7 19.8 %collective-permute-start.13 = (bf16[384,512]{1,0:T(8,128)(2,1)S(1)}, bf16[384,512]{1,0:T(8,128)(2,1)S(1)}, u32[]{:S(2)}, u32[]{:S(2)}) collective-permute-start(bf16[384,512]{1,0:T(8,128)(2,1)S(1)} %get-tuple-element.79), channel_id=1, source_target_pairs={{0,32},{32,64},{64,96},{96,0},{1,33},{33,65},{65,97},{97,1},{2,34}... | collective-permute-start | bytes 1179656 | tf_op jit(solution)/shard_map/ppermute | solution.py:507
  33.3 19.1 %collective-permute-start.12 = (bf16[384,512]{1,0:T(8,128)(2,1)S(1)}, bf16[384,512]{1,0:T(8,128)(2,1)S(1)}, u32[]{:S(2)}, u32[]{:S(2)}) collective-permute-start(bf16[384,512]{1,0:T(8,128)(2,1)S(1)} %get-tuple-element.79), channel_id=1, source_target_pairs={{0,64},{32,96},{64,0},{96,32},{1,65},{33,97},{65,1},{97,33},{2,66}... | collective-permute-start | bytes 1179656 | tf_op jit(solution)/shard_map/ppermute | solution.py:507
  33.3 19.6 %collective-permute-start.11 = (bf16[384,512]{1,0:T(8,128)(2,1)S(1)}, bf16[384,512]{1,0:T(8,128)(2,1)S(1)}, u32[]{:S(2)}, u32[]{:S(2)}) collective-permute-start(bf16[384,512]{1,0:T(8,128)(2,1)S(1)} %get-tuple-element.79), channel_id=1, source_target_pairs={{0,96},{32,0},{64,32},{96,64},{1,97},{33,1},{65,33},{97,65},{2,98}... | collective-permute-start | bytes 1179656 | tf_op jit(solution)/shard_map/ppermute | solution.py:507
  59.7 12.8 %collective-permute-start.15 = (bf16[128,1536]{1,0:T(8,128)(2,1)}, bf16[128,1536]{1,0:T(8,128)(2,1)S(1)}, u32[]{:S(2)}, u32[]{:S(2)}) collective-permute-start(bf16[128,1536]{1,0:T(8,128)(2,1)} %get-tuple-element.35.norm0), channel_id=1, source_target_pairs={{0,3},{1,0},{2,1},{3,2},{4,7},{5,4},{6,5},{7,6},{8,11},{9,8},{10,9... | collective-permute-start | bytes 1179656 | tf_op jit(solution)/shard_map/ppermute | solution.py:507
  61.3 20.4 %collective-permute-start.16 = (bf16[128,1536]{1,0:T(8,128)(2,1)}, bf16[128,1536]{1,0:T(8,128)(2,1)}, u32[]{:S(2)}, u32[]{:S(2)}) collective-permute-start(bf16[128,1536]{1,0:T(8,128)(2,1)} %get-tuple-element.35.norm0), channel_id=1, source_target_pairs={{0,2},{1,3},{2,0},{3,1},{4,6},{5,7},{6,4},{7,5},{8,10},{9,11},{10,... | collective-permute-start | bytes 1179656 | tf_op jit(solution)/shard_map/ppermute | solution.py:507
  63.7 18.0 %collective-permute-start.17 = (bf16[128,1536]{1,0:T(8,128)(2,1)}, bf16[128,1536]{1,0:T(8,128)(2,1)}, u32[]{:S(2)}, u32[]{:S(2)}) collective-permute-start(bf16[128,1536]{1,0:T(8,128)(2,1)} %get-tuple-element.35.norm0), channel_id=1, source_target_pairs={{0,1},{1,2},{2,3},{3,0},{4,5},{5,6},{6,7},{7,4},{8,9},{9,10},{10,1... | collective-permute-start | bytes 1179656 | tf_op jit(solution)/shard_map/ppermute | solution.py:507
  105.2 12.4 %collective-permute-start.21 = (bf16[1536,128]{1,0:T(8,128)(2,1)}, bf16[1536,128]{1,0:T(8,128)(2,1)}, u32[]{:S(2)}, u32[]{:S(2)}) collective-permute-start(bf16[1536,128]{1,0:T(8,128)(2,1)} %get-tuple-element.70), channel_id=1, source_target_pairs={{0,64},{32,96},{64,0},{96,32},{1,65},{33,97},{65,1},{97,33},{2,66}... | collective-permute-start | bytes 1179656 | tf_op jit(solution)/shard_map/ppermute | solution.py:507
  106.5 20.1 %collective-permute-start.20 = (bf16[1536,128]{1,0:T(8,128)(2,1)S(1)}, bf16[1536,128]{1,0:T(8,128)(2,1)}, u32[]{:S(2)}, u32[]{:S(2)}) collective-permute-start(bf16[1536,128]{1,0:T(8,128)(2,1)S(1)} %get-tuple-element.68), channel_id=1, source_target_pairs={{0,32},{32,64},{64,96},{96,0},{1,33},{33,65},{65,97},{97,1},{2,34}... | collective-permute-start | bytes 1179656 | tf_op jit(solution)/shard_map/ppermute | solution.py:507
  107.3 20.7 %collective-permute-start.24 = (bf16[128,1536]{1,0:T(8,128)(2,1)}, bf16[128,1536]{1,0:T(8,128)(2,1)S(1)}, u32[]{:S(2)}, u32[]{:S(2)}) collective-permute-start(bf16[128,1536]{1,0:T(8,128)(2,1)} %get-tuple-element.50), channel_id=1, source_target_pairs={{0,3},{1,0},{2,1},{3,2},{4,7},{5,4},{6,5},{7,6},{8,11},{9,8},{10,9... | collective-permute-start | bytes 1179656 | tf_op jit(solution)/shard_map/ppermute | solution.py:507
  108.3 19.7 %collective-permute-start.23 = (bf16[128,1536]{1,0:T(8,128)(2,1)}, bf16[128,1536]{1,0:T(8,128)(2,1)S(1)}, u32[]{:S(2)}, u32[]{:S(2)}) collective-permute-start(bf16[128,1536]{1,0:T(8,128)(2,1)} %get-tuple-element.48), channel_id=1, source_target_pairs={{0,2},{1,3},{2,0},{3,1},{4,6},{5,7},{6,4},{7,5},{8,10},{9,11},{10,... | collective-permute-start | bytes 1179656 | tf_op jit(solution)/shard_map/ppermute | solution.py:507
  115.6 12.4 %collective-permute-start.18 = (bf16[128,1536]{1,0:T(8,128)(2,1)}, bf16[128,1536]{1,0:T(8,128)(2,1)S(1)}, u32[]{:S(2)}, u32[]{:S(2)}) collective-permute-start(bf16[128,1536]{1,0:T(8,128)(2,1)} %get-tuple-element.44), channel_id=1, source_target_pairs={{0,1},{1,2},{2,3},{3,0},{4,5},{5,6},{6,7},{7,4},{8,9},{9,10},{10,1... | collective-permute-start | bytes 1179656 | tf_op jit(solution)/shard_map/ppermute | solution.py:507
  131.5 13.3 %collective-permute-start.29 = (bf16[16,1536]{1,0:T(8,128)(2,1)}, bf16[16,1536]{1,0:T(8,128)(2,1)}, u32[]{:S(2)}, u32[]{:S(2)}) collective-permute-start(bf16[16,1536]{1,0:T(8,128)(2,1)} %get-tuple-element.76), channel_id=1, source_target_pairs={{1,0},{2,1},{3,2},{5,4},{6,5},{7,6},{9,8},{10,9},{11,10},{13,12},{... | collective-permute-start | bytes 147464 | tf_op jit(solution)/shard_map/ppermute | solution.py:616
  140.1 45.8 %collective-permute-start.28 = (bf16[128,1536]{1,0:T(8,128)(2,1)}, bf16[128,1536]{1,0:T(8,128)(2,1)}, u32[]{:S(2)}, u32[]{:S(2)}) collective-permute-start(bf16[128,1536]{1,0:T(8,128)(2,1)} %get-tuple-element.66), channel_id=1, source_target_pairs={{0,3},{1,0},{2,1},{3,2},{4,7},{5,4},{6,5},{7,6},{8,11},{9,8},{10,9... | collective-permute-start | bytes 1179656 | tf_op jit(solution)/shard_map/ppermute | solution.py:507
  141.1 44.8 %collective-permute-start.27 = (bf16[128,1536]{1,0:T(8,128)(2,1)}, bf16[128,1536]{1,0:T(8,128)(2,1)}, u32[]{:S(2)}, u32[]{:S(2)}) collective-permute-start(bf16[128,1536]{1,0:T(8,128)(2,1)} %get-tuple-element.67), channel_id=1, source_target_pairs={{0,2},{1,3},{2,0},{3,1},{4,6},{5,7},{6,4},{7,5},{8,10},{9,11},{10,... | collective-permute-start | bytes 1179656 | tf_op jit(solution)/shard_map/ppermute | solution.py:507
  142.8 43.1 %collective-permute-start.26 = (bf16[128,1536]{1,0:T(8,128)(2,1)S(1)}, bf16[128,1536]{1,0:T(8,128)(2,1)}, u32[]{:S(2)}, u32[]{:S(2)}) collective-permute-start(bf16[128,1536]{1,0:T(8,128)(2,1)S(1)} %get-tuple-element.65), channel_id=1, source_target_pairs={{0,1},{1,2},{2,3},{3,0},{4,5},{5,6},{6,7},{7,4},{8,9},{9,10},{10,1... | collective-permute-start | bytes 1179656 | tf_op jit(solution)/shard_map/ppermute | solution.py:507
  145.1 21.8 %collective-permute-start.36 = (bf16[12,640]{1,0:T(8,128)(2,1)S(1)}, bf16[12,640]{1,0:T(8,128)(2,1)S(1)}, u32[]{:S(2)}, u32[]{:S(2)}) collective-permute-start(bf16[12,640]{1,0:T(8,128)(2,1)S(1)} %bitcast.178), channel_id=1, source_target_pairs={{0,3},{1,0},{2,1},{3,2},{4,67},{5,64},{6,65},{7,66},{8,7},{9,4},{1... | collective-permute-start | bytes 46088 | tf_op jit(solution)/shard_map/ppermute | solution.py:499
  (32 other events, 240.2 us)

commit v6 on v5

--- a/solution.py
+++ b/solution.py
@@ -626,6 +626,7 @@
     edge_next = behind(edge(bases[0, :span], skip[:8]))
     w_rows = gather_in_x(w_query, w_kv)
     out_home = moved(w_out, lambda z, y, c, x: (y, x, c, z))
+    w_rows = after(w_rows, cells)
     beside = lax.ppermute(after(cot, w_rows), "x", [(i, i ^ 1) for i in range(4)])
     across = lax.ppermute(jnp.stack([cot, beside]), "x", [(i, 3 - i) for i in range(4)])
     side = width // 3

time: 192 us -> 195 us (1.016); the launches traced: 189 us -> 195 us
  waiting for transfers between devices: 28.2 us -> 33.4 us
  starting transfers between devices: 75.1 us -> 78.1 us
    ppermute x24, waiting for transfers between devices: 19.2 us -> 22.4 us  [turned(): return lax.ppermute(value, axis, [(i, (i + by) % 4) for i in range(4)])]
    ppermute x8, starting transfers between devices: 32.5 us -> 35.4 us  [moved(): return lax.ppermute(value, AXES, pairs)]
    ppermute x8, waiting for transfers between devices: 9.01 us -> 11 us  [moved(): return lax.ppermute(value, AXES, pairs)]
    unnamed x42 -> x46, local copies, waits for them, and re-layouts: 4.29 us -> 4.83 us
  transfers between devices with their start and end apart: 38 -> 38, of which waited for: 8 -> 7; matrix products, arithmetic and copies ran while one was open for 11% -> 9% of each run, Pallas kernels for 19% -> 18%
where the time goes in v6:
time: 195 us
  starting transfers between devices  78.1 us (40%)
  Pallas kernels  50.9 us (26%)
  waiting for transfers between devices  33.4 us (17%)
  other arithmetic  16.4 us (8%)
  local copies, waits for them, and re-layouts  14.3 us (7%)
    ppermute x8, starting transfers between devices, moved(): return lax.ppermute(value, AXES, pairs)  35.4 us
    ppermute x24, starting transfers between devices, turned(): return lax.ppermute(value, axis, [(i, (i + by) % 4) for i in range(4)])  30.6 us
    ppermute x24, waiting for transfers between devices, turned(): return lax.ppermute(value, axis, [(i, (i + by) % 4) for i in range(4)])  22.4 us
    pallas_call x1, Pallas kernels, attend(): pl.pallas_call(attend_kernel, grid_spec=pltpu.PrefetchScalarGridSpec(num_...  15.7 us
    pallas_call x1, Pallas kernels, back(): pl.pallas_call(back_kernel, grid=(1,), in_specs=[whole(a) for a in small]...  12.8 us
    pallas_call x1, Pallas kernels, front(): pl.pallas_call(front_kernel, grid_spec=pltpu.PrefetchScalarGridSpec(num_s...  11.6 us
    ppermute x8, waiting for transfers between devices, moved(): return lax.ppermute(value, AXES, pairs)  11 us
    ppermute x2, starting transfers between devices, behind(): return lax.ppermute(value, 'x', [(i + 1, i) for i in range(3)])  6.52 us
  transfers between devices with their start and end apart: 38, of which 7 were waited for; matrix products, arithmetic and copies ran while one was open for 9% of the time, Pallas kernels for 18%

profile of v6, /device:TPU:15, one launch (start us, length us, event | category | flops | bytes accessed | tf_op | source)
XLA Modules:
  0.0 194.6 jit_solution(1700648732463250562)
XLA Ops:
  2.5 2.1 %collective-permute-start.3 = (bf16[12,640]{1,0:T(8,128)(2,1)S(1)}, bf16[12,640]{1,0:T(8,128)(2,1)S(1)}, u32[]{:S(2)}, u32[]{:S(2)}) collective-permute-start(bf16[12,640]{1,0:T(8,128)(2,1)S(1)} %get-tuple-element.95), channel_id=1, source_target_pairs={{0,2},{1,3},{2,0},{3,1},{4,6},{5,7},{6,4},{7,5},{8,10},{9,11},{10,... | collective-permute-start | bytes 46088 | tf_op jit(solution)/shard_map/ppermute | solution.py:507
  4.6 7.7 %collective-permute-start.7 = (bf16[12,1536]{1,0:T(8,128)(2,1)}, bf16[12,1536]{1,0:T(8,128)(2,1)S(1)}, u32[]{:S(2)}, u32[]{:S(2)}) collective-permute-start(bf16[12,1536]{1,0:T(8,128)(2,1)} %param.18), channel_id=1, source_target_pairs={{0,0},{1,8},{2,16},{3,24},{4,4},{5,12},{6,20},{7,28},{8,32},{9,40}... | collective-permute-start | bytes 110600 | tf_op jit(solution)/shard_map/ppermute | solution.py:499
  21.5 2.2 %collective-permute-start.5 = (bf16[128,1536]{1,0:T(8,128)(2,1)}, bf16[128,1536]{1,0:T(8,128)(2,1)S(1)}, u32[]{:S(2)}, u32[]{:S(2)}) collective-permute-start(bf16[128,1536]{1,0:T(8,128)(2,1)} %bitcast.140), channel_id=1, source_target_pairs={{0,1},{1,0},{2,3},{3,2},{4,5},{5,4},{6,7},{7,6},{8,9},{9,8},{10,11... | collective-permute-start | bytes 1179656 | tf_op jit(solution)/shard_map/ppermute | solution.py:630
  23.8 2.3 %collective-permute-start.10 = (bf16[4,12,1024]{2,0,1:T(4,128)(2,1)S(1)}, bf16[4,12,1024]{2,0,1:T(4,128)(2,1)S(1)}, u32[]{:S(2)}, u32[]{:S(2)}) collective-permute-start(bf16[4,12,1024]{2,0,1:T(4,128)(2,1)S(1)} %get-tuple-element.83), channel_id=1, source_target_pairs={{0,8},{8,16},{16,24},{24,0},{1,9},{9,17},{17,25},{25,1},{2,10},{10... | collective-permute-start | bytes 294920 | tf_op jit(solution)/shard_map/ppermute | solution.py:507
  34.6 2.4 %collective-permute-start.11 = (bf16[384,512]{1,0:T(8,128)(2,1)S(1)}, bf16[384,512]{1,0:T(8,128)(2,1)S(1)}, u32[]{:S(2)}, u32[]{:S(2)}) collective-permute-start(bf16[384,512]{1,0:T(8,128)(2,1)S(1)} %get-tuple-element.81), channel_id=1, source_target_pairs={{0,96},{32,0},{64,32},{96,64},{1,97},{33,1},{65,33},{97,65},{2,98}... | collective-permute-start | bytes 1179656 | tf_op jit(solution)/shard_map/ppermute | solution.py:507
  38.3 11.6 %front.1 = (f32[128,1536]{1,0:T(8,128)}, bf16[128,1536]{1,0:T(8,128)(2,1)}) custom-call(s32[2]{0:T(128)} %pad_add_fusion.ends, s32[256,64]{1,0:T(8,128)} %reshape.114.cells, bf16[256,1536]{1,0:T(8,128)(2,1)} %bitcast.142, bf16[8,1664]{1,0:T(8,128)(2,1)} %copy-done.14, bf16[8,1664]{1,0:T(8,128)(2,1)} %copy-done.15, f32[6,1536]{1,0:T(8,128)} %pad_maximum_fusion.6.table, ...), custom_call_target="tpu_custom_call" | custom-call | flops 3019898880 | bytes 26738688 | tf_op jit(solution)/shard_map/front/pallas_call | solution.py:130
  49.9 4.2 %collective-permute-done.11 = bf16[384,512]{1,0:T(8,128)(2,1)S(1)} collective-permute-done((bf16[384,512]{1,0:T(8,128)(2,1)S(1)}, bf16[384,512]{1,0:T(8,128)(2,1)S(1)}, u32[]{:S(2)}, u32[]{:S(2)}) %collective-permute-start.11) | collective-permute-done | bytes 393248 | tf_op jit(solution)/shard_map/ppermute | solution.py:507
  57.1 2.0 %collective-permute-start.14 = (bf16[4,384,512]{2,1,0:T(8,128)(2,1)S(1)}, bf16[4,384,512]{2,1,0:T(8,128)(2,1)S(1)}, u32[]{:S(2)}, u32[]{:S(2)}) collective-permute-start(bf16[4,384,512]{2,1,0:T(8,128)(2,1)S(1)} %pad_maximum_fusion.near), channel_id=1, source_target_pairs={{0,4},{1,5},{2,6},{3,7},{4,0},{5,1},{6,2},{7,3},{8,12},{9,13},{10,... | collective-permute-start | bytes 4718600 | tf_op jit(solution)/shard_map/ppermute | solution.py:499
  65.6 5.6 %prep.1 = (bf16[1536,640]{1,0:T(8,128)(2,1)}, bf16[384,1536]{1,0:T(8,128)(2,1)}, bf16[512,1536]{1,0:T(8,128)(2,1)}, bf16[2,512,192]{2,1,0:T(8,128)(2,1)}) custom-call(s32[4]{0:T(128)} %pad_add_fusion.1.place, bf16[128,1536]{1,0:T(8,128)(2,1)} %bitcast.141, bf16[128,1536]{1,0:T(8,128)(2,1)} %copy-done.8, bf16[2,128,1536]{2,1,0:T(8,128)(2,1)} %copy-done.10, ...), custom_call_target="tpu_custom_call" | custom-call | flops 603979776 | bytes 23592960 | tf_op jit(solution)/shard_map/prep/pallas_call | solution.py:318
  71.3 9.0 %collective-permute-done.16.norm2 = bf16[128,1536]{1,0:T(8,128)(2,1)} collective-permute-done((bf16[128,1536]{1,0:T(8,128)(2,1)}, bf16[128,1536]{1,0:T(8,128)(2,1)}, u32[]{:S(2)}, u32[]{:S(2)}) %collective-permute-start.16) | collective-permute-done | bytes 393248 | tf_op jit(solution)/shard_map/ppermute | solution.py:507
  80.3 15.7 %attend.1 = (bf16[2,512,192]{2,1,0:T(8,128)(2,1)}, f32[128,1536]{1,0:T(8,128)}, bf16[128,1536]{1,0:T(8,128)(2,1)}, bf16[128,1536]{1,0:T(8,128)(2,1)}, bf16[128,1...) custom-call(s32[4]{0:T(128)} %pad_add_fusion.1.place, ...), custom_call_target="tpu_custom_call" | custom-call | flops 5234491392 | bytes 9437184 | tf_op jit(solution)/shard_map/attend/pallas_call | solution.py:429
  96.9 3.2 %collective-permute-done.19 = bf16[4,1536,128]{2,1,0:T(8,128)(2,1)S(1)} collective-permute-done((bf16[4,1536,128]{2,1,0:T(8,128)(2,1)}, bf16[4,1536,128]{2,1,0:T(8,128)(2,1)S(1)}, u32[]{:S(2)}, u32[]{:S(2)}) %collective-permute-start.19) | collective-permute-done | bytes 1572896 | tf_op jit(solution)/shard_map/ppermute | solution.py:499
  103.0 2.2 %collective-permute-start.22 = (bf16[1536,128]{1,0:T(8,128)(2,1)}, bf16[1536,128]{1,0:T(8,128)(2,1)}, u32[]{:S(2)}, u32[]{:S(2)}) collective-permute-start(bf16[1536,128]{1,0:T(8,128)(2,1)} %get-tuple-element.71), channel_id=1, source_target_pairs={{0,96},{32,0},{64,32},{96,64},{1,97},{33,1},{65,33},{97,65},{2,98}... | collective-permute-start | bytes 1179656 | tf_op jit(solution)/shard_map/ppermute | solution.py:507
  107.1 2.1 %collective-permute-start.23 = (bf16[128,1536]{1,0:T(8,128)(2,1)}, bf16[128,1536]{1,0:T(8,128)(2,1)S(1)}, u32[]{:S(2)}, u32[]{:S(2)}) collective-permute-start(bf16[128,1536]{1,0:T(8,128)(2,1)} %get-tuple-element.50), channel_id=1, source_target_pairs={{0,2},{1,3},{2,0},{3,1},{4,6},{5,7},{6,4},{7,5},{8,10},{9,11},{10,... | collective-permute-start | bytes 1179656 | tf_op jit(solution)/shard_map/ppermute | solution.py:507
  109.2 5.2 %mix.1 = bf16[4,128,1536]{2,1,0:T(8,128)(2,1)} custom-call(s32[4]{0:T(128)} %pad_add_fusion.1.place, bf16[2,512,192]{2,1,0:T(8,128)(2,1)} %get-tuple-element.43.heads, bf16[384,1536]{1,0:T(8,128)(2,1)} %get-tuple-element.44.w_out), custom_call_target="tpu_custom_call" | custom-call | flops 603979776 | bytes 2359296 | tf_op jit(solution)/shard_map/mix/pallas_call | solution.py:464
  117.1 8.3 %collective-permute-done.20 = bf16[1536,128]{1,0:T(8,128)(2,1)} collective-permute-done((bf16[1536,128]{1,0:T(8,128)(2,1)S(1)}, bf16[1536,128]{1,0:T(8,128)(2,1)}, u32[]{:S(2)}, u32[]{:S(2)}) %collective-permute-start.20) | collective-permute-done | bytes 393248 | tf_op jit(solution)/shard_map/ppermute | solution.py:507
  130.4 4.6 %collective-permute-start.29 = (bf16[16,1536]{1,0:T(8,128)(2,1)}, bf16[16,1536]{1,0:T(8,128)(2,1)}, u32[]{:S(2)}, u32[]{:S(2)}) collective-permute-start(bf16[16,1536]{1,0:T(8,128)(2,1)} %get-tuple-element.78), channel_id=1, source_target_pairs={{1,0},{2,1},{3,2},{5,4},{6,5},{7,6},{9,8},{10,9},{11,10},{13,12},{... | collective-permute-start | bytes 147464 | tf_op jit(solution)/shard_map/ppermute | solution.py:616
  142.2 2.0 %collective-permute-start.26 = (bf16[128,1536]{1,0:T(8,128)(2,1)S(1)}, bf16[128,1536]{1,0:T(8,128)(2,1)}, u32[]{:S(2)}, u32[]{:S(2)}) collective-permute-start(bf16[128,1536]{1,0:T(8,128)(2,1)S(1)} %get-tuple-element.67), channel_id=1, source_target_pairs={{0,1},{1,2},{2,3},{3,0},{4,5},{5,6},{6,7},{7,4},{8,9},{9,10},{10,1... | collective-permute-start | bytes 1179656 | tf_op jit(solution)/shard_map/ppermute | solution.py:507
  146.4 12.8 %back.1 = bf16[256,1536]{1,0:T(8,128)(2,1)} custom-call(s32[256,64]{1,0:T(8,128)} %reshape.114.cells, bf16[256,1536]{1,0:T(8,128)(2,1)} %bitcast.143, f32[6,1536]{1,0:T(8,128)} %pad_maximum_fusion.6.table, bf16[128,1536]{1,0:T(8,128)(2,1)} %copy-done.6, bf16[16,1536]{1,0:T(8,128)(2,1)} %collective-permute-done.25.grad_prev, ...), custom_call_target="tpu_custom_call" | custom-call | flops 3019898880 | bytes 26738688 | tf_op jit(solution)/shard_map/back/pallas_call | solution.py:251
  159.2 13.7 %collective-permute-start.33 = (bf16[12,640]{1,0:T(8,128)(2,1)S(1)}, bf16[12,640]{1,0:T(8,128)(2,1)S(1)}, u32[]{:S(2)}, u32[]{:S(2)}) collective-permute-start(bf16[12,640]{1,0:T(8,128)(2,1)S(1)} %bitcast.179), channel_id=1, source_target_pairs={{0,0},{1,1},{2,2},{3,3},{4,64},{5,65},{6,66},{7,67},{8,4},{9,5},{1... | collective-permute-start | bytes 46088 | tf_op jit(solution)/shard_map/ppermute | solution.py:499
  174.8 5.0 %collective-permute-start.35 = (bf16[12,640]{1,0:T(8,128)(2,1)S(1)}, bf16[12,640]{1,0:T(8,128)(2,1)S(1)}, u32[]{:S(2)}, u32[]{:S(2)}) collective-permute-start(bf16[12,640]{1,0:T(8,128)(2,1)S(1)} %bitcast.176), channel_id=1, source_target_pairs={{0,2},{1,3},{2,0},{3,1},{4,66},{5,67},{6,64},{7,65},{8,6},{9,7},{1... | collective-permute-start | bytes 46088 | tf_op jit(solution)/shard_map/ppermute | solution.py:499
  179.8 2.7 %collective-permute-start.37 = (bf16[12,1536]{1,0:T(8,128)(2,1)S(1)}, bf16[12,1536]{1,0:T(8,128)(2,1)S(1)}, u32[]{:S(2)}, u32[]{:S(2)}) collective-permute-start(bf16[12,1536]{1,0:T(8,128)(2,1)S(1)} %bitcast.172), channel_id=1, source_target_pairs={{0,0},{1,32},{2,64},{3,96},{4,16},{5,48},{6,80},{7,112},{8,1},{9,3... | collective-permute-start | bytes 110600 | tf_op jit(solution)/shard_map/ppermute | solution.py:499
  183.4 7.8 %collective-permute-done.37 = bf16[12,1536]{1,0:T(8,128)(2,1)S(1)} collective-permute-done((bf16[12,1536]{1,0:T(8,128)(2,1)S(1)}, bf16[12,1536]{1,0:T(8,128)(2,1)S(1)}, u32[]{:S(2)}, u32[]{:S(2)}) %collective-permute-start.37) | collective-permute-done | bytes 36896 | tf_op jit(solution)/shard_map/ppermute | solution.py:499
  191.8 2.2 %fusion.3 = bf16[128,1536]{1,0:T(8,128)(2,1)} fusion(f32[128,1536]{1,0:T(8,128)S(1)} %copy-done, bf16[128,1536]{1,0:T(8,128)(2,1)} %collective-permute-done.28, bf16[128,1536]{1,0:T(8,128)(2,1)} %collective-permute-done.27, bf16[128,1536]{1,0:T(8,128)(2,1)} %collective-permute-done.26, bf16[4,128,1536]{2,1,0:T(8,128)(2,1)S(1)} %copy-done.2), kind=kLoop, calls=%fused_computation.7 | loop fusion | flops 1769472 | bytes 2752512 | tf_op jit(solution)/shard_map/convert_element_type | solution.py:676
  (207 shorter events, 56.6 us)
Async XLA Ops:
  2.2 18.7 %collective-permute-start.2 = (bf16[12,640]{1,0:T(8,128)(2,1)S(1)}, bf16[12,640]{1,0:T(8,128)(2,1)S(1)}, u32[]{:S(2)}, u32[]{:S(2)}) collective-permute-start(bf16[12,640]{1,0:T(8,128)(2,1)S(1)} %get-tuple-element.94), channel_id=1, source_target_pairs={{0,1},{1,2},{2,3},{3,0},{4,5},{5,6},{6,7},{7,4},{8,9},{9,10},{10,1... | collective-permute-start | bytes 46088 | tf_op jit(solution)/shard_map/ppermute | solution.py:507
  2.5 18.5 %collective-permute-start.3 = (bf16[12,640]{1,0:T(8,128)(2,1)S(1)}, bf16[12,640]{1,0:T(8,128)(2,1)S(1)}, u32[]{:S(2)}, u32[]{:S(2)}) collective-permute-start(bf16[12,640]{1,0:T(8,128)(2,1)S(1)} %get-tuple-element.95), channel_id=1, source_target_pairs={{0,2},{1,3},{2,0},{3,1},{4,6},{5,7},{6,4},{7,5},{8,10},{9,11},{10,... | collective-permute-start | bytes 46088 | tf_op jit(solution)/shard_map/ppermute | solution.py:507
  4.6 16.4 %collective-permute-start.4 = (bf16[12,640]{1,0:T(8,128)(2,1)S(1)}, bf16[12,640]{1,0:T(8,128)(2,1)S(1)}, u32[]{:S(2)}, u32[]{:S(2)}) collective-permute-start(bf16[12,640]{1,0:T(8,128)(2,1)S(1)} %get-tuple-element.92), channel_id=1, source_target_pairs={{0,3},{1,0},{2,1},{3,2},{4,7},{5,4},{6,5},{7,6},{8,11},{9,8},{10,9... | collective-permute-start | bytes 46088 | tf_op jit(solution)/shard_map/ppermute | solution.py:507
  4.6 19.1 %collective-permute-start.7 = (bf16[12,1536]{1,0:T(8,128)(2,1)}, bf16[12,1536]{1,0:T(8,128)(2,1)S(1)}, u32[]{:S(2)}, u32[]{:S(2)}) collective-permute-start(bf16[12,1536]{1,0:T(8,128)(2,1)} %param.18), channel_id=1, source_target_pairs={{0,0},{1,8},{2,16},{3,24},{4,4},{5,12},{6,20},{7,28},{8,32},{9,40}... | collective-permute-start | bytes 110600 | tf_op jit(solution)/shard_map/ppermute | solution.py:499
  15.1 19.5 %collective-permute-start = (bf16[8,1664]{1,0:T(8,128)(2,1)S(1)}, bf16[8,1664]{1,0:T(8,128)(2,1)S(1)}, u32[]{:S(2)}, u32[]{:S(2)}) collective-permute-start(bf16[8,1664]{1,0:T(8,128)(2,1)S(1)} %concatenate.40), channel_id=1, source_target_pairs={{0,1},{1,2},{2,3},{4,5},{5,6},{6,7},{8,9},{9,10},{10,11},{12,13},{... | collective-permute-start | bytes 79880 | tf_op jit(solution)/shard_map/ppermute | solution.py:613
  32.7 23.5 %collective-permute-start.6 = (bf16[2,128,1536]{2,1,0:T(8,128)(2,1)S(1)}, bf16[2,128,1536]{2,1,0:T(8,128)(2,1)S(1)}, u32[]{:S(2)}, u32[]{:S(2)}) collective-permute-start(bf16[2,128,1536]{2,1,0:T(8,128)(2,1)S(1)} %pad_maximum_fusion.1), channel_id=1, source_target_pairs={{0,3},{1,2},{2,1},{3,0},{4,7},{5,6},{6,5},{7,4},{8,11},{9,10},{10,... | collective-permute-start | bytes 2359304 | tf_op jit(solution)/shard_map/ppermute | solution.py:631
  34.2 15.7 %collective-permute-start.13 = (bf16[384,512]{1,0:T(8,128)(2,1)S(1)}, bf16[384,512]{1,0:T(8,128)(2,1)S(1)}, u32[]{:S(2)}, u32[]{:S(2)}) collective-permute-start(bf16[384,512]{1,0:T(8,128)(2,1)S(1)} %get-tuple-element.81), channel_id=1, source_target_pairs={{0,32},{32,64},{64,96},{96,0},{1,33},{33,65},{65,97},{97,1},{2,34}... | collective-permute-start | bytes 1179656 | tf_op jit(solution)/shard_map/ppermute | solution.py:507
  34.3 15.6 %collective-permute-start.12 = (bf16[384,512]{1,0:T(8,128)(2,1)S(1)}, bf16[384,512]{1,0:T(8,128)(2,1)S(1)}, u32[]{:S(2)}, u32[]{:S(2)}) collective-permute-start(bf16[384,512]{1,0:T(8,128)(2,1)S(1)} %get-tuple-element.81), channel_id=1, source_target_pairs={{0,64},{32,96},{64,0},{96,32},{1,65},{33,97},{65,1},{97,33},{2,66}... | collective-permute-start | bytes 1179656 | tf_op jit(solution)/shard_map/ppermute | solution.py:507
  34.6 19.5 %collective-permute-start.11 = (bf16[384,512]{1,0:T(8,128)(2,1)S(1)}, bf16[384,512]{1,0:T(8,128)(2,1)S(1)}, u32[]{:S(2)}, u32[]{:S(2)}) collective-permute-start(bf16[384,512]{1,0:T(8,128)(2,1)S(1)} %get-tuple-element.81), channel_id=1, source_target_pairs={{0,96},{32,0},{64,32},{96,64},{1,97},{33,1},{65,33},{97,65},{2,98}... | collective-permute-start | bytes 1179656 | tf_op jit(solution)/shard_map/ppermute | solution.py:507
  59.1 12.2 %collective-permute-start.15 = (bf16[128,1536]{1,0:T(8,128)(2,1)}, bf16[128,1536]{1,0:T(8,128)(2,1)S(1)}, u32[]{:S(2)}, u32[]{:S(2)}) collective-permute-start(bf16[128,1536]{1,0:T(8,128)(2,1)} %get-tuple-element.37.norm0), channel_id=1, source_target_pairs={{0,3},{1,0},{2,1},{3,2},{4,7},{5,4},{6,5},{7,6},{8,11},{9,8},{10,9... | collective-permute-start | bytes 1179656 | tf_op jit(solution)/shard_map/ppermute | solution.py:507
  60.6 19.7 %collective-permute-start.16 = (bf16[128,1536]{1,0:T(8,128)(2,1)}, bf16[128,1536]{1,0:T(8,128)(2,1)}, u32[]{:S(2)}, u32[]{:S(2)}) collective-permute-start(bf16[128,1536]{1,0:T(8,128)(2,1)} %get-tuple-element.37.norm0), channel_id=1, source_target_pairs={{0,2},{1,3},{2,0},{3,1},{4,6},{5,7},{6,4},{7,5},{8,10},{9,11},{10,... | collective-permute-start | bytes 1179656 | tf_op jit(solution)/shard_map/ppermute | solution.py:507
  62.2 18.0 %collective-permute-start.17 = (bf16[128,1536]{1,0:T(8,128)(2,1)}, bf16[128,1536]{1,0:T(8,128)(2,1)}, u32[]{:S(2)}, u32[]{:S(2)}) collective-permute-start(bf16[128,1536]{1,0:T(8,128)(2,1)} %get-tuple-element.37.norm0), channel_id=1, source_target_pairs={{0,1},{1,2},{2,3},{3,0},{4,5},{5,6},{6,7},{7,4},{8,9},{9,10},{10,1... | collective-permute-start | bytes 1179656 | tf_op jit(solution)/shard_map/ppermute | solution.py:507
  103.0 11.4 %collective-permute-start.22 = (bf16[1536,128]{1,0:T(8,128)(2,1)}, bf16[1536,128]{1,0:T(8,128)(2,1)}, u32[]{:S(2)}, u32[]{:S(2)}) collective-permute-start(bf16[1536,128]{1,0:T(8,128)(2,1)} %get-tuple-element.71), channel_id=1, source_target_pairs={{0,96},{32,0},{64,32},{96,64},{1,97},{33,1},{65,33},{97,65},{2,98}... | collective-permute-start | bytes 1179656 | tf_op jit(solution)/shard_map/ppermute | solution.py:507
  105.2 11.9 %collective-permute-start.21 = (bf16[1536,128]{1,0:T(8,128)(2,1)}, bf16[1536,128]{1,0:T(8,128)(2,1)}, u32[]{:S(2)}, u32[]{:S(2)}) collective-permute-start(bf16[1536,128]{1,0:T(8,128)(2,1)} %get-tuple-element.72), channel_id=1, source_target_pairs={{0,64},{32,96},{64,0},{96,32},{1,65},{33,97},{65,1},{97,33},{2,66}... | collective-permute-start | bytes 1179656 | tf_op jit(solution)/shard_map/ppermute | solution.py:507
  105.2 20.3 %collective-permute-start.20 = (bf16[1536,128]{1,0:T(8,128)(2,1)S(1)}, bf16[1536,128]{1,0:T(8,128)(2,1)}, u32[]{:S(2)}, u32[]{:S(2)}) collective-permute-start(bf16[1536,128]{1,0:T(8,128)(2,1)S(1)} %get-tuple-element.70), channel_id=1, source_target_pairs={{0,32},{32,64},{64,96},{96,0},{1,33},{33,65},{65,97},{97,1},{2,34}... | collective-permute-start | bytes 1179656 | tf_op jit(solution)/shard_map/ppermute | solution.py:507
  105.7 21.1 %collective-permute-start.24 = (bf16[128,1536]{1,0:T(8,128)(2,1)}, bf16[128,1536]{1,0:T(8,128)(2,1)S(1)}, u32[]{:S(2)}, u32[]{:S(2)}) collective-permute-start(bf16[128,1536]{1,0:T(8,128)(2,1)} %get-tuple-element.52), channel_id=1, source_target_pairs={{0,3},{1,0},{2,1},{3,2},{4,7},{5,4},{6,5},{7,6},{8,11},{9,8},{10,9... | collective-permute-start | bytes 1179656 | tf_op jit(solution)/shard_map/ppermute | solution.py:507
  107.1 19.8 %collective-permute-start.23 = (bf16[128,1536]{1,0:T(8,128)(2,1)}, bf16[128,1536]{1,0:T(8,128)(2,1)S(1)}, u32[]{:S(2)}, u32[]{:S(2)}) collective-permute-start(bf16[128,1536]{1,0:T(8,128)(2,1)} %get-tuple-element.50), channel_id=1, source_target_pairs={{0,2},{1,3},{2,0},{3,1},{4,6},{5,7},{6,4},{7,5},{8,10},{9,11},{10,... | collective-permute-start | bytes 1179656 | tf_op jit(solution)/shard_map/ppermute | solution.py:507
  114.4 12.5 %collective-permute-start.18 = (bf16[128,1536]{1,0:T(8,128)(2,1)}, bf16[128,1536]{1,0:T(8,128)(2,1)S(1)}, u32[]{:S(2)}, u32[]{:S(2)}) collective-permute-start(bf16[128,1536]{1,0:T(8,128)(2,1)} %get-tuple-element.46), channel_id=1, source_target_pairs={{0,1},{1,2},{2,3},{3,0},{4,5},{5,6},{6,7},{7,4},{8,9},{9,10},{10,1... | collective-permute-start | bytes 1179656 | tf_op jit(solution)/shard_map/ppermute | solution.py:507
  130.4 13.9 %collective-permute-start.29 = (bf16[16,1536]{1,0:T(8,128)(2,1)}, bf16[16,1536]{1,0:T(8,128)(2,1)}, u32[]{:S(2)}, u32[]{:S(2)}) collective-permute-start(bf16[16,1536]{1,0:T(8,128)(2,1)} %get-tuple-element.78), channel_id=1, source_target_pairs={{1,0},{2,1},{3,2},{5,4},{6,5},{7,6},{9,8},{10,9},{11,10},{13,12},{... | collective-permute-start | bytes 147464 | tf_op jit(solution)/shard_map/ppermute | solution.py:616
  140.9 50.9 %collective-permute-start.28 = (bf16[128,1536]{1,0:T(8,128)(2,1)}, bf16[128,1536]{1,0:T(8,128)(2,1)}, u32[]{:S(2)}, u32[]{:S(2)}) collective-permute-start(bf16[128,1536]{1,0:T(8,128)(2,1)} %get-tuple-element.68), channel_id=1, source_target_pairs={{0,3},{1,0},{2,1},{3,2},{4,7},{5,4},{6,5},{7,6},{8,11},{9,8},{10,9... | collective-permute-start | bytes 1179656 | tf_op jit(solution)/shard_map/ppermute | solution.py:507
  140.9 50.9 %collective-permute-start.27 = (bf16[128,1536]{1,0:T(8,128)(2,1)}, bf16[128,1536]{1,0:T(8,128)(2,1)}, u32[]{:S(2)}, u32[]{:S(2)}) collective-permute-start(bf16[128,1536]{1,0:T(8,128)(2,1)} %get-tuple-element.69), channel_id=1, source_target_pairs={{0,2},{1,3},{2,0},{3,1},{4,6},{5,7},{6,4},{7,5},{8,10},{9,11},{10,... | collective-permute-start | bytes 1179656 | tf_op jit(solution)/shard_map/ppermute | solution.py:507
  142.2 49.5 %collective-permute-start.26 = (bf16[128,1536]{1,0:T(8,128)(2,1)S(1)}, bf16[128,1536]{1,0:T(8,128)(2,1)}, u32[]{:S(2)}, u32[]{:S(2)}) collective-permute-start(bf16[128,1536]{1,0:T(8,128)(2,1)S(1)} %get-tuple-element.67), channel_id=1, source_target_pairs={{0,1},{1,2},{2,3},{3,0},{4,5},{5,6},{6,7},{7,4},{8,9},{9,10},{10,1... | collective-permute-start | bytes 1179656 | tf_op jit(solution)/shard_map/ppermute | solution.py:507
  144.6 28.4 %collective-permute-start.36 = (bf16[12,640]{1,0:T(8,128)(2,1)S(1)}, bf16[12,640]{1,0:T(8,128)(2,1)S(1)}, u32[]{:S(2)}, u32[]{:S(2)}) collective-permute-start(bf16[12,640]{1,0:T(8,128)(2,1)S(1)} %bitcast.178), channel_id=1, source_target_pairs={{0,3},{1,0},{2,1},{3,2},{4,67},{5,64},{6,65},{7,66},{8,7},{9,4},{1... | collective-permute-start | bytes 46088 | tf_op jit(solution)/shard_map/ppermute | solution.py:499
  159.2 15.5 %collective-permute-start.33 = (bf16[12,640]{1,0:T(8,128)(2,1)S(1)}, bf16[12,640]{1,0:T(8,128)(2,1)S(1)}, u32[]{:S(2)}, u32[]{:S(2)}) collective-permute-start(bf16[12,640]{1,0:T(8,128)(2,1)S(1)} %bitcast.179), channel_id=1, source_target_pairs={{0,0},{1,1},{2,2},{3,3},{4,64},{5,65},{6,66},{7,67},{8,4},{9,5},{1... | collective-permute-start | bytes 46088 | tf_op jit(solution)/shard_map/ppermute | solution.py:499
  (34 other events, 268.8 us)

commit v7 on v5

--- a/solution.py
+++ b/solution.py
@@ -453,26 +453,29 @@
     )(place, *ins)
 
 
-def mix_kernel(place, heads, w_out, out):
-    total = ndot(heads[0], w_out[0:VD, :]) + ndot(heads[1], w_out[VD : 2 * VD, :])
-    out[0] = total.astype(BF16)
+def mix_kernel(place, heads, w_out, part0, part1, part2, part3):
+    for turn, out in enumerate((part0, part1, part2, part3)):
+        length = out.shape[0]
+        at = pl.multiple_of(lax.rem(place[0] + turn, 4) * length, length)
+        total = ndot(heads[0, pl.ds(at, length), :], w_out[0:VD, :])
+        total = total + ndot(heads[1, pl.ds(at, length), :], w_out[VD : 2 * VD, :])
+        out[...] = total.astype(BF16)
 
 
 def mix(place, heads, w_out):
     rows = heads.shape[1] // 4
     width = w_out.shape[1]
+    whole = lambda array: pl.BlockSpec(array.shape, lambda n, s: (0,) * array.ndim)
+    outs = [jax.ShapeDtypeStruct((rows, width), BF16)] * 4
     return pl.pallas_call(
         mix_kernel,
         grid_spec=pltpu.PrefetchScalarGridSpec(
             num_scalar_prefetch=1,
-            grid=(4,),
-            in_specs=[
-                pl.BlockSpec((2, rows, VD), lambda n, s: (0, lax.rem(s[0] + n, 4), 0)),
-                pl.BlockSpec(w_out.shape, lambda n, s: (0, 0)),
-            ],
-            out_specs=pl.BlockSpec((1, rows, width), lambda n, s: (n, 0, 0)),
-        ),
-        out_shape=jax.ShapeDtypeStruct((4, rows, width), BF16),
+            grid=(1,),
+            in_specs=[whole(heads), whole(w_out)],
+            out_specs=[whole(out) for out in outs],
+        ),
+        out_shape=outs,
         compiler_params=pltpu.CompilerParams(vmem_limit_bytes=VMEM_LIMIT),
         cost_estimate=pl.CostEstimate(
             flops=16 * rows * width * VD, bytes_accessed=12 * rows * width, transcendentals=0
@@ -657,22 +660,23 @@
     norms = [after(norm, w_in) for norm in norms]
     heads, *d_parts, own, other = attend(spot, norms, w_in, cot_all, d_heads)
     d_parts[1:] = [turned(d_parts[k], "x", k) for k in range(1, 4)]
-    mine = (own.astype(F32) + flipped(other).astype(F32)).astype(BF16)
+    other = flipped(other)
+    mine = [(own[k].astype(F32) + other[k].astype(F32)).astype(BF16) for k in range(4)]
     total = mine[0].astype(F32)
     for k in range(1, 4):
         total = total + turned(mine[k], "z", k).astype(F32)
     mine = total.astype(BF16)
+    out_parts = mix(spot, heads, full_out)
     d_normed = d_parts[0]
     for k in range(1, 4):
-        d_normed = d_normed + after(d_parts[k], mine).astype(F32)
+        d_normed = d_normed + after(d_parts[k], mine, out_parts[0]).astype(F32)
     mine = summed(split_rows(mine), "y")
 
     d_pooled = cot.astype(F32) + rms_back(pooled, attn_gain, d_normed)
     grad = (d_pooled * 0.5).astype(BF16)
-    out_parts = mix(spot, heads, full_out)
     grad_prev, grad_next = ahead(grad[half - 16 :]), behind(grad[:16])
     grad_next = after(grad_next, mine)
-    coarse = (pooled + returned(after(out_parts, grad_prev))).astype(BF16)
+    coarse = (pooled + returned([after(part, grad_prev) for part in out_parts])).astype(BF16)
     skip_grad = back(cells, skip, table, grad, grad_prev, grad_next, conv_weight)
 
     factor = 1.0 / 32

time: 192 us -> 188 us (0.979)
  local copies, waits for them, and re-layouts: 15.2 us -> 9.48 us
  starting transfers between devices: 75.1 us -> 78.5 us
    ppermute x8, starting transfers between devices: 32.5 us -> 36.5 us  [moved(): return lax.ppermute(value, AXES, pairs)]
    ppermute x2, starting transfers between devices: 8.12 us -> 5.91 us  [behind(): return lax.ppermute(value, 'x', [(i + 1, i) for i in range(3)])]
  transfers between devices with their start and end apart: 38 -> 38, of which waited for: 8 -> 7; matrix products, arithmetic and copies ran while one was open for 11% -> 10% of each run, Pallas kernels for 19% -> 18%
where the time goes in v7:
time: 188 us; the launch traced here: 186 us
  starting transfers between devices  78.5 us (42%)
  Pallas kernels  49.6 us (26%)
  waiting for transfers between devices  29.8 us (16%)
  other arithmetic  17.1 us (9%)
  local copies, waits for them, and re-layouts  9.48 us (5%)
    ppermute x8, starting transfers between devices, moved(): return lax.ppermute(value, AXES, pairs)  36.5 us
    ppermute x24, starting transfers between devices, turned(): return lax.ppermute(value, axis, [(i, (i + by) % 4) for i in range(4)])  30.6 us
    ppermute x24, waiting for transfers between devices, turned(): return lax.ppermute(value, axis, [(i, (i + by) % 4) for i in range(4)])  20.9 us
    pallas_call x1, Pallas kernels, attend(): pl.pallas_call(attend_kernel, grid_spec=pltpu.PrefetchScalarGridSpec(num_...  15.7 us
    pallas_call x1, Pallas kernels, back(): pl.pallas_call(back_kernel, grid=(1,), in_specs=[whole(a) for a in small]...  12.8 us
    pallas_call x1, Pallas kernels, front(): pl.pallas_call(front_kernel, grid_spec=pltpu.PrefetchScalarGridSpec(num_s...  11.6 us
    ppermute x8, waiting for transfers between devices, moved(): return lax.ppermute(value, AXES, pairs)  8.91 us
    ppermute x2, starting transfers between devices, behind(): return lax.ppermute(value, 'x', [(i + 1, i) for i in range(3)])  5.91 us
  transfers between devices with their start and end apart: 38, of which 7 were waited for; matrix products, arithmetic and copies ran while one was open for 10% of the time, Pallas kernels for 18%

profile of v7, /device:TPU:15, one launch (start us, length us, event | category | flops | bytes accessed | tf_op | source)
XLA Modules:
  0.0 186.0 jit_solution(8499816205588972375)
XLA Ops:
  2.5 2.1 %collective-permute-start.3 = (bf16[12,640]{1,0:T(8,128)(2,1)S(1)}, bf16[12,640]{1,0:T(8,128)(2,1)S(1)}, u32[]{:S(2)}, u32[]{:S(2)}) collective-permute-start(bf16[12,640]{1,0:T(8,128)(2,1)S(1)} %get-tuple-element.104), channel_id=1, source_target_pairs={{0,2},{1,3},{2,0},{3,1},{4,6},{5,7},{6,4},{7,5},{8,10},{9,11},{10,... | collective-permute-start | bytes 46088 | tf_op jit(solution)/shard_map/ppermute | solution.py:510
  4.6 7.7 %collective-permute-start.7 = (bf16[12,1536]{1,0:T(8,128)(2,1)}, bf16[12,1536]{1,0:T(8,128)(2,1)S(1)}, u32[]{:S(2)}, u32[]{:S(2)}) collective-permute-start(bf16[12,1536]{1,0:T(8,128)(2,1)} %param.18), channel_id=1, source_target_pairs={{0,0},{1,8},{2,16},{3,24},{4,4},{5,12},{6,20},{7,28},{8,32},{9,40}... | collective-permute-start | bytes 110600 | tf_op jit(solution)/shard_map/ppermute | solution.py:502
  18.6 2.2 %collective-permute-start.5 = (bf16[128,1536]{1,0:T(8,128)(2,1)}, bf16[128,1536]{1,0:T(8,128)(2,1)S(1)}, u32[]{:S(2)}, u32[]{:S(2)}) collective-permute-start(bf16[128,1536]{1,0:T(8,128)(2,1)} %bitcast.131), channel_id=1, source_target_pairs={{0,1},{1,0},{2,3},{3,2},{4,5},{5,4},{6,7},{7,6},{8,9},{9,8},{10,11... | collective-permute-start | bytes 1179656 | tf_op jit(solution)/shard_map/ppermute | solution.py:632
  20.9 2.3 %collective-permute-start.10 = (bf16[4,12,1024]{2,0,1:T(4,128)(2,1)S(1)}, bf16[4,12,1024]{2,0,1:T(4,128)(2,1)S(1)}, u32[]{:S(2)}, u32[]{:S(2)}) collective-permute-start(bf16[4,12,1024]{2,0,1:T(4,128)(2,1)S(1)} %get-tuple-element.92), channel_id=1, source_target_pairs={{0,8},{8,16},{16,24},{24,0},{1,9},{9,17},{17,25},{25,1},{2,10},{10... | collective-permute-start | bytes 294920 | tf_op jit(solution)/shard_map/ppermute | solution.py:510
  33.1 2.6 %collective-permute-start.11 = (bf16[384,512]{1,0:T(8,128)(2,1)S(1)}, bf16[384,512]{1,0:T(8,128)(2,1)S(1)}, u32[]{:S(2)}, u32[]{:S(2)}) collective-permute-start(bf16[384,512]{1,0:T(8,128)(2,1)S(1)} %get-tuple-element.90), channel_id=1, source_target_pairs={{0,96},{32,0},{64,32},{96,64},{1,97},{33,1},{65,33},{97,65},{2,98}... | collective-permute-start | bytes 1179656 | tf_op jit(solution)/shard_map/ppermute | solution.py:510
  39.0 11.6 %front.1 = (f32[128,1536]{1,0:T(8,128)}, bf16[128,1536]{1,0:T(8,128)(2,1)}) custom-call(s32[2]{0:T(128)} %pad_add_fusion.ends, s32[256,64]{1,0:T(8,128)} %reshape.128.cells, bf16[256,1536]{1,0:T(8,128)(2,1)} %bitcast.133, bf16[8,1664]{1,0:T(8,128)(2,1)} %copy-done.13, bf16[8,1664]{1,0:T(8,128)(2,1)} %copy-done.14, f32[6,1536]{1,0:T(8,128)} %pad_maximum_fusion.6.table, ...), custom_call_target="tpu_custom_call" | custom-call | flops 3019898880 | bytes 26738688 | tf_op jit(solution)/shard_map/front/pallas_call | solution.py:130
  50.7 2.1 %collective-permute-done.11 = bf16[384,512]{1,0:T(8,128)(2,1)S(1)} collective-permute-done((bf16[384,512]{1,0:T(8,128)(2,1)S(1)}, bf16[384,512]{1,0:T(8,128)(2,1)S(1)}, u32[]{:S(2)}, u32[]{:S(2)}) %collective-permute-start.11) | collective-permute-done | bytes 393248 | tf_op jit(solution)/shard_map/ppermute | solution.py:510
  53.0 2.1 %collective-permute-start.14 = (bf16[4,384,512]{2,1,0:T(8,128)(2,1)S(1)}, bf16[4,384,512]{2,1,0:T(8,128)(2,1)S(1)}, u32[]{:S(2)}, u32[]{:S(2)}) collective-permute-start(bf16[4,384,512]{2,1,0:T(8,128)(2,1)S(1)} %pad_maximum_fusion.near), channel_id=1, source_target_pairs={{0,4},{1,5},{2,6},{3,7},{4,0},{5,1},{6,2},{7,3},{8,12},{9,13},{10,... | collective-permute-start | bytes 4718600 | tf_op jit(solution)/shard_map/ppermute | solution.py:502
  61.7 5.7 %prep.1 = (bf16[1536,640]{1,0:T(8,128)(2,1)}, bf16[384,1536]{1,0:T(8,128)(2,1)}, bf16[512,1536]{1,0:T(8,128)(2,1)}, bf16[2,512,192]{2,1,0:T(8,128)(2,1)}) custom-call(s32[4]{0:T(128)} %pad_add_fusion.1.place, bf16[128,1536]{1,0:T(8,128)(2,1)} %bitcast.132, bf16[128,1536]{1,0:T(8,128)(2,1)} %copy-done.7, bf16[2,128,1536]{2,1,0:T(8,128)(2,1)} %collective-permute-done.6.cot2, ...), custom_call_target="tpu_custom_call" | custom-call | flops 603979776 | bytes 23592960 | tf_op jit(solution)/shard_map/prep/pallas_call | solution.py:318
  67.4 8.1 %collective-permute-done.16.norm2 = bf16[128,1536]{1,0:T(8,128)(2,1)} collective-permute-done((bf16[128,1536]{1,0:T(8,128)(2,1)S(1)}, bf16[128,1536]{1,0:T(8,128)(2,1)}, u32[]{:S(2)}, u32[]{:S(2)}) %collective-permute-start.16) | collective-permute-done | bytes 393248 | tf_op jit(solution)/shard_map/ppermute | solution.py:510
  75.5 15.7 %attend.1 = (bf16[2,512,192]{2,1,0:T(8,128)(2,1)}, f32[128,1536]{1,0:T(8,128)}, bf16[128,1536]{1,0:T(8,128)(2,1)}, bf16[128,1536]{1,0:T(8,128)(2,1)}, bf16[128,1...) custom-call(s32[4]{0:T(128)} %pad_add_fusion.1.place, ...), custom_call_target="tpu_custom_call" | custom-call | flops 5234491392 | bytes 9437184 | tf_op jit(solution)/shard_map/attend/pallas_call | solution.py:429
  92.8 3.2 %collective-permute-done.19 = bf16[4,1536,128]{2,1,0:T(8,128)(2,1)S(1)} collective-permute-done((bf16[4,1536,128]{2,1,0:T(8,128)(2,1)}, bf16[4,1536,128]{2,1,0:T(8,128)(2,1)S(1)}, u32[]{:S(2)}, u32[]{:S(2)}) %collective-permute-start.19) | collective-permute-done | bytes 1572896 | tf_op jit(solution)/shard_map/ppermute | solution.py:502
  96.0 2.4 %fusion.4 = (bf16[1536,128]{1,0:T(8,128)(2,1)}, bf16[1536,128]{1,0:T(8,128)(2,1)S(1)}, bf16[1536,128]{1,0:T(8,128)(2,1)}) fusion(bf16[4,1536,128]{2,1,0:T(8,128)(2,1)S(1)} %collective-permute-done.19, bf16[4,1536,128]{2,1,0:T(8,128)(2,1)} %get-tuple-element.53), kind=kLoop, calls=%fused_computation.24 | loop fusion | flops 2359296 | bytes 3538944 | tf_op jit(solution)/shard_map/convert_element_type | solution.py:664
  98.5 2.3 %collective-permute-start.22 = (bf16[1536,128]{1,0:T(8,128)(2,1)S(1)}, bf16[1536,128]{1,0:T(8,128)(2,1)S(1)}, u32[]{:S(2)}, u32[]{:S(2)}) collective-permute-start(bf16[1536,128]{1,0:T(8,128)(2,1)S(1)} %get-tuple-element.80), channel_id=1, source_target_pairs={{0,96},{32,0},{64,32},{96,64},{1,97},{33,1},{65,33},{97,65},{2,98}... | collective-permute-start | bytes 1179656 | tf_op jit(solution)/shard_map/ppermute | solution.py:510
  103.1 2.1 %collective-permute-start.23 = (bf16[128,1536]{1,0:T(8,128)(2,1)}, bf16[128,1536]{1,0:T(8,128)(2,1)S(1)}, u32[]{:S(2)}, u32[]{:S(2)}) collective-permute-start(bf16[128,1536]{1,0:T(8,128)(2,1)} %get-tuple-element.56), channel_id=1, source_target_pairs={{0,2},{1,3},{2,0},{3,1},{4,6},{5,7},{6,4},{7,5},{8,10},{9,11},{10,... | collective-permute-start | bytes 1179656 | tf_op jit(solution)/shard_map/ppermute | solution.py:510
  105.2 3.8 %mix.1 = (bf16[128,1536]{1,0:T(8,128)(2,1)}, bf16[128,1536]{1,0:T(8,128)(2,1)}, bf16[128,1536]{1,0:T(8,128)(2,1)}, bf16[128,1536]{1,0:T(8,128)(2,1)}) custom-call(s32[4]{0:T(128)} %pad_add_fusion.1.place, bf16[2,512,192]{2,1,0:T(8,128)(2,1)} %get-tuple-element.48.heads, bf16[384,1536]{1,0:T(8,128)(2,1)} %get-tuple-element.49.w_out), custom_call_target="tpu_custom_call" | custom-call | flops 603979776 | bytes 2359296 | tf_op jit(solution)/shard_map/mix/pallas_call | solution.py:470
  112.6 9.0 %collective-permute-done.20 = bf16[1536,128]{1,0:T(8,128)(2,1)} collective-permute-done((bf16[1536,128]{1,0:T(8,128)(2,1)}, bf16[1536,128]{1,0:T(8,128)(2,1)}, u32[]{:S(2)}, u32[]{:S(2)}) %collective-permute-start.20) | collective-permute-done | bytes 393248 | tf_op jit(solution)/shard_map/ppermute | solution.py:510
  130.1 4.0 %collective-permute-start.29 = (bf16[16,1536]{1,0:T(8,128)(2,1)S(1)}, bf16[16,1536]{1,0:T(8,128)(2,1)S(1)}, u32[]{:S(2)}, u32[]{:S(2)}) collective-permute-start(bf16[16,1536]{1,0:T(8,128)(2,1)S(1)} %get-tuple-element.87), channel_id=1, source_target_pairs={{1,0},{2,1},{3,2},{5,4},{6,5},{7,6},{9,8},{10,9},{11,10},{13,12},{... | collective-permute-start | bytes 147464 | tf_op jit(solution)/shard_map/ppermute | solution.py:619
  139.6 12.8 %back.1 = bf16[256,1536]{1,0:T(8,128)(2,1)} custom-call(s32[256,64]{1,0:T(8,128)} %reshape.128.cells, bf16[256,1536]{1,0:T(8,128)(2,1)} %bitcast.134, f32[6,1536]{1,0:T(8,128)} %pad_maximum_fusion.6.table, bf16[128,1536]{1,0:T(8,128)(2,1)} %copy-done.5, bf16[16,1536]{1,0:T(8,128)(2,1)} %copy-done.11, bf16[16,1536]{1,0:T(8,128)(2,1)} %copy-done.12, ...), custom_call_target="tpu_custom_call" | custom-call | flops 3019898880 | bytes 26738688 | tf_op jit(solution)/shard_map/back/pallas_call | solution.py:251
  152.5 12.6 %collective-permute-start.33 = (bf16[12,640]{1,0:T(8,128)(2,1)S(1)}, bf16[12,640]{1,0:T(8,128)(2,1)S(1)}, u32[]{:S(2)}, u32[]{:S(2)}) collective-permute-start(bf16[12,640]{1,0:T(8,128)(2,1)S(1)} %bitcast.170), channel_id=1, source_target_pairs={{0,0},{1,1},{2,2},{3,3},{4,64},{5,65},{6,66},{7,67},{8,4},{9,5},{1... | collective-permute-start | bytes 46088 | tf_op jit(solution)/shard_map/ppermute | solution.py:502
  165.2 3.3 %collective-permute-start.34 = (bf16[12,640]{1,0:T(8,128)(2,1)S(1)}, bf16[12,640]{1,0:T(8,128)(2,1)S(1)}, u32[]{:S(2)}, u32[]{:S(2)}) collective-permute-start(bf16[12,640]{1,0:T(8,128)(2,1)S(1)} %bitcast.168), channel_id=1, source_target_pairs={{0,1},{1,2},{2,3},{3,0},{4,65},{5,66},{6,67},{7,64},{8,5},{9,6},{1... | collective-permute-start | bytes 46088 | tf_op jit(solution)/shard_map/ppermute | solution.py:502
  168.5 3.5 %collective-permute-start.35 = (bf16[12,640]{1,0:T(8,128)(2,1)S(1)}, bf16[12,640]{1,0:T(8,128)(2,1)S(1)}, u32[]{:S(2)}, u32[]{:S(2)}) collective-permute-start(bf16[12,640]{1,0:T(8,128)(2,1)S(1)} %bitcast.167), channel_id=1, source_target_pairs={{0,2},{1,3},{2,0},{3,1},{4,66},{5,67},{6,64},{7,65},{8,6},{9,7},{1... | collective-permute-start | bytes 46088 | tf_op jit(solution)/shard_map/ppermute | solution.py:502
  172.1 5.1 %collective-permute-start.37 = (bf16[12,1536]{1,0:T(8,128)(2,1)S(1)}, bf16[12,1536]{1,0:T(8,128)(2,1)S(1)}, u32[]{:S(2)}, u32[]{:S(2)}) collective-permute-start(bf16[12,1536]{1,0:T(8,128)(2,1)S(1)} %bitcast.163), channel_id=1, source_target_pairs={{0,0},{1,32},{2,64},{3,96},{4,16},{5,48},{6,80},{7,112},{8,1},{9,3... | collective-permute-start | bytes 110600 | tf_op jit(solution)/shard_map/ppermute | solution.py:502
  178.1 5.7 %collective-permute-done.37 = bf16[12,1536]{1,0:T(8,128)(2,1)S(1)} collective-permute-done((bf16[12,1536]{1,0:T(8,128)(2,1)S(1)}, bf16[12,1536]{1,0:T(8,128)(2,1)S(1)}, u32[]{:S(2)}, u32[]{:S(2)}) %collective-permute-start.37) | collective-permute-done | bytes 36896 | tf_op jit(solution)/shard_map/ppermute | solution.py:502
  (199 shorter events, 52.5 us)
Async XLA Ops:
  2.2 15.8 %collective-permute-start.2 = (bf16[12,640]{1,0:T(8,128)(2,1)S(1)}, bf16[12,640]{1,0:T(8,128)(2,1)S(1)}, u32[]{:S(2)}, u32[]{:S(2)}) collective-permute-start(bf16[12,640]{1,0:T(8,128)(2,1)S(1)} %get-tuple-element.103), channel_id=1, source_target_pairs={{0,1},{1,2},{2,3},{3,0},{4,5},{5,6},{6,7},{7,4},{8,9},{9,10},{10,1... | collective-permute-start | bytes 46088 | tf_op jit(solution)/shard_map/ppermute | solution.py:510
  2.5 15.6 %collective-permute-start.3 = (bf16[12,640]{1,0:T(8,128)(2,1)S(1)}, bf16[12,640]{1,0:T(8,128)(2,1)S(1)}, u32[]{:S(2)}, u32[]{:S(2)}) collective-permute-start(bf16[12,640]{1,0:T(8,128)(2,1)S(1)} %get-tuple-element.104), channel_id=1, source_target_pairs={{0,2},{1,3},{2,0},{3,1},{4,6},{5,7},{6,4},{7,5},{8,10},{9,11},{10,... | collective-permute-start | bytes 46088 | tf_op jit(solution)/shard_map/ppermute | solution.py:510
  4.6 13.5 %collective-permute-start.4 = (bf16[12,640]{1,0:T(8,128)(2,1)S(1)}, bf16[12,640]{1,0:T(8,128)(2,1)S(1)}, u32[]{:S(2)}, u32[]{:S(2)}) collective-permute-start(bf16[12,640]{1,0:T(8,128)(2,1)S(1)} %get-tuple-element.101), channel_id=1, source_target_pairs={{0,3},{1,0},{2,1},{3,2},{4,7},{5,4},{6,5},{7,6},{8,11},{9,8},{10,9... | collective-permute-start | bytes 46088 | tf_op jit(solution)/shard_map/ppermute | solution.py:510
  4.6 16.2 %collective-permute-start.7 = (bf16[12,1536]{1,0:T(8,128)(2,1)}, bf16[12,1536]{1,0:T(8,128)(2,1)S(1)}, u32[]{:S(2)}, u32[]{:S(2)}) collective-permute-start(bf16[12,1536]{1,0:T(8,128)(2,1)} %param.18), channel_id=1, source_target_pairs={{0,0},{1,8},{2,16},{3,24},{4,4},{5,12},{6,20},{7,28},{8,32},{9,40}... | collective-permute-start | bytes 110600 | tf_op jit(solution)/shard_map/ppermute | solution.py:502
  15.1 18.0 %collective-permute-start = (bf16[8,1664]{1,0:T(8,128)(2,1)S(1)}, bf16[8,1664]{1,0:T(8,128)(2,1)S(1)}, u32[]{:S(2)}, u32[]{:S(2)}) collective-permute-start(bf16[8,1664]{1,0:T(8,128)(2,1)S(1)} %concatenate.40), channel_id=1, source_target_pairs={{0,1},{1,2},{2,3},{4,5},{5,6},{6,7},{8,9},{9,10},{10,11},{12,13},{... | collective-permute-start | bytes 79880 | tf_op jit(solution)/shard_map/ppermute | solution.py:616
  18.6 11.8 %collective-permute-start.5 = (bf16[128,1536]{1,0:T(8,128)(2,1)}, bf16[128,1536]{1,0:T(8,128)(2,1)S(1)}, u32[]{:S(2)}, u32[]{:S(2)}) collective-permute-start(bf16[128,1536]{1,0:T(8,128)(2,1)} %bitcast.131), channel_id=1, source_target_pairs={{0,1},{1,0},{2,3},{3,2},{4,5},{5,4},{6,7},{7,6},{8,9},{9,8},{10,11... | collective-permute-start | bytes 1179656 | tf_op jit(solution)/shard_map/ppermute | solution.py:632
  31.4 21.6 %collective-permute-start.6 = (bf16[2,128,1536]{2,1,0:T(8,128)(2,1)}, bf16[2,128,1536]{2,1,0:T(8,128)(2,1)}, u32[]{:S(2)}, u32[]{:S(2)}) collective-permute-start(bf16[2,128,1536]{2,1,0:T(8,128)(2,1)} %pad_maximum_fusion.1), channel_id=1, source_target_pairs={{0,3},{1,2},{2,1},{3,0},{4,7},{5,6},{6,5},{7,4},{8,11},{9,10},{10,... | collective-permute-start | bytes 2359304 | tf_op jit(solution)/shard_map/ppermute | solution.py:633
  32.9 17.7 %collective-permute-start.13 = (bf16[384,512]{1,0:T(8,128)(2,1)S(1)}, bf16[384,512]{1,0:T(8,128)(2,1)S(1)}, u32[]{:S(2)}, u32[]{:S(2)}) collective-permute-start(bf16[384,512]{1,0:T(8,128)(2,1)S(1)} %get-tuple-element.90), channel_id=1, source_target_pairs={{0,32},{32,64},{64,96},{96,0},{1,33},{33,65},{65,97},{97,1},{2,34}... | collective-permute-start | bytes 1179656 | tf_op jit(solution)/shard_map/ppermute | solution.py:510
  33.0 17.7 %collective-permute-start.12 = (bf16[384,512]{1,0:T(8,128)(2,1)S(1)}, bf16[384,512]{1,0:T(8,128)(2,1)S(1)}, u32[]{:S(2)}, u32[]{:S(2)}) collective-permute-start(bf16[384,512]{1,0:T(8,128)(2,1)S(1)} %get-tuple-element.90), channel_id=1, source_target_pairs={{0,64},{32,96},{64,0},{96,32},{1,65},{33,97},{65,1},{97,33},{2,66}... | collective-permute-start | bytes 1179656 | tf_op jit(solution)/shard_map/ppermute | solution.py:510
  33.1 19.7 %collective-permute-start.11 = (bf16[384,512]{1,0:T(8,128)(2,1)S(1)}, bf16[384,512]{1,0:T(8,128)(2,1)S(1)}, u32[]{:S(2)}, u32[]{:S(2)}) collective-permute-start(bf16[384,512]{1,0:T(8,128)(2,1)S(1)} %get-tuple-element.90), channel_id=1, source_target_pairs={{0,96},{32,0},{64,32},{96,64},{1,97},{33,1},{65,33},{97,65},{2,98}... | collective-permute-start | bytes 1179656 | tf_op jit(solution)/shard_map/ppermute | solution.py:510
  55.1 12.4 %collective-permute-start.15 = (bf16[128,1536]{1,0:T(8,128)(2,1)S(1)}, bf16[128,1536]{1,0:T(8,128)(2,1)}, u32[]{:S(2)}, u32[]{:S(2)}) collective-permute-start(bf16[128,1536]{1,0:T(8,128)(2,1)S(1)} %copy-done.15), channel_id=1, source_target_pairs={{0,3},{1,0},{2,1},{3,2},{4,7},{5,4},{6,5},{7,6},{8,11},{9,8},{10,9... | collective-permute-start | bytes 1179656 | tf_op jit(solution)/shard_map/ppermute | solution.py:510
  56.8 18.8 %collective-permute-start.16 = (bf16[128,1536]{1,0:T(8,128)(2,1)S(1)}, bf16[128,1536]{1,0:T(8,128)(2,1)}, u32[]{:S(2)}, u32[]{:S(2)}) collective-permute-start(bf16[128,1536]{1,0:T(8,128)(2,1)S(1)} %copy-done.15), channel_id=1, source_target_pairs={{0,2},{1,3},{2,0},{3,1},{4,6},{5,7},{6,4},{7,5},{8,10},{9,11},{10,... | collective-permute-start | bytes 1179656 | tf_op jit(solution)/shard_map/ppermute | solution.py:510
  58.5 17.0 %collective-permute-start.17 = (bf16[128,1536]{1,0:T(8,128)(2,1)S(1)}, bf16[128,1536]{1,0:T(8,128)(2,1)}, u32[]{:S(2)}, u32[]{:S(2)}) collective-permute-start(bf16[128,1536]{1,0:T(8,128)(2,1)S(1)} %copy-done.15), channel_id=1, source_target_pairs={{0,1},{1,2},{2,3},{3,0},{4,5},{5,6},{6,7},{7,4},{8,9},{9,10},{10,1... | collective-permute-start | bytes 1179656 | tf_op jit(solution)/shard_map/ppermute | solution.py:510
  100.7 11.9 %collective-permute-start.21 = (bf16[1536,128]{1,0:T(8,128)(2,1)}, bf16[1536,128]{1,0:T(8,128)(2,1)}, u32[]{:S(2)}, u32[]{:S(2)}) collective-permute-start(bf16[1536,128]{1,0:T(8,128)(2,1)} %get-tuple-element.81), channel_id=1, source_target_pairs={{0,64},{32,96},{64,0},{96,32},{1,65},{33,97},{65,1},{97,33},{2,66}... | collective-permute-start | bytes 1179656 | tf_op jit(solution)/shard_map/ppermute | solution.py:510
  100.8 20.8 %collective-permute-start.20 = (bf16[1536,128]{1,0:T(8,128)(2,1)}, bf16[1536,128]{1,0:T(8,128)(2,1)}, u32[]{:S(2)}, u32[]{:S(2)}) collective-permute-start(bf16[1536,128]{1,0:T(8,128)(2,1)} %get-tuple-element.79), channel_id=1, source_target_pairs={{0,32},{32,64},{64,96},{96,0},{1,33},{33,65},{65,97},{97,1},{2,34}... | collective-permute-start | bytes 1179656 | tf_op jit(solution)/shard_map/ppermute | solution.py:510
  101.7 21.5 %collective-permute-start.24 = (bf16[128,1536]{1,0:T(8,128)(2,1)}, bf16[128,1536]{1,0:T(8,128)(2,1)S(1)}, u32[]{:S(2)}, u32[]{:S(2)}) collective-permute-start(bf16[128,1536]{1,0:T(8,128)(2,1)} %get-tuple-element.58), channel_id=1, source_target_pairs={{0,3},{1,0},{2,1},{3,2},{4,7},{5,4},{6,5},{7,6},{8,11},{9,8},{10,9... | collective-permute-start | bytes 1179656 | tf_op jit(solution)/shard_map/ppermute | solution.py:510
  103.1 20.1 %collective-permute-start.23 = (bf16[128,1536]{1,0:T(8,128)(2,1)}, bf16[128,1536]{1,0:T(8,128)(2,1)S(1)}, u32[]{:S(2)}, u32[]{:S(2)}) collective-permute-start(bf16[128,1536]{1,0:T(8,128)(2,1)} %get-tuple-element.56), channel_id=1, source_target_pairs={{0,2},{1,3},{2,0},{3,1},{4,6},{5,7},{6,4},{7,5},{8,10},{9,11},{10,... | collective-permute-start | bytes 1179656 | tf_op jit(solution)/shard_map/ppermute | solution.py:510
  109.4 13.8 %collective-permute-start.18 = (bf16[128,1536]{1,0:T(8,128)(2,1)}, bf16[128,1536]{1,0:T(8,128)(2,1)S(1)}, u32[]{:S(2)}, u32[]{:S(2)}) collective-permute-start(bf16[128,1536]{1,0:T(8,128)(2,1)} %get-tuple-element.52), channel_id=1, source_target_pairs={{0,1},{1,2},{2,3},{3,0},{4,5},{5,6},{6,7},{7,4},{8,9},{9,10},{10,1... | collective-permute-start | bytes 1179656 | tf_op jit(solution)/shard_map/ppermute | solution.py:510
  125.8 11.7 %collective-permute-start.30 = (bf16[384,128]{1,0:T(8,128)(2,1)}, bf16[384,128]{1,0:T(8,128)(2,1)}, u32[]{:S(2)}, u32[]{:S(2)}) collective-permute-start(bf16[384,128]{1,0:T(8,128)(2,1)} %get-tuple-element.84), channel_id=1, source_target_pairs={{0,8},{8,16},{16,24},{24,0},{1,9},{9,17},{17,25},{25,1},{2,10},{10... | collective-permute-start | bytes 294920 | tf_op jit(solution)/shard_map/ppermute | solution.py:510
  134.1 50.3 %collective-permute-start.28 = (bf16[128,1536]{1,0:T(8,128)(2,1)}, bf16[128,1536]{1,0:T(8,128)(2,1)S(1)}, u32[]{:S(2)}, u32[]{:S(2)}) collective-permute-start(bf16[128,1536]{1,0:T(8,128)(2,1)} %get-tuple-element.66), channel_id=1, source_target_pairs={{0,3},{1,0},{2,1},{3,2},{4,7},{5,4},{6,5},{7,6},{8,11},{9,8},{10,9... | collective-permute-start | bytes 1179656 | tf_op jit(solution)/shard_map/ppermute | solution.py:510
  134.5 49.9 %collective-permute-start.27 = (bf16[128,1536]{1,0:T(8,128)(2,1)}, bf16[128,1536]{1,0:T(8,128)(2,1)S(1)}, u32[]{:S(2)}, u32[]{:S(2)}) collective-permute-start(bf16[128,1536]{1,0:T(8,128)(2,1)} %get-tuple-element.64), channel_id=1, source_target_pairs={{0,2},{1,3},{2,0},{3,1},{4,6},{5,7},{6,4},{7,5},{8,10},{9,11},{10,... | collective-permute-start | bytes 1179656 | tf_op jit(solution)/shard_map/ppermute | solution.py:510
  135.6 48.9 %collective-permute-start.26 = (bf16[128,1536]{1,0:T(8,128)(2,1)}, bf16[128,1536]{1,0:T(8,128)(2,1)S(1)}, u32[]{:S(2)}, u32[]{:S(2)}) collective-permute-start(bf16[128,1536]{1,0:T(8,128)(2,1)} %get-tuple-element.62), channel_id=1, source_target_pairs={{0,1},{1,2},{2,3},{3,0},{4,5},{5,6},{6,7},{7,4},{8,9},{9,10},{10,1... | collective-permute-start | bytes 1179656 | tf_op jit(solution)/shard_map/ppermute | solution.py:510
  138.9 26.3 %collective-permute-start.36 = (bf16[12,640]{1,0:T(8,128)(2,1)S(1)}, bf16[12,640]{1,0:T(8,128)(2,1)S(1)}, u32[]{:S(2)}, u32[]{:S(2)}) collective-permute-start(bf16[12,640]{1,0:T(8,128)(2,1)S(1)} %bitcast.169), channel_id=1, source_target_pairs={{0,3},{1,0},{2,1},{3,2},{4,67},{5,64},{6,65},{7,66},{8,7},{9,4},{1... | collective-permute-start | bytes 46088 | tf_op jit(solution)/shard_map/ppermute | solution.py:502
  152.5 16.0 %collective-permute-start.33 = (bf16[12,640]{1,0:T(8,128)(2,1)S(1)}, bf16[12,640]{1,0:T(8,128)(2,1)S(1)}, u32[]{:S(2)}, u32[]{:S(2)}) collective-permute-start(bf16[12,640]{1,0:T(8,128)(2,1)S(1)} %bitcast.170), channel_id=1, source_target_pairs={{0,0},{1,1},{2,2},{3,3},{4,64},{5,65},{6,66},{7,67},{8,4},{9,5},{1... | collective-permute-start | bytes 46088 | tf_op jit(solution)/shard_map/ppermute | solution.py:502
  (30 other events, 237.8 us)
